TPU v7x, 128 devices: a whole 4x4x4 slice. The times are simulated.
128 devices in a mesh: dp: 8 (over y, z_lo), seq: 16 (over z_hi, x, core).
Axes of the slice: x: 4, y: 4, z: 4 (z_hi: 2, z_lo: 2; z = z_hi * 2 + z_lo), core: 2. Of those that a mesh axis runs over, the one named last changes fastest.
Arguments:
- query: bfloat16 [8, 12288, 1536], P('dp', 'seq'), may hold values from -6 to 6
- key_states: bfloat16 [8, 12288, 1536], P('dp', 'seq'), may hold values from -6 to 6
- value_states: bfloat16 [8, 12288, 1536], P('dp', 'seq'), may hold values from -6 to 6
- attn_out: bfloat16 [8, 12288, 1536], P('dp', 'seq'), may hold values from -0.59765625 to 0.59765625
- log_norm: float32 [8, 12, 12288], P('dp', None, 'seq'), may hold values from 6 to 7
- out_grad: bfloat16 [8, 12288, 3072], P('dp', 'seq'), may hold values from -24 to 24
- out_weight: bfloat16 [1536, 3072], P('dp'), may hold values from -0.15625 to 0.15625
- tile_lists: int32 [8, 32, 3], P('dp'), may hold values from 0 to 31, as said below
Outputs:
- query_grad: bfloat16 [8, 12288, 1536], P('dp', 'seq')
- key_grad: bfloat16 [8, 12288, 1536], P('dp', 'seq')
- value_grad: bfloat16 [8, 12288, 1536], P('dp', 'seq')
- weight_grad: float32 [1536, 3072], P('dp')
Inputs may be any that keep to these rules, and one draw needn't show every extreme that they name: `tile_lists`: row i of a clip's list names 3 different tiles: tile i itself and tiles j with (i // 2) * 2 - 1 <= j <= (i // 2) * 2 + 2.
All inputs are finite; a program needn't handle non-finite values.
Results may differ from a plain program's by a relative error of at most 0.0095.
Values may be sent and summed in bfloat16 or wider, within the bound.
No kernel may reach another device: no remote copies, remote signals or barrier semaphores. Data moves between devices by JAX's collectives and lax.ppermute only.
A program may use at most 256 MiB of HBM per device.

v0:
```python
import math

import jax
import jax.numpy as jnp
from jax import lax
from jax.sharding import PartitionSpec as P

TILE = 384


def with_halo(value, sides, width):
    for axis, dim in sides:
        size, length = (lax.axis_size(axis), value.shape[dim])
        up = [(i, (i + 1) % size) for i in range(size - 1)]
        down = [(j, i) for i, j in up]
        last = lax.slice_in_dim(value, length - width, length, axis=dim)
        initial = lax.slice_in_dim(value, 0, width, axis=dim)
        before = lax.ppermute(last, axis, up)
        after = lax.ppermute(initial, axis, down)
        value = jnp.concatenate([before, value, after], axis=dim)
    return value


def passed_along(value, axis, by):
    size = lax.axis_size(axis)
    pairs = [(i, i + by) for i in range(size) if 0 <= i + by < size]
    return lax.ppermute(value, axis, pairs)


def body(query, key_states, value_states, attn_out, log_norm, out_grad, out_weight, tile_lists):
    token_count = query.shape[1]
    feature_width = query.shape[2]
    head_count = log_norm.shape[1]
    keep_count = tile_lists.shape[2]
    head_dim = feature_width // head_count
    tiles_dev = token_count // TILE
    window_tiles = tiles_dev + 2
    window_count = window_tiles * TILE
    group_count = 2
    group_heads = head_count // group_count
    group_width = feature_width // group_count
    item_count = tiles_dev * group_count
    score_scale = 1.0 / math.sqrt(head_dim)
    grad_rows = out_grad[0]
    out_rows = attn_out[0]
    query_rows_all = query[0]
    norm_all = log_norm[0]
    attn_grad = jnp.einsum(
        "td,rd->tr",
        grad_rows,
        lax.all_gather(out_weight, "dp", axis=0, tiled=True),
        preferred_element_type=jnp.float32,
    ).astype(jnp.bfloat16)
    row_delta = (
        (attn_grad.astype(jnp.float32) * out_rows.astype(jnp.float32))
        .reshape(token_count, head_count, head_dim)
        .sum(axis=2)
        .T
    )
    summed = lax.psum_scatter(
        jnp.einsum("th,td->hd", out_rows, grad_rows, preferred_element_type=jnp.float32),
        ("dp", "seq"),
        scatter_dimension=0,
        tiled=True,
    )
    weight_grad = lax.all_gather(summed, "seq", axis=0, tiled=True)
    slab_index = lax.axis_index("seq")
    first_tile = slab_index * tiles_dev - 1
    own_lists = lax.dynamic_slice_in_dim(tile_lists[0], slab_index * tiles_dev, tiles_dev, 0)
    local_lists = own_lists - first_tile
    window = with_halo(jnp.stack([key_states[0], value_states[0]]), (("seq", 1),), TILE)
    window_keys = window[0]
    window_values = window[1]
    item_ids = jnp.arange(item_count, dtype=jnp.int32)
    tile_ids = item_ids // group_count
    group_ids = item_ids % group_count
    window_slots = jnp.arange(window_tiles, dtype=jnp.int32)

    def attend_item(totals, inputs):
        key_total, value_total, query_total = totals
        tile, group = inputs
        row_start = tile * TILE
        column_start = group * group_width
        head_start = group * group_heads
        kept_tiles = lax.dynamic_index_in_dim(local_lists, tile, 0, keepdims=False)
        query_block = lax.dynamic_slice(
            query_rows_all, (row_start, column_start), (TILE, group_width)
        )
        grad_block = lax.dynamic_slice(attn_grad, (row_start, column_start), (TILE, group_width))
        norm_block = lax.dynamic_slice(norm_all, (head_start, row_start), (group_heads, TILE))
        delta_block = lax.dynamic_slice(row_delta, (head_start, row_start), (group_heads, TILE))
        group_keys = lax.dynamic_slice_in_dim(window_keys, column_start, group_width, 1).reshape(
            window_tiles, TILE, group_width
        )
        group_values = lax.dynamic_slice_in_dim(
            window_values, column_start, group_width, 1
        ).reshape(window_tiles, TILE, group_width)
        kept_keys = jnp.take(group_keys, kept_tiles, axis=0).reshape(
            keep_count * TILE, group_heads, head_dim
        )
        kept_values = jnp.take(group_values, kept_tiles, axis=0).reshape(
            keep_count * TILE, group_heads, head_dim
        )
        query_heads = query_block.reshape(TILE, group_heads, head_dim)
        grad_heads = grad_block.reshape(TILE, group_heads, head_dim)
        scores = (
            jnp.einsum("qhd,khd->hqk", query_heads, kept_keys, preferred_element_type=jnp.float32)
            * score_scale
        )
        weights = jnp.exp(scores - norm_block[:, :, None])
        prob_grad = jnp.einsum(
            "qhd,khd->hqk", grad_heads, kept_values, preferred_element_type=jnp.float32
        )
        weights_half = weights.astype(jnp.bfloat16)
        score_grad = (weights * (prob_grad - delta_block[:, :, None])).astype(jnp.bfloat16)
        value_part = jnp.einsum(
            "hqk,qhd->khd", weights_half, grad_heads, preferred_element_type=jnp.float32
        ).reshape(keep_count, TILE, group_width)
        key_part = jnp.einsum(
            "hqk,qhd->khd", score_grad, query_heads, preferred_element_type=jnp.float32
        ).reshape(keep_count, TILE, group_width)
        query_part = (
            jnp.einsum("hqk,khd->qhd", score_grad, kept_keys, preferred_element_type=jnp.float32)
            * score_scale
        )
        query_part = query_part.reshape(TILE, group_width).astype(jnp.bfloat16)
        placing = (kept_tiles[:, None] == window_slots[None, :]).astype(jnp.float32)
        key_add = jnp.einsum(
            "kw,kte->wte", placing, key_part, precision=lax.Precision.HIGHEST
        ).reshape(window_count, group_width)
        value_add = jnp.einsum(
            "kw,kte->wte", placing, value_part, precision=lax.Precision.HIGHEST
        ).reshape(window_count, group_width)
        key_old = lax.dynamic_slice_in_dim(key_total, column_start, group_width, 1)
        value_old = lax.dynamic_slice_in_dim(value_total, column_start, group_width, 1)
        key_total = lax.dynamic_update_slice_in_dim(key_total, key_old + key_add, column_start, 1)
        value_total = lax.dynamic_update_slice_in_dim(
            value_total, value_old + value_add, column_start, 1
        )
        query_total = lax.dynamic_update_slice(query_total, query_part, (row_start, column_start))
        return ((key_total, value_total, query_total), None)

    empty_total = jnp.zeros((window_count, feature_width), jnp.float32)
    empty_query = jnp.zeros((token_count, feature_width), jnp.bfloat16)
    (key_window, value_window, query_rows), unused = lax.scan(
        attend_item, (empty_total, empty_total, empty_query), (tile_ids, group_ids)
    )
    low_rims = jnp.stack([key_window[:TILE], value_window[:TILE]]).astype(jnp.bfloat16)
    high_rims = jnp.stack(
        [key_window[TILE + token_count :], value_window[TILE + token_count :]]
    ).astype(jnp.bfloat16)
    from_below = passed_along(high_rims, "seq", 1)
    from_above = passed_along(low_rims, "seq", -1)
    key_sum = key_window[TILE : TILE + token_count]
    value_sum = value_window[TILE : TILE + token_count]
    key_sum = (
        key_sum.at[:TILE]
        .add(from_below[0].astype(jnp.float32))
        .at[token_count - TILE :]
        .add(from_above[0].astype(jnp.float32))
    )
    value_sum = (
        value_sum.at[:TILE]
        .add(from_below[1].astype(jnp.float32))
        .at[token_count - TILE :]
        .add(from_above[1].astype(jnp.float32))
    )
    query_grad = query_rows[None]
    key_grad = (key_sum * score_scale).astype(jnp.bfloat16)[None]
    value_grad = value_sum.astype(jnp.bfloat16)[None]
    return (query_grad, key_grad, value_grad, weight_grad)


def solution(mesh):
    placed = (
        P("dp", "seq", None),
        P("dp", "seq", None),
        P("dp", "seq", None),
        P("dp", "seq", None),
        P("dp", None, "seq"),
        P("dp", "seq", None),
        P("dp", None),
        P("dp", None, None),
    )
    return jax.shard_map(
        body,
        mesh=mesh,
        in_specs=placed,
        out_specs=(P("dp", "seq", None), P("dp", "seq", None), P("dp", "seq", None), P("dp", None)),
        check_vma=False,
    )
```

profile of v0, /device:TPU:7, one launch (start us, length us, event | category | flops | bytes accessed | tf_op | source)
XLA Modules:
  0.0 1241.0 jit_solution(11317247192271641247)
XLA Ops:
  8.0 13.9 %fusion.22 = f32[1536,3072]{1,0:T(8,128)} fusion(bf16[1,768,3072]{2,1,0:T(8,128)(2,1)} %param.25, bf16[1,768,1536]{2,1,0:T(8,128)(2,1)} %param.23), kind=kOutput, calls=%fused_computation.37 | convolution fusion | flops 7247757312 | bytes 25952256 | tf_op jit(solution)/shard_map/th,td->hd/dot_general | solution.py:61
  21.8 339.7 %fusion.2 = f32[16,3072]{1,0:T(8,128)S(1)} fusion(f32[1536,3072]{1,0:T(8,128)} %fusion.22), kind=kCustom, calls=%all-reduce-scatter | all-reduce-scatter fusion | flops 6291457 | bytes 19070976
  365.6 29.6 %collective-permute-start.31 = (f32[16,3072]{1,0:T(8,128)S(1)}, f32[16,3072]{1,0:T(8,128)S(1)}, u32[]{:S(2)}, u32[]{:S(2)}) collective-permute-start(f32[16,3072]{1,0:T(8,128)S(1)} %fusion.2), channel_id=1, source_target_pairs={{0,28},{1,29},{2,30},{3,31},{4,32},{5,33},{6,34},{7,35},{8,36},{9,... | collective-permute-start | bytes 589832
  395.3 8.4 collective-permute-start.35
  407.7 6.8 collective-permute-start
  426.5 22.4 %collective-permute-done.29 = f32[16,3072]{1,0:T(8,128)S(1)} collective-permute-done((f32[16,3072]{1,0:T(8,128)S(1)}, f32[16,3072]{1,0:T(8,128)S(1)}, u32[]{:S(2)}, u32[]{:S(2)}) %collective-permute-start.29) | collective-permute-done | bytes 196640
  452.3 10.5 collective-permute-start.24
  468.0 6.5 collective-permute-start.22
  476.2 15.9 %collective-permute-start.20 = (f32[16,3072]{1,0:T(8,128)S(1)}, f32[16,3072]{1,0:T(8,128)S(1)}, u32[]{:S(2)}, u32[]{:S(2)}) collective-permute-start(f32[16,3072]{1,0:T(8,128)S(1)} %fusion.2), channel_id=1, source_target_pairs={{0,17},{1,18},{2,19},{3,20},{4,21},{5,22},{6,23},{7,24},{8,25},{9,... | collective-permute-start | bytes 589832
  496.7 6.0 collective-permute-start.17
  502.6 11.1 collective-permute-start.16
  516.8 11.6 collective-permute-start.13
  537.3 6.3 collective-permute-start.9
  543.7 7.0 collective-permute-start.8
  575.2 85.4 %concatenate.12 = f32[524,3072]{1,0:T(8,128)} concatenate(f32[12,3072]{1,0:T(8,128)} %copy-done.15, f32[16,3072]{1,0:T(8,128)S(1)} %collective-permute-done.34, f32[16,3072]{1,0:T(8,128)S(1)} %collective-permute-done.33, f32[16,3072]{1,0:T(8,128)S(1)} %collective-permute-done.32, f32[16,3072]{1,0:T(8,128)S(1)} %collective-permute-done.31, f32[16,3072]{1,0:T(8,128)} %copy-done.16, ...), dimensions={0} | concatenate | bytes 12877824
  672.4 13.5 %convert_multiply_fusion = (f32[768,1536]{1,0:T(8,128)}, bf16[768,1536]{1,0:T(8,128)(2,1)S(1)}) fusion(bf16[1,768,1536]{2,1,0:T(8,128)(2,1)} %param.23, bf16[1536,3072]{1,0:T(8,128)(2,1)} %all-gather.4.cloned.1.call-done, bf16[1,768,3072]{2,1,0:T(8,128)(2,1)} %param.25), kind=kOutput, calls=%fused_computation.42 | convolution fusion | flops 7252475904 | bytes 23592960 | tf_op jit(solution)/shard_map/td,rd->tr/dot_general | solution.py:48
  685.9 6.0 copy.64
  705.8 470.2 %while.19 = (s32[]{:T(128)}, f32[1536,1536]{1,0:T(8,128)}, f32[1536,1536]{1,0:T(8,128)}, bf16[768,1536]{1,0:T(8,128)(2,1)}, s32[4]{0:T(128)S(1)}, /*index=5*/s32...) while((s32[]{:T(128)}, f32[1536,1536]{1,0:T(8,128)}, ...), condition=%wide.region_2.4_spmd.clone, body=%wide.region_1.3_spmd.clone.sunk | while | flops 3508274176 | bytes 231280416 | solution.py:145
  774.5 6.1 reshape.220
  780.7 6.8 copy.95
  787.4 6.8 fusion.85
  800.9 6.7 copy.93
  807.6 6.8 fusion.84
  817.5 6.8 dynamic_update_slice.17
  824.2 11.6 constant_dynamic-update-slice_fusion.5
  873.0 5.9 multiply_convert_fusion.3
  888.4 6.1 reshape.220
  894.5 6.8 copy.95
  901.3 6.8 fusion.85
  914.8 6.7 copy.93
  921.5 6.8 fusion.84
  931.3 6.1 dynamic_update_slice.17
  937.4 11.7 constant_dynamic-update-slice_fusion.5
  1001.6 6.1 reshape.220
  1007.7 6.8 copy.95
  1014.5 6.8 fusion.85
  1028.0 6.7 copy.93
  1034.7 6.8 fusion.84
  1044.5 6.6 dynamic_update_slice.17
  1051.2 11.6 constant_dynamic-update-slice_fusion.5
  1115.3 6.1 reshape.220
  1121.4 6.8 copy.95
  1128.2 6.8 fusion.85
  1141.7 6.7 copy.93
  1148.4 6.8 fusion.84
  1164.2 11.7 constant_dynamic-update-slice_fusion.5
  1185.0 8.5 collective-permute-start.2
  1204.0 15.5 %collective-permute-done.2 = bf16[2,384,1536]{2,1,0:T(8,128)(2,1)} collective-permute-done((bf16[2,384,1536]{2,1,0:T(8,128)(2,1)}, bf16[2,384,1536]{2,1,0:T(8,128)(2,1)}, u32[]{:S(2)}, u32[]{:S(2)}) %collective-permute-start.2) | collective-permute-done | bytes 2359328 | tf_op jit(solution)/shard_map/ppermute | solution.py:27
  (324 shorter events, 363.3 us)
Async XLA Ops:
  7.2 546.7 %copy-start = (s32[1,32,3]{1,0,2:T(1,128)S(1)}, s32[1,32,3]{1,0,2:T(1,128)}, u32[]{:S(2)}) copy-start(s32[1,32,3]{1,0,2:T(1,128)} %param.27) | copy-start | bytes 1156
  7.2 665.2 %all-gather.4.cloned.1.call-start = ((), (), s32[]{:S(2)}) async-start(), calls=%async_computation | async-start | bytes 10616832 | tf_op jit(solution)/shard_map/all_gather | solution.py:51
  7.9 1187.7 %all-gather.6.cloned.1.call-start = ((), (), s32[]{:S(2)}) async-start(), calls=%async_computation.1 | async-start | bytes 3342336 | tf_op jit(solution)/shard_map/all_gather | solution.py:66
  21.8 381.9 %copy-start.9 = (bf16[1,768,1536]{2,1,0:T(8,128)(2,1)S(1)}, bf16[1,768,1536]{2,1,0:T(8,128)(2,1)}, u32[]{:S(2)}) copy-start(bf16[1,768,1536]{2,1,0:T(8,128)(2,1)} %param.21) | copy-start | bytes 7077892
  361.6 52.9 %collective-permute-start.34 = (f32[16,3072]{1,0:T(8,128)S(1)}, f32[16,3072]{1,0:T(8,128)S(1)}, u32[]{:S(2)}, u32[]{:S(2)}) collective-permute-start(f32[16,3072]{1,0:T(8,128)S(1)} %fusion.2), channel_id=1, source_target_pairs={{0,31},{1,32},{2,33},{3,34},{4,35},{5,36},{6,37},{7,38},{8,39},{9,... | collective-permute-start | bytes 589832
  363.0 53.4 %collective-permute-start.33 = (f32[16,3072]{1,0:T(8,128)S(1)}, f32[16,3072]{1,0:T(8,128)S(1)}, u32[]{:S(2)}, u32[]{:S(2)}) collective-permute-start(f32[16,3072]{1,0:T(8,128)S(1)} %fusion.2), channel_id=1, source_target_pairs={{0,30},{1,31},{2,32},{3,33},{4,34},{5,35},{6,36},{7,37},{8,38},{9,... | collective-permute-start | bytes 589832
  364.3 56.1 %collective-permute-start.32 = (f32[16,3072]{1,0:T(8,128)S(1)}, f32[16,3072]{1,0:T(8,128)S(1)}, u32[]{:S(2)}, u32[]{:S(2)}) collective-permute-start(f32[16,3072]{1,0:T(8,128)S(1)} %fusion.2), channel_id=1, source_target_pairs={{0,29},{1,30},{2,31},{3,32},{4,33},{5,34},{6,35},{7,36},{8,37},{9,... | collective-permute-start | bytes 589832
  365.6 56.1 %collective-permute-start.31 = (f32[16,3072]{1,0:T(8,128)S(1)}, f32[16,3072]{1,0:T(8,128)S(1)}, u32[]{:S(2)}, u32[]{:S(2)}) collective-permute-start(f32[16,3072]{1,0:T(8,128)S(1)} %fusion.2), channel_id=1, source_target_pairs={{0,28},{1,29},{2,30},{3,31},{4,32},{5,33},{6,34},{7,35},{8,36},{9,... | collective-permute-start | bytes 589832
  395.3 12.4 collective-permute-start.35
  404.1 150.0 %copy-start.36 = (f32[1,12,768]{2,0,1:T(1,128)S(1)}, f32[1,12,768]{2,0,1:T(1,128)}, u32[]{:S(2)}) copy-start(f32[1,12,768]{2,0,1:T(1,128)} %param.24) | copy-start | bytes 110596
  407.7 126.8 %copy-start.15 = (f32[12,3072]{1,0:T(8,128)}, f32[12,3072]{1,0:T(8,128)S(1)}, u32[]{:S(2)}) copy-start(f32[12,3072]{1,0:T(8,128)S(1)} %collective-permute-done.35) | copy-start | bytes 442372
  407.7 254.6 %collective-permute-start = (bf16[2,384,1536]{2,1,0:T(8,128)(2,1)}, bf16[2,384,1536]{2,1,0:T(8,128)(2,1)S(1)}, u32[]{:S(2)}, u32[]{:S(2)}) collective-permute-start(bf16[2,384,1536]{2,1,0:T(8,128)(2,1)} %get-tuple-element.235), channel_id=1, source_target_pairs={{0,1},{1,2},{2,3},{3,4},{4,5},{5,6},{6,7},{7,8},{8,9},{9,10},{10,1... | collective-permute-start | bytes 7077896 | tf_op jit(solution)/shard_map/ppermute | solution.py:18
  414.5 249.2 %collective-permute-start.1 = (bf16[2,384,1536]{2,1,0:T(8,128)(2,1)}, bf16[2,384,1536]{2,1,0:T(8,128)(2,1)}, u32[]{:S(2)}, u32[]{:S(2)}) collective-permute-start(bf16[2,384,1536]{2,1,0:T(8,128)(2,1)} %get-tuple-element.236), channel_id=1, source_target_pairs={{1,0},{2,1},{3,2},{4,3},{5,4},{6,5},{7,6},{8,7},{9,8},{10,9},{11,1... | collective-permute-start | bytes 7077896 | tf_op jit(solution)/shard_map/ppermute | solution.py:19
  416.4 8.8 collective-permute-start.30
  420.4 28.4 %collective-permute-start.29 = (f32[16,3072]{1,0:T(8,128)S(1)}, f32[16,3072]{1,0:T(8,128)S(1)}, u32[]{:S(2)}, u32[]{:S(2)}) collective-permute-start(f32[16,3072]{1,0:T(8,128)S(1)} %fusion.2), channel_id=1, source_target_pairs={{0,26},{1,27},{2,28},{3,29},{4,30},{5,31},{6,32},{7,33},{8,34},{9,... | collective-permute-start | bytes 589832
  421.8 29.2 %collective-permute-start.28 = (f32[16,3072]{1,0:T(8,128)S(1)}, f32[16,3072]{1,0:T(8,128)S(1)}, u32[]{:S(2)}, u32[]{:S(2)}) collective-permute-start(f32[16,3072]{1,0:T(8,128)S(1)} %fusion.2), channel_id=1, source_target_pairs={{0,25},{1,26},{2,27},{3,28},{4,29},{5,30},{6,31},{7,32},{8,33},{9,... | collective-permute-start | bytes 589832
  425.2 111.9 %copy-start.16 = (f32[16,3072]{1,0:T(8,128)}, f32[16,3072]{1,0:T(8,128)S(1)}, u32[]{:S(2)}) copy-start(f32[16,3072]{1,0:T(8,128)S(1)} %collective-permute-done.30) | copy-start | bytes 589828
  425.2 27.1 %collective-permute-start.27 = (f32[16,3072]{1,0:T(8,128)S(1)}, f32[16,3072]{1,0:T(8,128)S(1)}, u32[]{:S(2)}, u32[]{:S(2)}) collective-permute-start(f32[16,3072]{1,0:T(8,128)S(1)} %fusion.2), channel_id=1, source_target_pairs={{0,24},{1,25},{2,26},{3,27},{4,28},{5,29},{6,30},{7,31},{8,32},{9,... | collective-permute-start | bytes 589832
  448.8 88.3 %copy-start.17 = (f32[16,3072]{1,0:T(8,128)}, f32[16,3072]{1,0:T(8,128)S(1)}, u32[]{:S(2)}) copy-start(f32[16,3072]{1,0:T(8,128)S(1)} %collective-permute-done.29) | copy-start | bytes 589828
  448.8 14.0 %collective-permute-start.26 = (f32[16,3072]{1,0:T(8,128)S(1)}, f32[16,3072]{1,0:T(8,128)S(1)}, u32[]{:S(2)}, u32[]{:S(2)}) collective-permute-start(f32[16,3072]{1,0:T(8,128)S(1)} %fusion.2), channel_id=1, source_target_pairs={{0,23},{1,24},{2,25},{3,26},{4,27},{5,28},{6,29},{7,30},{8,31},{9,... | collective-permute-start | bytes 589832
  451.0 86.2 %copy-start.18 = (f32[16,3072]{1,0:T(8,128)}, f32[16,3072]{1,0:T(8,128)S(1)}, u32[]{:S(2)}) copy-start(f32[16,3072]{1,0:T(8,128)S(1)} %collective-permute-done.28) | copy-start | bytes 589828
  451.0 17.0 %collective-permute-start.25 = (f32[16,3072]{1,0:T(8,128)S(1)}, f32[16,3072]{1,0:T(8,128)S(1)}, u32[]{:S(2)}, u32[]{:S(2)}) collective-permute-start(f32[16,3072]{1,0:T(8,128)S(1)} %fusion.2), channel_id=1, source_target_pairs={{0,22},{1,23},{2,24},{3,25},{4,26},{5,27},{6,28},{7,29},{8,30},{9,... | collective-permute-start | bytes 589832
  452.3 84.9 %copy-start.19 = (f32[16,3072]{1,0:T(8,128)}, f32[16,3072]{1,0:T(8,128)S(1)}, u32[]{:S(2)}) copy-start(f32[16,3072]{1,0:T(8,128)S(1)} %collective-permute-done.27) | copy-start | bytes 589828
  452.3 22.2 %collective-permute-start.24 = (f32[16,3072]{1,0:T(8,128)S(1)}, f32[16,3072]{1,0:T(8,128)S(1)}, u32[]{:S(2)}, u32[]{:S(2)}) collective-permute-start(f32[16,3072]{1,0:T(8,128)S(1)} %fusion.2), channel_id=1, source_target_pairs={{0,21},{1,22},{2,23},{3,24},{4,25},{5,26},{6,27},{7,28},{8,29},{9,... | collective-permute-start | bytes 589832
  462.8 74.3 %copy-start.20 = (f32[16,3072]{1,0:T(8,128)}, f32[16,3072]{1,0:T(8,128)S(1)}, u32[]{:S(2)}) copy-start(f32[16,3072]{1,0:T(8,128)S(1)} %collective-permute-done.26) | copy-start | bytes 589828
  462.8 13.4 %collective-permute-start.23 = (f32[16,3072]{1,0:T(8,128)S(1)}, f32[16,3072]{1,0:T(8,128)S(1)}, u32[]{:S(2)}, u32[]{:S(2)}) collective-permute-start(f32[16,3072]{1,0:T(8,128)S(1)} %fusion.2), channel_id=1, source_target_pairs={{0,20},{1,21},{2,22},{3,23},{4,24},{5,25},{6,26},{7,27},{8,28},{9,... | collective-permute-start | bytes 589832
  467.9 69.2 %copy-start.21 = (f32[16,3072]{1,0:T(8,128)}, f32[16,3072]{1,0:T(8,128)S(1)}, u32[]{:S(2)}) copy-start(f32[16,3072]{1,0:T(8,128)S(1)} %collective-permute-done.25) | copy-start | bytes 589828
  468.0 24.2 %collective-permute-start.22 = (f32[16,3072]{1,0:T(8,128)S(1)}, f32[16,3072]{1,0:T(8,128)S(1)}, u32[]{:S(2)}, u32[]{:S(2)}) collective-permute-start(f32[16,3072]{1,0:T(8,128)S(1)} %fusion.2), channel_id=1, source_target_pairs={{0,19},{1,20},{2,21},{3,22},{4,23},{5,24},{6,25},{7,26},{8,27},{9,... | collective-permute-start | bytes 589832
  474.5 20.2 %collective-permute-start.21 = (f32[16,3072]{1,0:T(8,128)S(1)}, f32[16,3072]{1,0:T(8,128)S(1)}, u32[]{:S(2)}, u32[]{:S(2)}) collective-permute-start(f32[16,3072]{1,0:T(8,128)S(1)} %fusion.2), channel_id=1, source_target_pairs={{0,18},{1,19},{2,20},{3,21},{4,22},{5,23},{6,24},{7,25},{8,26},{9,... | collective-permute-start | bytes 589832
  476.2 20.4 %collective-permute-start.20 = (f32[16,3072]{1,0:T(8,128)S(1)}, f32[16,3072]{1,0:T(8,128)S(1)}, u32[]{:S(2)}, u32[]{:S(2)}) collective-permute-start(f32[16,3072]{1,0:T(8,128)S(1)} %fusion.2), channel_id=1, source_target_pairs={{0,17},{1,18},{2,19},{3,20},{4,21},{5,22},{6,23},{7,24},{8,25},{9,... | collective-permute-start | bytes 589832
  492.2 10.4 collective-permute-start.19
  494.8 19.0 %collective-permute-start.18 = (f32[16,3072]{1,0:T(8,128)S(1)}, f32[16,3072]{1,0:T(8,128)S(1)}, u32[]{:S(2)}, u32[]{:S(2)}) collective-permute-start(f32[16,3072]{1,0:T(8,128)S(1)} %fusion.2), channel_id=1, source_target_pairs={{0,15},{1,16},{2,17},{3,18},{4,19},{5,20},{6,21},{7,22},{8,23},{9,... | collective-permute-start | bytes 589832
  496.7 18.4 %collective-permute-start.17 = (f32[16,3072]{1,0:T(8,128)S(1)}, f32[16,3072]{1,0:T(8,128)S(1)}, u32[]{:S(2)}, u32[]{:S(2)}) collective-permute-start(f32[16,3072]{1,0:T(8,128)S(1)} %fusion.2), channel_id=1, source_target_pairs={{0,14},{1,15},{2,16},{3,17},{4,18},{5,19},{6,20},{7,21},{8,22},{9,... | collective-permute-start | bytes 589832
  502.6 14.1 %collective-permute-start.16 = (f32[16,3072]{1,0:T(8,128)S(1)}, f32[16,3072]{1,0:T(8,128)S(1)}, u32[]{:S(2)}, u32[]{:S(2)}) collective-permute-start(f32[16,3072]{1,0:T(8,128)S(1)} %fusion.2), channel_id=1, source_target_pairs={{0,13},{1,14},{2,15},{3,16},{4,17},{5,18},{6,19},{7,20},{8,21},{9,... | collective-permute-start | bytes 589832
  513.8 14.6 %collective-permute-start.15 = (f32[16,3072]{1,0:T(8,128)S(1)}, f32[16,3072]{1,0:T(8,128)S(1)}, u32[]{:S(2)}, u32[]{:S(2)}) collective-permute-start(f32[16,3072]{1,0:T(8,128)S(1)} %fusion.2), channel_id=1, source_target_pairs={{0,12},{1,13},{2,14},{3,15},{4,16},{5,17},{6,18},{7,19},{8,20},{9,... | collective-permute-start | bytes 589832
  515.1 15.2 %collective-permute-start.14 = (f32[16,3072]{1,0:T(8,128)S(1)}, f32[16,3072]{1,0:T(8,128)S(1)}, u32[]{:S(2)}, u32[]{:S(2)}) collective-permute-start(f32[16,3072]{1,0:T(8,128)S(1)} %fusion.2), channel_id=1, source_target_pairs={{0,11},{1,12},{2,13},{3,14},{4,15},{5,16},{6,17},{7,18},{8,19},{9,... | collective-permute-start | bytes 589832
  516.8 17.7 %collective-permute-start.13 = (f32[16,3072]{1,0:T(8,128)S(1)}, f32[16,3072]{1,0:T(8,128)S(1)}, u32[]{:S(2)}, u32[]{:S(2)}) collective-permute-start(f32[16,3072]{1,0:T(8,128)S(1)} %fusion.2), channel_id=1, source_target_pairs={{0,10},{1,11},{2,12},{3,13},{4,14},{5,15},{6,16},{7,17},{8,18},{9,... | collective-permute-start | bytes 589832
  528.4 9.0 collective-permute-start.12
  530.3 13.3 %collective-permute-start.11 = (f32[16,3072]{1,0:T(8,128)S(1)}, f32[16,3072]{1,0:T(8,128)}, u32[]{:S(2)}, u32[]{:S(2)}) collective-permute-start(f32[16,3072]{1,0:T(8,128)S(1)} %fusion.2), channel_id=1, source_target_pairs={{0,8},{1,9},{2,10},{3,11},{4,12},{5,13},{6,14},{7,15},{8,16},{9,17... | collective-permute-start | bytes 589832
  534.5 16.3 %collective-permute-start.10 = (f32[16,3072]{1,0:T(8,128)S(1)}, f32[16,3072]{1,0:T(8,128)}, u32[]{:S(2)}, u32[]{:S(2)}) collective-permute-start(f32[16,3072]{1,0:T(8,128)S(1)} %fusion.2), channel_id=1, source_target_pairs={{0,7},{1,8},{2,9},{3,10},{4,11},{5,12},{6,13},{7,14},{8,15},{9,16}... | collective-permute-start | bytes 589832
  537.3 21.0 %collective-permute-start.9 = (f32[16,3072]{1,0:T(8,128)S(1)}, f32[16,3072]{1,0:T(8,128)}, u32[]{:S(2)}, u32[]{:S(2)}) collective-permute-start(f32[16,3072]{1,0:T(8,128)S(1)} %fusion.2), channel_id=1, source_target_pairs={{0,6},{1,7},{2,8},{3,9},{4,10},{5,11},{6,12},{7,13},{8,14},{9,15},... | collective-permute-start | bytes 589832
  543.7 18.9 %collective-permute-start.8 = (f32[16,3072]{1,0:T(8,128)S(1)}, f32[16,3072]{1,0:T(8,128)}, u32[]{:S(2)}, u32[]{:S(2)}) collective-permute-start(f32[16,3072]{1,0:T(8,128)S(1)} %fusion.2), channel_id=1, source_target_pairs={{0,5},{1,6},{2,7},{3,8},{4,9},{5,10},{6,11},{7,12},{8,13},{9,14},{... | collective-permute-start | bytes 589832
  550.7 16.4 %collective-permute-start.7 = (f32[16,3072]{1,0:T(8,128)S(1)}, f32[16,3072]{1,0:T(8,128)}, u32[]{:S(2)}, u32[]{:S(2)}) collective-permute-start(f32[16,3072]{1,0:T(8,128)S(1)} %fusion.2), channel_id=1, source_target_pairs={{0,4},{1,5},{2,6},{3,7},{4,8},{5,9},{6,10},{7,11},{8,12},{9,13},{1... | collective-permute-start | bytes 589832
  558.4 13.6 %collective-permute-start.6 = (f32[16,3072]{1,0:T(8,128)S(1)}, f32[16,3072]{1,0:T(8,128)S(1)}, u32[]{:S(2)}, u32[]{:S(2)}) collective-permute-start(f32[16,3072]{1,0:T(8,128)S(1)} %fusion.2), channel_id=1, source_target_pairs={{0,3},{1,4},{2,5},{3,6},{4,7},{5,8},{6,9},{7,10},{8,11},{9,12},{10... | collective-permute-start | bytes 589832
  562.6 9.3 collective-permute-start.5
  567.1 8.0 collective-permute-start.4
  1185.0 34.6 %collective-permute-start.2 = (bf16[2,384,1536]{2,1,0:T(8,128)(2,1)}, bf16[2,384,1536]{2,1,0:T(8,128)(2,1)}, u32[]{:S(2)}, u32[]{:S(2)}) collective-permute-start(bf16[2,384,1536]{2,1,0:T(8,128)(2,1)} %pad_maximum_fusion.1), channel_id=1, source_target_pairs={{0,1},{1,2},{2,3},{3,4},{4,5},{5,6},{6,7},{7,8},{8,9},{9,10},{10,1... | collective-permute-start | bytes 7077896 | tf_op jit(solution)/shard_map/ppermute | solution.py:27
  1193.7 33.9 %collective-permute-start.3 = (bf16[2,384,1536]{2,1,0:T(8,128)(2,1)S(1)}, bf16[2,384,1536]{2,1,0:T(8,128)(2,1)}, u32[]{:S(2)}, u32[]{:S(2)}) collective-permute-start(bf16[2,384,1536]{2,1,0:T(8,128)(2,1)S(1)} %pad_maximum_fusion.2), channel_id=1, source_target_pairs={{1,0},{2,1},{3,2},{4,3},{5,4},{6,5},{7,6},{8,7},{9,8},{10,9},{11,1... | collective-permute-start | bytes 7077896 | tf_op jit(solution)/shard_map/ppermute | solution.py:27
  (51 other events, 687.1 us)
Sparse Core Ops, SparseCore 0:
  9.7 190.3 all-gather.3
  662.3 55.3 all-gather.5
where the time goes:
time: 1260 us; the launch traced here: 1240 us
  local copies, waits for them, and re-layouts  388 us (31%)
  blocking collectives  340 us (27%)
  starting transfers between devices  186 us (15%)
  matrix products  146 us (12%)
  other arithmetic  85.1 us (7%)
  waiting for transfers between devices  47.7 us (4%)
  loops' own time  32.8 us (3%)
  between operations  15.4 us (1%)
    unnamed x1, blocking collectives  340 us
    unnamed x32, starting transfers between devices  167 us
    unnamed x66, local copies, waits for them, and re-layouts  100 us
    reshape x8, local copies, waits for them, and re-layouts, attend_item(): key_part = jnp.einsum('hqk,qhd->khd', score_grad, query_heads, preferred_...  51.5 us
    dynamic_update_slice x4, other arithmetic, attend_item(): lax.dynamic_update_slice_in_dim(value_total, value_old + value_add, colum...  46.5 us
    reshape x8, local copies, waits for them, and re-layouts, attend_item(): value_part = jnp.einsum('hqk,qhd->khd', weights_half, grad_heads, preferr...  41.6 us
    another operation x1, loops' own time, body(): lax.scan(attend_item, (empty_total, empty_total, empty_query), (tile_ids,...  32.8 us
    reshape x8, local copies, waits for them, and re-layouts, attend_item(): jnp.take(group_keys, kept_tiles, axis=0)  31.1 us
  transfers between devices with their start and end apart: 38, of which 7 were waited for; matrix products, arithmetic and copies ran while one was open for 76% of the time, Pallas kernels for 0%

commit v1 on v0

v1 whole, which is shorter than its diff:
```python
import functools
import math

import jax
import jax.numpy as jnp
from jax import lax
from jax.experimental import pallas as pl
from jax.experimental.pallas import tpu as pltpu
from jax.sharding import PartitionSpec as P

TILE = 384
HEAD = 128
LOG2E = math.log2(math.e)
SCALE = 1.0 / math.sqrt(HEAD)
F32 = jnp.float32
BF16 = jnp.bfloat16
NT = (((1,), (1,)), ((), ()))
NN = (((1,), (0,)), ((), ()))
TN = (((0,), (0,)), ((), ()))


def dot(a, b, dims):
    return lax.dot_general(a, b, dims, preferred_element_type=F32)


def attend_kernel(
    meta, q, kb, ko, ka, vb, vo, va, g, o, norm, dq_in, dq, dko, dvo, low, high, kw, vw, dka, dva
):
    head = meta[6] + pl.program_id(0)
    kw[0] = kb[...]
    kw[1] = ko[:TILE]
    kw[2] = ko[TILE:]
    kw[3] = ka[...]
    vw[0] = vb[...]
    vw[1] = vo[:TILE]
    vw[2] = vo[TILE:]
    vw[3] = va[...]
    dka[...] = jnp.zeros_like(dka)
    dva[...] = jnp.zeros_like(dva)
    ones = jnp.ones((16, HEAD), BF16)
    for t in range(2):
        rows = slice(t * TILE, (t + 1) * TILE)
        qt = q[rows, :]
        gt = g[rows, :]
        prod = gt.astype(F32) * o[rows, :].astype(F32)
        coarse = prod.astype(BF16)
        fine = (prod - coarse.astype(F32)).astype(BF16)
        delta = (dot(ones, coarse, NT) + dot(ones, fine, NT))[0:1]
        shift = norm[pl.ds(head, 1), rows] * LOG2E
        total = None
        for j in range(3):
            slot = meta[t * 3 + j]
            k = kw[slot]
            weights = jnp.exp2(dot(k, qt, NT) * (SCALE * LOG2E) - shift)
            score_grad = (weights * (dot(vw[slot], gt, NT) - delta)).astype(BF16)
            dva[slot] += dot(weights.astype(BF16), gt, NN)
            dka[slot] += dot(score_grad, qt, NN)
            part = dot(k, score_grad, TN)
            total = part if total is None else total + part
        dq[rows, :] = (total * SCALE).T.astype(BF16)
    dko[...] = dka[1:3].reshape(2 * TILE, HEAD)
    dvo[...] = dva[1:3].reshape(2 * TILE, HEAD)
    low[0] = dka[0].astype(BF16)
    low[1] = dva[0].astype(BF16)
    high[0] = dka[3].astype(BF16)
    high[1] = dva[3].astype(BF16)


def attend(meta, q, kb, ko, ka, vb, vo, va, g, o, norm, dq_full):
    heads = g.shape[1] // HEAD
    own = pl.BlockSpec((2 * TILE, HEAD), lambda i, m: (0, i + m[6]))
    rim = pl.BlockSpec((TILE, HEAD), lambda i, m: (0, i + m[6]))
    local = pl.BlockSpec((2 * TILE, HEAD), lambda i, m: (0, i))
    local_rim = pl.BlockSpec((2, TILE, HEAD), lambda i, m: (0, 0, i))
    whole = pl.BlockSpec(norm.shape, lambda i, m: (0, 0))
    anywhere = pl.BlockSpec(memory_space=pl.ANY)
    wide = jax.ShapeDtypeStruct((2 * TILE, heads * HEAD), F32)
    rims = jax.ShapeDtypeStruct((2, TILE, heads * HEAD), BF16)
    flops = heads * 6 * 5 * 2 * TILE * TILE * HEAD
    return pl.pallas_call(
        attend_kernel,
        grid_spec=pltpu.PrefetchScalarGridSpec(
            num_scalar_prefetch=1,
            grid=(heads,),
            in_specs=[own, rim, own, rim, rim, own, rim, local, own, whole, anywhere],
            out_specs=[own, local, local, local_rim, local_rim],
            scratch_shapes=[
                pltpu.VMEM((4, TILE, HEAD), BF16),
                pltpu.VMEM((4, TILE, HEAD), BF16),
                pltpu.VMEM((4, TILE, HEAD), F32),
                pltpu.VMEM((4, TILE, HEAD), F32),
            ],
        ),
        out_shape=[jax.ShapeDtypeStruct(q.shape, BF16), wide, wide, rims, rims],
        input_output_aliases={11: 0},
        compiler_params=pltpu.CompilerParams(vmem_limit_bytes=32 << 20),
        cost_estimate=pl.CostEstimate(
            flops=3 * flops, bytes_accessed=heads * 3_000_000, transcendentals=heads * 6 * TILE * TILE
        ),
    )(meta, q, kb, ko, ka, vb, vo, va, g, o, norm, dq_full)


def combine_kernel(meta, dko, dvo, below, above, dk_in, dv_in, dk, dv):
    dk[:TILE] = ((dko[:TILE] + below[0].astype(F32)) * SCALE).astype(BF16)
    dk[TILE:] = ((dko[TILE:] + above[0].astype(F32)) * SCALE).astype(BF16)
    dv[:TILE] = (dvo[:TILE] + below[1].astype(F32)).astype(BF16)
    dv[TILE:] = (dvo[TILE:] + above[1].astype(F32)).astype(BF16)


def combine(meta, dko, dvo, below, above, dk_full, dv_full):
    width = dko.shape[1]
    own = pl.BlockSpec((2 * TILE, HEAD), lambda i, m: (0, i))
    rim = pl.BlockSpec((2, TILE, HEAD), lambda i, m: (0, 0, i))
    placed = pl.BlockSpec((2 * TILE, HEAD), lambda i, m: (0, i + m[6]))
    anywhere = pl.BlockSpec(memory_space=pl.ANY)
    full = jax.ShapeDtypeStruct(dk_full.shape, BF16)
    return pl.pallas_call(
        combine_kernel,
        grid_spec=pltpu.PrefetchScalarGridSpec(
            num_scalar_prefetch=1,
            grid=(width // HEAD,),
            in_specs=[own, own, rim, rim, anywhere, anywhere],
            out_specs=[placed, placed],
        ),
        out_shape=[full, full],
        input_output_aliases={5: 0, 6: 1},
        compiler_params=pltpu.CompilerParams(vmem_limit_bytes=16 << 20),
        cost_estimate=pl.CostEstimate(flops=4_000_000, bytes_accessed=8_000_000, transcendentals=0),
    )(meta, dko, dvo, below, above, dk_full, dv_full)


def body(query, key_states, value_states, attn_out, log_norm, out_grad, out_weight, tile_lists):
    grad_rows = out_grad[0]
    out_rows = attn_out[0]
    q, k, v = query[0], key_states[0], value_states[0]
    norm = log_norm[0]
    tokens, width = q.shape
    model = grad_rows.shape[1]
    n_dp = lax.axis_size("dp")
    n_seq = lax.axis_size("seq")
    dp = lax.axis_index("dp")
    seq = lax.axis_index("seq")
    y = dp // 2
    core = seq % 2
    n_y = n_dp // 2

    def over_dp(value, target):
        return lax.ppermute(value, "dp", [(i, target(i)) for i in range(n_dp)])

    def over_seq(value, target):
        pairs = [(i, target(i)) for i in range(n_seq)]
        return lax.ppermute(value, "seq", [(i, j) for i, j in pairs if 0 <= j < n_seq])

    def swap(value):
        return over_seq(value, lambda i: i ^ 1)

    def flip(value):
        return over_dp(value, lambda i: i ^ 1)

    def up(value):
        return over_dp(value, lambda i: (i + 2) % n_dp)

    def down(value):
        return over_dp(value, lambda i: (i - 2) % n_dp)

    def take(value, index):
        return lax.dynamic_index_in_dim(value, index, 0, keepdims=False)

    half = model // 2
    mine = lax.dynamic_slice_in_dim(out_weight, core * half, half, 1)
    other = flip(mine)
    low_first = dp % 2 == 0
    pair0 = jnp.concatenate(
        [jnp.where(low_first, mine, other), jnp.where(low_first, other, mine)], axis=0
    )
    k_before = over_seq(k[tokens - TILE :], lambda i: i + 1)
    v_before = over_seq(v[tokens - TILE :], lambda i: i + 1)
    k_after = over_seq(k[:TILE], lambda i: i - 1)
    v_after = over_seq(v[:TILE], lambda i: i - 1)
    from_up = down(pair0)
    from_down = up(pair0)
    rows = pair0.shape[0]
    far_low = up(from_down[: rows // 2])
    far_high = down(from_up[rows // 2 :])
    slabs = [pair0, from_up, from_down, jnp.concatenate([far_low, far_high], axis=0)]
    groups = [y, (y + 1) % n_y, (y + n_y - 1) % n_y, (y + 2) % n_y]

    first_tile = seq * 2 - 1
    slots = (lax.dynamic_slice_in_dim(tile_lists[0], seq * 2, 2, 0) - first_tile).reshape(-1)

    send_grad = lax.dynamic_slice_in_dim(grad_rows, (1 - core) * half, half, 1)
    keep_grad = lax.dynamic_slice_in_dim(grad_rows, core * half, half, 1)
    sent = swap(dot(out_rows, send_grad, TN).astype(BF16))
    kept = dot(out_rows, keep_grad, TN)
    chip_sum = (kept + sent.astype(F32)).astype(BF16).reshape(n_y, width // n_y, half)

    group_heads = width // n_y // HEAD
    dq = jnp.zeros((tokens, width), BF16)
    dk = jnp.zeros((tokens, width), BF16)
    dv = jnp.zeros((tokens, width), BF16)
    pending = []
    for slab, group in zip(slabs, groups):
        across = swap(slab)
        rows_here = jnp.concatenate(
            [jnp.where(core == 0, slab, across), jnp.where(core == 0, across, slab)], axis=1
        )
        g = dot(grad_rows, rows_here, NT).astype(BF16)
        meta = jnp.concatenate([slots, (group * group_heads)[None]]).astype(jnp.int32)
        dq, dko, dvo, low, high = attend(
            meta, q, k_before, k, k_after, v_before, v, v_after, g, out_rows, norm, dq
        )
        below = over_seq(high, lambda i: i + 1)
        above = over_seq(low, lambda i: i - 1)
        pending.append((meta, dko, dvo, below, above))

    quarter = width // n_y
    far = take(chip_sum, (y + 2) % n_y)
    add_low = up(far[: quarter // 2])
    add_high = down(far[quarter // 2 :])
    plus = take(chip_sum, (y + 1) % n_y)
    minus = take(chip_sum, (y + n_y - 1) % n_y)
    plus = jnp.concatenate(
        [(plus[: quarter // 2].astype(F32) + add_low.astype(F32)).astype(BF16), plus[quarter // 2 :]]
    )
    minus = jnp.concatenate(
        [minus[: quarter // 2], (minus[quarter // 2 :].astype(F32) + add_high.astype(F32)).astype(BF16)]
    )
    from_minus = up(plus)
    from_plus = down(minus)
    y_sum = take(chip_sum, y).astype(F32) + from_minus.astype(F32) + from_plus.astype(F32)
    y_sum = y_sum.reshape(2, quarter // 2, half)
    passed = flip(take(y_sum, 1 - dp % 2).astype(BF16))
    dp_sum = take(y_sum, dp % 2) + passed.astype(F32)
    x = (seq // 2) % 4
    n_x = 4
    piece = dp_sum.shape[0] // n_x

    def shift_x(i, by):
        return i // 8 * 8 + ((i // 2 + by) % n_x) * 2 + i % 2

    parts = dp_sum.reshape(n_x, piece, half)
    total = take(parts, x)
    for by in range(1, n_x):
        out = take(parts, (x + by) % n_x).astype(BF16)
        total = total + over_seq(out, lambda i, by=by: shift_x(i, by)).astype(F32)
    crossed = over_seq(total.astype(BF16), lambda i: (i + 8) % 16)
    total = (total.astype(BF16).astype(F32) + crossed.astype(F32)).astype(BF16)
    ready = jnp.zeros((n_x, piece, half), BF16)
    ready = lax.dynamic_update_index_in_dim(ready, total, x, 0)
    for by in range(1, n_x):
        got = over_seq(total, lambda i, by=by: shift_x(i, by))
        ready = lax.dynamic_update_index_in_dim(ready, got, (x + n_x - by) % n_x, 0)
    ready = ready.reshape(n_x * piece, half)
    partner = swap(ready)
    weight_grad = jnp.concatenate(
        [jnp.where(core == 0, ready, partner), jnp.where(core == 0, partner, ready)], axis=1
    ).astype(F32)

    for item in pending:
        dk, dv = combine(*item, dk, dv)
    return (dq[None], dk[None], dv[None], weight_grad)


def solution(mesh):
    placed = (
        P("dp", "seq", None),
        P("dp", "seq", None),
        P("dp", "seq", None),
        P("dp", "seq", None),
        P("dp", None, "seq"),
        P("dp", "seq", None),
        P("dp", None),
        P("dp", None, None),
    )
    return jax.shard_map(
        body,
        mesh=mesh,
        in_specs=placed,
        out_specs=(P("dp", "seq", None), P("dp", "seq", None), P("dp", "seq", None), P("dp", None)),
        check_vma=False,
    )
```

time: 1260 us -> 273 us (0.22); the launches traced: 1240 us -> 269 us
  local copies, waits for them, and re-layouts: 388 us -> 14.4 us
  blocking collectives: 340 us -> 0 us
  matrix products: 146 us -> 29.2 us
  starting transfers between devices: 186 us -> 100 us
  other arithmetic: 85.1 us -> 13.2 us
  Pallas kernels: 0 us -> 54.7 us
  loops' own time: 32.8 us -> 0 us
  between operations: 15.4 us -> 1.57 us
    unnamed x1 -> x0, blocking collectives: 340 us -> none
    unnamed x32 -> x0, starting transfers between devices: 167 us -> none
    reshape x28 -> x0, local copies, waits for them, and re-layouts: 143 us -> none  [the longest x8 51.5 us: attend_item(): key_part = jnp.einsum('hqk,qhd->khd', score_grad, query_heads, preferred_...]
    dot_general x30 -> x6, matrix products: 146 us -> 29.2 us  [dot(): return lax.dot_general(a, b, dims, preferred_element_type=F32)]
    unnamed x66 -> x35, local copies, waits for them, and re-layouts: 100 us -> 1.04 us
    ppermute x4 -> x35, starting transfers between devices: 19.1 us -> 100 us  [the longest x25 75.3 us: over_seq(): lax.ppermute(value, 'seq', [(i, j) for i, j in pairs if 0 <= j < n_seq])]
    pallas_call x0 -> x8, Pallas kernels: none -> 54.7 us  [the longest x4 44.9 us: attend(): pl.pallas_call(attend_kernel, grid_spec=pltpu.PrefetchScalarGridSpec(num_...]
    dynamic_update_slice x4 -> x1, other arithmetic: 46.5 us -> 0.04 us  [body(): ready = lax.dynamic_update_index_in_dim(ready, total, x, 0)]
  transfers between devices with their start and end apart: 38 -> 35, of which waited for: 7 -> 12; matrix products, arithmetic and copies ran while one was open for 76% -> 20% of each run, Pallas kernels for 0% -> 20%
where the time goes in v1:
time: 273 us; the launch traced here: 269 us
  starting transfers between devices  100 us (37%)
  waiting for transfers between devices  55.3 us (20%)
  Pallas kernels  54.7 us (20%)
  matrix products  29.2 us (11%)
  local copies, waits for them, and re-layouts  14.4 us (5%)
  other arithmetic  13.2 us (5%)
    ppermute x25, starting transfers between devices, over_seq(): lax.ppermute(value, 'seq', [(i, j) for i, j in pairs if 0 <= j < n_seq])  75.3 us
    pallas_call x4, Pallas kernels, attend(): pl.pallas_call(attend_kernel, grid_spec=pltpu.PrefetchScalarGridSpec(num_...  44.9 us
    ppermute x10, waiting for transfers between devices, over_dp(): return lax.ppermute(value, 'dp', [(i, target(i)) for i in range(n_dp)])  44.1 us
    dot_general x6, matrix products, dot(): return lax.dot_general(a, b, dims, preferred_element_type=F32)  29.2 us
    ppermute x10, starting transfers between devices, over_dp(): return lax.ppermute(value, 'dp', [(i, target(i)) for i in range(n_dp)])  25.1 us
    ppermute x25, waiting for transfers between devices, over_seq(): lax.ppermute(value, 'seq', [(i, j) for i, j in pairs if 0 <= j < n_seq])  11.2 us
    pallas_call x4, Pallas kernels, combine(): pl.pallas_call(combine_kernel, grid_spec=pltpu.PrefetchScalarGridSpec(num...  9.78 us
  transfers between devices with their start and end apart: 35, of which 12 were waited for; matrix products, arithmetic and copies ran while one was open for 20% of the time, Pallas kernels for 20%

profile of v1, /device:TPU:7, one launch (start us, length us, event | category | flops | bytes accessed | tf_op | source)
XLA Modules:
  0.0 268.8 jit_solution(16127045518873472119)
XLA Ops:
  1.8 1.7 collective-permute-start.4
  3.5 3.2 %slice_bitcast_fusion.2 = (bf16[384,1536]{1,0:T(8,128)(2,1)}, bf16[384,1536]{1,0:T(8,128)(2,1)}) fusion(bf16[1,768,1536]{2,1,0:T(8,128)(2,1)} %param.9), kind=kLoop, calls=%fused_computation.50 | loop fusion | bytes 4718592 | tf_op jit(solution)/shard_map/slice | solution.py:178
  6.7 2.9 %collective-permute-start.1 = (bf16[384,1536]{1,0:T(8,128)(2,1)}, bf16[384,1536]{1,0:T(8,128)(2,1)}, u32[]{:S(2)}, u32[]{:S(2)}) collective-permute-start(bf16[384,1536]{1,0:T(8,128)(2,1)} %get-tuple-element.78), channel_id=1, source_target_pairs={{1,0},{2,1},{3,2},{4,3},{5,4},{6,5},{7,6},{8,7},{9,8},{10,9},{11,1... | collective-permute-start | bytes 3538952 | tf_op jit(solution)/shard_map/ppermute | solution.py:152
  9.6 6.9 %collective-permute-done.4 = bf16[192,1536]{1,0:T(8,128)(2,1)S(1)} collective-permute-done((bf16[192,1536]{1,0:T(8,128)(2,1)S(1)}, bf16[192,1536]{1,0:T(8,128)(2,1)S(1)}, u32[]{:S(2)}, u32[]{:S(2)}) %collective-permute-start.4) | collective-permute-done | bytes 589856 | tf_op jit(solution)/shard_map/ppermute | solution.py:148
  20.0 2.7 %collective-permute-start.7 = (bf16[384,1536]{1,0:T(8,128)(2,1)}, bf16[384,1536]{1,0:T(8,128)(2,1)}, u32[]{:S(2)}, u32[]{:S(2)}) collective-permute-start(bf16[384,1536]{1,0:T(8,128)(2,1)} %pad_maximum_fusion), channel_id=1, source_target_pairs={{0,96},{16,112},{32,0},{48,16},{64,32},{80,48},{96,64},{112,80},{1... | collective-permute-start | bytes 3538952 | tf_op jit(solution)/shard_map/ppermute | solution.py:148
  22.7 7.2 %fusion.1 = bf16[1536,1536]{1,0:T(8,128)(2,1)} fusion(bf16[1,768,3072]{2,1,0:T(8,128)(2,1)} %param.13, s32[]{:T(128)S(6)} %select_n.189, bf16[1,768,1536]{2,1,0:T(8,128)(2,1)S(1)} %copy-done.5), kind=kOutput, calls=%fused_computation.3 | convolution fusion | flops 3626237952 | bytes 9437188 | tf_op jit(solution)/shard_map/dot_general | solution.py:23
  32.0 5.3 %collective-permute-start = (bf16[384,1536]{1,0:T(8,128)(2,1)}, bf16[384,1536]{1,0:T(8,128)(2,1)}, u32[]{:S(2)}, u32[]{:S(2)}) collective-permute-start(bf16[384,1536]{1,0:T(8,128)(2,1)} %get-tuple-element.79), channel_id=1, source_target_pairs={{0,1},{1,2},{2,3},{3,4},{4,5},{5,6},{6,7},{7,8},{8,9},{9,10},{10,1... | collective-permute-start | bytes 3538952 | tf_op jit(solution)/shard_map/ppermute | solution.py:152
  37.4 11.0 %collective-permute-done.7 = bf16[384,1536]{1,0:T(8,128)(2,1)} collective-permute-done((bf16[384,1536]{1,0:T(8,128)(2,1)}, bf16[384,1536]{1,0:T(8,128)(2,1)}, u32[]{:S(2)}, u32[]{:S(2)}) %collective-permute-start.7) | collective-permute-done | bytes 1179680 | tf_op jit(solution)/shard_map/ppermute | solution.py:148
  48.4 2.7 collective-permute-start.3
  51.5 6.2 %collective-permute-start.2 = (bf16[384,1536]{1,0:T(8,128)(2,1)}, bf16[384,1536]{1,0:T(8,128)(2,1)}, u32[]{:S(2)}, u32[]{:S(2)}) collective-permute-start(bf16[384,1536]{1,0:T(8,128)(2,1)} %get-tuple-element.77), channel_id=1, source_target_pairs={{0,1},{1,2},{2,3},{3,4},{4,5},{5,6},{6,7},{7,8},{8,9},{9,10},{10,1... | collective-permute-start | bytes 3538952 | tf_op jit(solution)/shard_map/ppermute | solution.py:152
  60.3 1.7 broadcast_select_fusion.1
  62.0 5.1 %fusion.47.g = bf16[768,384]{1,0:T(8,128)(2,1)S(1)} fusion(bf16[1,768,3072]{2,1,0:T(8,128)(2,1)} %param.13, bf16[384,1536]{1,0:T(8,128)(2,1)S(1)} %get-tuple-element.69, bf16[384,1536]{1,0:T(8,128)(2,1)S(1)} %get-tuple-element.68), kind=kOutput, calls=%fused_computation.34 | convolution fusion | flops 1816952832 | bytes 7667712 | tf_op jit(solution)/shard_map/dot_general | solution.py:23
  67.1 3.4 %collective-permute-start.8 = (bf16[192,1536]{1,0:T(8,128)(2,1)S(1)}, bf16[192,1536]{1,0:T(8,128)(2,1)S(1)}, u32[]{:S(2)}, u32[]{:S(2)}) collective-permute-start(bf16[192,1536]{1,0:T(8,128)(2,1)S(1)} %slice.83), channel_id=1, source_target_pairs={{0,96},{16,112},{32,0},{48,16},{64,32},{80,48},{96,64},{112,80},{1... | collective-permute-start | bytes 1769480 | tf_op jit(solution)/shard_map/ppermute | solution.py:148
  71.2 1.6 broadcast_1_dq_in_dk_in_dv_in.2.clone.dq_in
  72.8 11.3 %shard_map.111 = (bf16[768,1536]{1,0:T(8,128)(2,1)}, f32[768,384]{1,0:T(8,128)S(1)}, f32[768,384]{1,0:T(8,128)S(1)}, bf16[2,384,384]{2,1,0:T(8,128)(2,1)S(1)}, bf16[2,384,384]{2,1,0:T(8,128)(2,1)S(1)}) custom-call(s32[7]{0:T(128)S(1)} %get-tuple-element.87.meta, bf16[768,1536]{1,0:T(8,128)(2,1)S(1)} %bitcast.136, ...), custom_call_target="tpu_custom_call", output_to_operand_aliasing={{0}: (11, {})} | custom-call | flops 10192158720 | bytes 9000000 | tf_op jit(solution)/shard_map/pallas_call | solution.py:80
  84.0 8.0 %collective-permute-start.19 = (bf16[2,384,384]{2,1,0:T(8,128)(2,1)S(1)}, bf16[2,384,384]{2,1,0:T(8,128)(2,1)S(1)}, u32[]{:S(2)}, u32[]{:S(2)}) collective-permute-start(bf16[2,384,384]{2,1,0:T(8,128)(2,1)S(1)} %get-tuple-element.50), channel_id=1, source_target_pairs={{0,1},{1,2},{2,3},{3,4},{4,5},{5,6},{6,7},{7,8},{8,9},{9,10},{10,1... | collective-permute-start | bytes 1769480 | tf_op jit(solution)/shard_map/ppermute | solution.py:152
  92.0 1.9 collective-permute-start.20
  96.5 2.6 fusion.52.g
  99.1 6.6 %fusion = bf16[1536,1536]{1,0:T(8,128)(2,1)S(1)} fusion(bf16[1536,1536]{1,0:T(8,128)(2,1)} %collective-permute-done.21, bf16[1,768,3072]{2,1,0:T(8,128)(2,1)} %param.13, s32[]{:T(128)S(6)} %select_n.175, bf16[1,768,1536]{2,1,0:T(8,128)(2,1)S(1)} %copy-done.6), kind=kOutput, calls=%fused_computation.1 | convolution fusion | flops 3630956544 | bytes 14155780 | tf_op jit(solution)/shard_map/dot_general | solution.py:23
  106.5 2.7 %collective-permute-start.24 = (bf16[192,1536]{1,0:T(8,128)(2,1)S(1)}, bf16[192,1536]{1,0:T(8,128)(2,1)S(1)}, u32[]{:S(2)}, u32[]{:S(2)}) collective-permute-start(bf16[192,1536]{1,0:T(8,128)(2,1)S(1)} %get-tuple-element.66), channel_id=1, source_target_pairs={{0,96},{16,112},{32,0},{48,16},{64,32},{80,48},{96,64},{112,80},{1... | collective-permute-start | bytes 1769480 | tf_op jit(solution)/shard_map/ppermute | solution.py:148
  109.3 1.9 broadcast_select_fusion.5
  111.2 11.6 %collective-permute-done.22 = bf16[192,1536]{1,0:T(8,128)(2,1)S(1)} collective-permute-done((bf16[192,1536]{1,0:T(8,128)(2,1)S(1)}, bf16[192,1536]{1,0:T(8,128)(2,1)S(1)}, u32[]{:S(2)}, u32[]{:S(2)}) %collective-permute-start.22) | collective-permute-done | bytes 589856 | tf_op jit(solution)/shard_map/ppermute | solution.py:148
  124.3 2.6 collective-permute-start.25
  127.9 2.6 fusion.57.g
  130.6 11.2 %shard_map.112 = (bf16[768,1536]{1,0:T(8,128)(2,1)}, f32[768,384]{1,0:T(8,128)S(1)}, f32[768,384]{1,0:T(8,128)S(1)}, bf16[2,384,384]{2,1,0:T(8,128)(2,1)S(1)}, bf16[2,384,384]{2,1,0:T(8,128)(2,1)S(1)}) custom-call(s32[7]{0:T(128)S(1)} %get-tuple-element.89.meta, bf16[768,1536]{1,0:T(8,128)(2,1)S(1)} %bitcast.137, ...), custom_call_target="tpu_custom_call", output_to_operand_aliasing={{0}: (11, {})} | custom-call | flops 10192158720 | bytes 9000000 | tf_op jit(solution)/shard_map/pallas_call | solution.py:80
  141.8 9.9 %collective-permute-done.25 = bf16[384,1536]{1,0:T(8,128)(2,1)} collective-permute-done((bf16[384,1536]{1,0:T(8,128)(2,1)}, bf16[384,1536]{1,0:T(8,128)(2,1)}, u32[]{:S(2)}, u32[]{:S(2)}) %collective-permute-start.25) | collective-permute-done | bytes 1179680 | tf_op jit(solution)/shard_map/ppermute | solution.py:148
  151.6 4.2 %collective-permute-done.23 = bf16[384,1536]{1,0:T(8,128)(2,1)} collective-permute-done((bf16[384,1536]{1,0:T(8,128)(2,1)}, bf16[384,1536]{1,0:T(8,128)(2,1)}, u32[]{:S(2)}, u32[]{:S(2)}) %collective-permute-start.23) | collective-permute-done | bytes 1179680 | tf_op jit(solution)/shard_map/ppermute | solution.py:148
  155.8 2.0 fusion.22
  158.0 11.3 %collective-permute-start.26 = (bf16[192,1536]{1,0:T(8,128)(2,1)S(1)}, bf16[192,1536]{1,0:T(8,128)(2,1)S(1)}, u32[]{:S(2)}, u32[]{:S(2)}) collective-permute-start(bf16[192,1536]{1,0:T(8,128)(2,1)S(1)} %fusion.69), channel_id=1, source_target_pairs={{0,16},{16,0},{32,48},{48,32},{64,80},{80,64},{96,112},{112,96},{1... | collective-permute-start | bytes 1769480 | tf_op jit(solution)/shard_map/ppermute | solution.py:148
  169.2 11.2 %shard_map.113 = (bf16[768,1536]{1,0:T(8,128)(2,1)}, f32[768,384]{1,0:T(8,128)S(1)}, f32[768,384]{1,0:T(8,128)S(1)}, bf16[2,384,384]{2,1,0:T(8,128)(2,1)S(1)}, bf16[2,384,384]{2,1,0:T(8,128)(2,1)S(1)}) custom-call(s32[7]{0:T(128)S(1)} %get-tuple-element.88.meta, bf16[768,1536]{1,0:T(8,128)(2,1)S(1)} %bitcast.138, ...), custom_call_target="tpu_custom_call", output_to_operand_aliasing={{0}: (11, {})} | custom-call | flops 10192158720 | bytes 9000000 | tf_op jit(solution)/shard_map/pallas_call | solution.py:80
  182.5 2.4 collective-permute-done.27
  184.8 15.8 %collective-permute-start.17 = (bf16[2,384,384]{2,1,0:T(8,128)(2,1)S(1)}, bf16[2,384,384]{2,1,0:T(8,128)(2,1)S(1)}, u32[]{:S(2)}, u32[]{:S(2)}) collective-permute-start(bf16[2,384,384]{2,1,0:T(8,128)(2,1)S(1)} %get-tuple-element.46), channel_id=1, source_target_pairs={{0,1},{1,2},{2,3},{3,4},{4,5},{5,6},{6,7},{7,8},{8,9},{9,10},{10,1... | collective-permute-start | bytes 1769480 | tf_op jit(solution)/shard_map/ppermute | solution.py:152
  200.7 1.9 collective-permute-start.18
  202.8 5.1 %fusion.62.g = bf16[768,384]{1,0:T(8,128)(2,1)S(1)} fusion(bf16[1,768,3072]{2,1,0:T(8,128)(2,1)} %param.13, bf16[384,1536]{1,0:T(8,128)(2,1)S(1)} %get-tuple-element.75, bf16[384,1536]{1,0:T(8,128)(2,1)S(1)} %get-tuple-element.74), kind=kOutput, calls=%fused_computation.37 | convolution fusion | flops 1816952832 | bytes 7667712 | tf_op jit(solution)/shard_map/dot_general | solution.py:23
  208.4 4.7 %collective-permute-start.31 = (bf16[48,1536]{1,0:T(8,128)(2,1)S(1)}, bf16[48,1536]{1,0:T(8,128)(2,1)S(1)}, u32[]{:S(2)}, u32[]{:S(2)}) collective-permute-start(bf16[48,1536]{1,0:T(8,128)(2,1)S(1)} %get-tuple-element.61), channel_id=1, source_target_pairs={{0,2},{1,3},{2,4},{3,5},{4,6},{5,7},{6,0},{7,1},{8,10},{9,11},{10,... | collective-permute-start | bytes 442376 | tf_op jit(solution)/shard_map/ppermute | solution.py:152
  213.1 11.2 %shard_map.114 = (bf16[768,1536]{1,0:T(8,128)(2,1)}, f32[768,384]{1,0:T(8,128)S(1)}, f32[768,384]{1,0:T(8,128)S(1)}, bf16[2,384,384]{2,1,0:T(8,128)(2,1)S(1)}, bf16[2,384,384]{2,1,0:T(8,128)(2,1)S(1)}) custom-call(s32[7]{0:T(128)S(1)} %get-tuple-element.90.meta, bf16[768,1536]{1,0:T(8,128)(2,1)S(1)} %bitcast.139, ...), custom_call_target="tpu_custom_call", output_to_operand_aliasing={{0}: (11, {})} | custom-call | flops 10192158720 | bytes 9000000 | tf_op jit(solution)/shard_map/pallas_call | solution.py:80
  224.3 5.5 %collective-permute-done.32 = bf16[48,1536]{1,0:T(8,128)(2,1)S(1)} collective-permute-done((bf16[48,1536]{1,0:T(8,128)(2,1)S(1)}, bf16[48,1536]{1,0:T(8,128)(2,1)S(1)}, u32[]{:S(2)}, u32[]{:S(2)}) %collective-permute-start.32) | collective-permute-done | bytes 147488 | tf_op jit(solution)/shard_map/ppermute | solution.py:152
  229.8 10.4 %collective-permute-start.15 = (bf16[2,384,384]{2,1,0:T(8,128)(2,1)S(1)}, bf16[2,384,384]{2,1,0:T(8,128)(2,1)S(1)}, u32[]{:S(2)}, u32[]{:S(2)}) collective-permute-start(bf16[2,384,384]{2,1,0:T(8,128)(2,1)S(1)} %get-tuple-element.42), channel_id=1, source_target_pairs={{0,1},{1,2},{2,3},{3,4},{4,5},{5,6},{6,7},{7,8},{8,9},{9,10},{10,1... | collective-permute-start | bytes 1769480 | tf_op jit(solution)/shard_map/ppermute | solution.py:152
  240.3 1.9 collective-permute-start.16
  242.2 7.3 %collective-permute-start.13 = (bf16[2,384,384]{2,1,0:T(8,128)(2,1)S(1)}, bf16[2,384,384]{2,1,0:T(8,128)(2,1)S(1)}, u32[]{:S(2)}, u32[]{:S(2)}) collective-permute-start(bf16[2,384,384]{2,1,0:T(8,128)(2,1)S(1)} %get-tuple-element.38), channel_id=1, source_target_pairs={{0,1},{1,2},{2,3},{3,4},{4,5},{5,6},{6,7},{7,8},{8,9},{9,10},{10,1... | collective-permute-start | bytes 1769480 | tf_op jit(solution)/shard_map/ppermute | solution.py:152
  249.5 1.9 collective-permute-start.14
  251.6 1.6 broadcast_1_dq_in_dk_in_dv_in.2.clone.1.dv_in
  254.7 2.4 shard_map.115
  257.1 2.4 shard_map.116
  259.6 2.4 shard_map.117
  262.0 2.3 collective-permute-done.14.above
  264.3 2.4 shard_map.118
  266.9 1.7 maximum_convert_fusion
  (108 shorter events, 20.6 us)
Async XLA Ops:
  0.6 29.6 %copy-start = (s32[1,32,3]{1,0,2:T(1,128)S(1)}, s32[1,32,3]{1,0,2:T(1,128)}, u32[]{:S(2)}) copy-start(s32[1,32,3]{1,0,2:T(1,128)} %param.15) | copy-start | bytes 1156
  1.8 14.7 %copy-start.10 = (bf16[192,3072]{1,0:T(8,128)(2,1)S(1)}, bf16[192,3072]{1,0:T(8,128)(2,1)}, u32[]{:S(2)}) copy-start(bf16[192,3072]{1,0:T(8,128)(2,1)} %param.14) | copy-start | bytes 3538948
  1.8 14.7 %collective-permute-start.4 = (bf16[192,1536]{1,0:T(8,128)(2,1)S(1)}, bf16[192,1536]{1,0:T(8,128)(2,1)S(1)}, u32[]{:S(2)}, u32[]{:S(2)}) collective-permute-start(bf16[192,1536]{1,0:T(8,128)(2,1)S(1)} %constant_dynamic-slice_fusion), channel_id=1, source_target_pairs={{0,16},{16,0},{32,48},{48,32},{64,80},{80,64},{96,112},{112,96},{1... | collective-permute-start | bytes 1769480 | tf_op jit(solution)/shard_map/ppermute | solution.py:148
  6.7 60.4 %collective-permute-start.1 = (bf16[384,1536]{1,0:T(8,128)(2,1)}, bf16[384,1536]{1,0:T(8,128)(2,1)}, u32[]{:S(2)}, u32[]{:S(2)}) collective-permute-start(bf16[384,1536]{1,0:T(8,128)(2,1)} %get-tuple-element.78), channel_id=1, source_target_pairs={{1,0},{2,1},{3,2},{4,3},{5,4},{6,5},{7,6},{8,7},{9,8},{10,9},{11,1... | collective-permute-start | bytes 3538952 | tf_op jit(solution)/shard_map/ppermute | solution.py:152
  9.6 13.1 %copy-start.5 = (bf16[1,768,1536]{2,1,0:T(8,128)(2,1)S(1)}, bf16[1,768,1536]{2,1,0:T(8,128)(2,1)}, u32[]{:S(2)}) copy-start(bf16[1,768,1536]{2,1,0:T(8,128)(2,1)} %param.11) | copy-start | bytes 7077892
  18.6 11.8 %copy-start.3 = (bf16[1,768,1536]{2,1,0:T(8,128)(2,1)S(1)}, bf16[1,768,1536]{2,1,0:T(8,128)(2,1)}, u32[]{:S(2)}) copy-start(bf16[1,768,1536]{2,1,0:T(8,128)(2,1)} %param.10) | copy-start | bytes 7077892
  18.6 13.4 %collective-permute-start.12 = (bf16[384,1536]{1,0:T(8,128)(2,1)}, bf16[384,1536]{1,0:T(8,128)(2,1)}, u32[]{:S(2)}, u32[]{:S(2)}) collective-permute-start(bf16[384,1536]{1,0:T(8,128)(2,1)} %pad_maximum_fusion), channel_id=1, source_target_pairs={{0,1},{1,0},{2,3},{3,2},{4,5},{5,4},{6,7},{7,6},{8,9},{9,8},{10,11... | collective-permute-start | bytes 3538952 | tf_op jit(solution)/shard_map/ppermute | solution.py:152
  20.0 28.4 %collective-permute-start.7 = (bf16[384,1536]{1,0:T(8,128)(2,1)}, bf16[384,1536]{1,0:T(8,128)(2,1)}, u32[]{:S(2)}, u32[]{:S(2)}) collective-permute-start(bf16[384,1536]{1,0:T(8,128)(2,1)} %pad_maximum_fusion), channel_id=1, source_target_pairs={{0,96},{16,112},{32,0},{48,16},{64,32},{80,48},{96,64},{112,80},{1... | collective-permute-start | bytes 3538952 | tf_op jit(solution)/shard_map/ppermute | solution.py:148
  22.7 28.8 %collective-permute-start.5 = (bf16[384,1536]{1,0:T(8,128)(2,1)}, bf16[384,1536]{1,0:T(8,128)(2,1)}, u32[]{:S(2)}, u32[]{:S(2)}) collective-permute-start(bf16[384,1536]{1,0:T(8,128)(2,1)} %pad_maximum_fusion), channel_id=1, source_target_pairs={{0,32},{16,48},{32,64},{48,80},{64,96},{80,112},{96,0},{112,16},{1... | collective-permute-start | bytes 3538952 | tf_op jit(solution)/shard_map/ppermute | solution.py:148
  29.9 69.2 %collective-permute-start.21 = (bf16[1536,1536]{1,0:T(8,128)(2,1)}, bf16[1536,1536]{1,0:T(8,128)(2,1)}, u32[]{:S(2)}, u32[]{:S(2)}) collective-permute-start(bf16[1536,1536]{1,0:T(8,128)(2,1)} %fusion.1), channel_id=1, source_target_pairs={{0,1},{1,0},{2,3},{3,2},{4,5},{5,4},{6,7},{7,6},{8,9},{9,8},{10,11... | collective-permute-start | bytes 14155784 | tf_op jit(solution)/shard_map/ppermute | solution.py:152
  30.5 27.4 %copy-start.11 = (f32[1,12,768]{2,0,1:T(1,128)S(1)}, f32[1,12,768]{2,0,1:T(1,128)}, u32[]{:S(2)}) copy-start(f32[1,12,768]{2,0,1:T(1,128)} %param.12) | copy-start | bytes 110596
  32.0 38.4 %collective-permute-start = (bf16[384,1536]{1,0:T(8,128)(2,1)}, bf16[384,1536]{1,0:T(8,128)(2,1)}, u32[]{:S(2)}, u32[]{:S(2)}) collective-permute-start(bf16[384,1536]{1,0:T(8,128)(2,1)} %get-tuple-element.79), channel_id=1, source_target_pairs={{0,1},{1,2},{2,3},{3,4},{4,5},{5,6},{6,7},{7,8},{8,9},{9,10},{10,1... | collective-permute-start | bytes 3538952 | tf_op jit(solution)/shard_map/ppermute | solution.py:152
  48.4 22.0 %collective-permute-start.3 = (bf16[384,1536]{1,0:T(8,128)(2,1)}, bf16[384,1536]{1,0:T(8,128)(2,1)}, u32[]{:S(2)}, u32[]{:S(2)}) collective-permute-start(bf16[384,1536]{1,0:T(8,128)(2,1)} %get-tuple-element.76), channel_id=1, source_target_pairs={{1,0},{2,1},{3,2},{4,3},{5,4},{6,5},{7,6},{8,7},{9,8},{10,9},{11,1... | collective-permute-start | bytes 3538952 | tf_op jit(solution)/shard_map/ppermute | solution.py:152
  51.5 19.7 %collective-permute-start.2 = (bf16[384,1536]{1,0:T(8,128)(2,1)}, bf16[384,1536]{1,0:T(8,128)(2,1)}, u32[]{:S(2)}, u32[]{:S(2)}) collective-permute-start(bf16[384,1536]{1,0:T(8,128)(2,1)} %get-tuple-element.77), channel_id=1, source_target_pairs={{0,1},{1,2},{2,3},{3,4},{4,5},{5,6},{6,7},{7,8},{8,9},{9,10},{10,1... | collective-permute-start | bytes 3538952 | tf_op jit(solution)/shard_map/ppermute | solution.py:152
  62.0 10.8 %copy-start.4 = (bf16[1,768,1536]{2,1,0:T(8,128)(2,1)S(1)}, bf16[1,768,1536]{2,1,0:T(8,128)(2,1)}, u32[]{:S(2)}) copy-start(bf16[1,768,1536]{2,1,0:T(8,128)(2,1)} %param.8) | copy-start | bytes 7077892
  62.0 10.8 %copy-start.6 = (bf16[1,768,1536]{2,1,0:T(8,128)(2,1)S(1)}, bf16[1,768,1536]{2,1,0:T(8,128)(2,1)}, u32[]{:S(2)}) copy-start(bf16[1,768,1536]{2,1,0:T(8,128)(2,1)} %param.11) | copy-start | bytes 7077892
  67.1 5.7 %copy-start.2 = (bf16[1,768,1536]{2,1,0:T(8,128)(2,1)S(1)}, bf16[1,768,1536]{2,1,0:T(8,128)(2,1)}, u32[]{:S(2)}) copy-start(bf16[1,768,1536]{2,1,0:T(8,128)(2,1)} %param.9) | copy-start | bytes 7077892
  67.1 26.9 %collective-permute-start.8 = (bf16[192,1536]{1,0:T(8,128)(2,1)S(1)}, bf16[192,1536]{1,0:T(8,128)(2,1)S(1)}, u32[]{:S(2)}, u32[]{:S(2)}) collective-permute-start(bf16[192,1536]{1,0:T(8,128)(2,1)S(1)} %slice.83), channel_id=1, source_target_pairs={{0,96},{16,112},{32,0},{48,16},{64,32},{80,48},{96,64},{112,80},{1... | collective-permute-start | bytes 1769480 | tf_op jit(solution)/shard_map/ppermute | solution.py:148
  70.5 21.6 %collective-permute-start.6 = (bf16[192,1536]{1,0:T(8,128)(2,1)S(1)}, bf16[192,1536]{1,0:T(8,128)(2,1)S(1)}, u32[]{:S(2)}, u32[]{:S(2)}) collective-permute-start(bf16[192,1536]{1,0:T(8,128)(2,1)S(1)} %slice.82), channel_id=1, source_target_pairs={{0,32},{16,48},{32,64},{48,80},{64,96},{80,112},{96,0},{112,16},{1... | collective-permute-start | bytes 1769480 | tf_op jit(solution)/shard_map/ppermute | solution.py:148
  70.5 23.9 %collective-permute-start.11 = (bf16[384,1536]{1,0:T(8,128)(2,1)}, bf16[384,1536]{1,0:T(8,128)(2,1)S(1)}, u32[]{:S(2)}, u32[]{:S(2)}) collective-permute-start(bf16[384,1536]{1,0:T(8,128)(2,1)} %collective-permute-done.7), channel_id=1, source_target_pairs={{0,1},{1,0},{2,3},{3,2},{4,5},{5,4},{6,7},{7,6},{8,9},{9,8},{10,11... | collective-permute-start | bytes 3538952 | tf_op jit(solution)/shard_map/ppermute | solution.py:152
  71.2 25.2 %slice-start = ((s8[4718592]{0:T(1024)(128)(4,1)}), s8[4194304]{0:T(1024)(128)(4,1)S(1)}, s32[]{:S(2)}) async-start(s8[4718592]{0:T(1024)(128)(4,1)} %bitcast.155), calls=%async_computation | async-start | bytes 8388608
  72.8 23.7 %slice-start.1 = ((s8[4718592]{0:T(1024)(128)(4,1)}), s8[524288]{0:T(1024)(128)(4,1)S(1)}, s32[]{:S(2)}) async-start(s8[4718592]{0:T(1024)(128)(4,1)} %bitcast.155), calls=%async_computation.1 | async-start | bytes 1048576
  84.0 145.8 %collective-permute-start.19 = (bf16[2,384,384]{2,1,0:T(8,128)(2,1)S(1)}, bf16[2,384,384]{2,1,0:T(8,128)(2,1)S(1)}, u32[]{:S(2)}, u32[]{:S(2)}) collective-permute-start(bf16[2,384,384]{2,1,0:T(8,128)(2,1)S(1)} %get-tuple-element.50), channel_id=1, source_target_pairs={{0,1},{1,2},{2,3},{3,4},{4,5},{5,6},{6,7},{7,8},{8,9},{9,10},{10,1... | collective-permute-start | bytes 1769480 | tf_op jit(solution)/shard_map/ppermute | solution.py:152
  92.0 148.3 %collective-permute-start.20 = (bf16[2,384,384]{2,1,0:T(8,128)(2,1)S(1)}, bf16[2,384,384]{2,1,0:T(8,128)(2,1)S(1)}, u32[]{:S(2)}, u32[]{:S(2)}) collective-permute-start(bf16[2,384,384]{2,1,0:T(8,128)(2,1)S(1)} %get-tuple-element.51), channel_id=1, source_target_pairs={{1,0},{2,1},{3,2},{4,3},{5,4},{6,5},{7,6},{8,7},{9,8},{10,9},{11,1... | collective-permute-start | bytes 1769480 | tf_op jit(solution)/shard_map/ppermute | solution.py:152
  94.0 12.5 %collective-permute-start.10 = (bf16[384,1536]{1,0:T(8,128)(2,1)}, bf16[384,1536]{1,0:T(8,128)(2,1)}, u32[]{:S(2)}, u32[]{:S(2)}) collective-permute-start(bf16[384,1536]{1,0:T(8,128)(2,1)} %collective-permute-done.5), channel_id=1, source_target_pairs={{0,1},{1,0},{2,3},{3,2},{4,5},{5,4},{6,7},{7,6},{8,9},{9,8},{10,11... | collective-permute-start | bytes 3538952 | tf_op jit(solution)/shard_map/ppermute | solution.py:152
  94.4 87.9 %collective-permute-start.9 = (bf16[384,1536]{1,0:T(8,128)(2,1)S(1)}, bf16[384,1536]{1,0:T(8,128)(2,1)S(1)}, u32[]{:S(2)}, u32[]{:S(2)}) collective-permute-start(bf16[384,1536]{1,0:T(8,128)(2,1)S(1)} %constant_dynamic-update-slice_fusion), channel_id=1, source_target_pairs={{0,1},{1,0},{2,3},{3,2},{4,5},{5,4},{6,7},{7,6},{8,9},{9,8},{10,11... | collective-permute-start | bytes 3538952 | tf_op jit(solution)/shard_map/ppermute | solution.py:152
  105.8 17.0 %collective-permute-start.22 = (bf16[192,1536]{1,0:T(8,128)(2,1)S(1)}, bf16[192,1536]{1,0:T(8,128)(2,1)S(1)}, u32[]{:S(2)}, u32[]{:S(2)}) collective-permute-start(bf16[192,1536]{1,0:T(8,128)(2,1)S(1)} %get-tuple-element.64), channel_id=1, source_target_pairs={{0,32},{16,48},{32,64},{48,80},{64,96},{80,112},{96,0},{112,16},{1... | collective-permute-start | bytes 1769480 | tf_op jit(solution)/shard_map/ppermute | solution.py:148
  106.5 16.3 %collective-permute-start.24 = (bf16[192,1536]{1,0:T(8,128)(2,1)S(1)}, bf16[192,1536]{1,0:T(8,128)(2,1)S(1)}, u32[]{:S(2)}, u32[]{:S(2)}) collective-permute-start(bf16[192,1536]{1,0:T(8,128)(2,1)S(1)} %get-tuple-element.66), channel_id=1, source_target_pairs={{0,96},{16,112},{32,0},{48,16},{64,32},{80,48},{96,64},{112,80},{1... | collective-permute-start | bytes 1769480 | tf_op jit(solution)/shard_map/ppermute | solution.py:148
  109.3 18.7 %slice-start.2 = ((s8[4718592]{0:T(1024)(128)(4,1)}), s8[4194304]{0:T(1024)(128)(4,1)S(1)}, s32[]{:S(2)}) async-start(s8[4718592]{0:T(1024)(128)(4,1)} %bitcast.157), calls=%async_computation.2 | async-start | bytes 8388608
  111.2 16.7 %slice-start.3 = ((s8[4718592]{0:T(1024)(128)(4,1)}), s8[524288]{0:T(1024)(128)(4,1)S(1)}, s32[]{:S(2)}) async-start(s8[4718592]{0:T(1024)(128)(4,1)} %bitcast.157), calls=%async_computation.3 | async-start | bytes 1048576
  124.3 27.4 %collective-permute-start.25 = (bf16[384,1536]{1,0:T(8,128)(2,1)}, bf16[384,1536]{1,0:T(8,128)(2,1)}, u32[]{:S(2)}, u32[]{:S(2)}) collective-permute-start(bf16[384,1536]{1,0:T(8,128)(2,1)} %pad_maximum_fusion.2), channel_id=1, source_target_pairs={{0,96},{16,112},{32,0},{48,16},{64,32},{80,48},{96,64},{112,80},{1... | collective-permute-start | bytes 3538952 | tf_op jit(solution)/shard_map/ppermute | solution.py:148
  127.9 27.9 %collective-permute-start.23 = (bf16[384,1536]{1,0:T(8,128)(2,1)}, bf16[384,1536]{1,0:T(8,128)(2,1)}, u32[]{:S(2)}, u32[]{:S(2)}) collective-permute-start(bf16[384,1536]{1,0:T(8,128)(2,1)} %pad_maximum_fusion.1), channel_id=1, source_target_pairs={{0,32},{16,48},{32,64},{48,80},{64,96},{80,112},{96,0},{112,16},{1... | collective-permute-start | bytes 3538952 | tf_op jit(solution)/shard_map/ppermute | solution.py:148
  158.0 22.6 %collective-permute-start.26 = (bf16[192,1536]{1,0:T(8,128)(2,1)S(1)}, bf16[192,1536]{1,0:T(8,128)(2,1)S(1)}, u32[]{:S(2)}, u32[]{:S(2)}) collective-permute-start(bf16[192,1536]{1,0:T(8,128)(2,1)S(1)} %fusion.69), channel_id=1, source_target_pairs={{0,16},{16,0},{32,48},{48,32},{64,80},{80,64},{96,112},{112,96},{1... | collective-permute-start | bytes 1769480 | tf_op jit(solution)/shard_map/ppermute | solution.py:148
  180.8 4.1 %collective-permute-start.27 = (bf16[48,1536]{1,0:T(8,128)(2,1)S(1)}, bf16[48,1536]{1,0:T(8,128)(2,1)S(1)}, u32[]{:S(2)}, u32[]{:S(2)}) collective-permute-start(bf16[48,1536]{1,0:T(8,128)(2,1)S(1)} %get-tuple-element.82), channel_id=1, source_target_pairs={{0,2},{1,3},{2,4},{3,5},{4,6},{5,7},{6,0},{7,1},{8,10},{9,11},{10,... | collective-permute-start | bytes 442376 | tf_op jit(solution)/shard_map/ppermute | solution.py:152
  180.9 19.8 %collective-permute-start.29 = (bf16[48,1536]{1,0:T(8,128)(2,1)S(1)}, bf16[48,1536]{1,0:T(8,128)(2,1)S(1)}, u32[]{:S(2)}, u32[]{:S(2)}) collective-permute-start(bf16[48,1536]{1,0:T(8,128)(2,1)S(1)} %get-tuple-element.83), channel_id=1, source_target_pairs={{0,6},{1,7},{2,0},{3,1},{4,2},{5,3},{6,4},{7,5},{8,14},{9,15},{10,... | collective-permute-start | bytes 442376 | tf_op jit(solution)/shard_map/ppermute | solution.py:152
  182.3 20.3 %collective-permute-start.28 = (bf16[48,1536]{1,0:T(8,128)(2,1)S(1)}, bf16[48,1536]{1,0:T(8,128)(2,1)S(1)}, u32[]{:S(2)}, u32[]{:S(2)}) collective-permute-start(bf16[48,1536]{1,0:T(8,128)(2,1)S(1)} %get-tuple-element.84), channel_id=1, source_target_pairs={{0,4},{1,5},{2,6},{3,7},{4,0},{5,1},{6,2},{7,3},{8,12},{9,13},{10,... | collective-permute-start | bytes 442376 | tf_op jit(solution)/shard_map/ppermute | solution.py:152
  184.8 57.4 %collective-permute-start.17 = (bf16[2,384,384]{2,1,0:T(8,128)(2,1)S(1)}, bf16[2,384,384]{2,1,0:T(8,128)(2,1)S(1)}, u32[]{:S(2)}, u32[]{:S(2)}) collective-permute-start(bf16[2,384,384]{2,1,0:T(8,128)(2,1)S(1)} %get-tuple-element.46), channel_id=1, source_target_pairs={{0,1},{1,2},{2,3},{3,4},{4,5},{5,6},{6,7},{7,8},{8,9},{9,10},{10,1... | collective-permute-start | bytes 1769480 | tf_op jit(solution)/shard_map/ppermute | solution.py:152
  200.7 50.8 %collective-permute-start.18 = (bf16[2,384,384]{2,1,0:T(8,128)(2,1)S(1)}, bf16[2,384,384]{2,1,0:T(8,128)(2,1)S(1)}, u32[]{:S(2)}, u32[]{:S(2)}) collective-permute-start(bf16[2,384,384]{2,1,0:T(8,128)(2,1)S(1)} %get-tuple-element.47), channel_id=1, source_target_pairs={{1,0},{2,1},{3,2},{4,3},{5,4},{6,5},{7,6},{8,7},{9,8},{10,9},{11,1... | collective-permute-start | bytes 1769480 | tf_op jit(solution)/shard_map/ppermute | solution.py:152
  202.7 5.6 %collective-permute-start.30 = (bf16[48,1536]{1,0:T(8,128)(2,1)S(1)}, bf16[48,1536]{1,0:T(8,128)(2,1)S(1)}, u32[]{:S(2)}, u32[]{:S(2)}) collective-permute-start(bf16[48,1536]{1,0:T(8,128)(2,1)S(1)} %fusion.72), channel_id=1, source_target_pairs={{0,8},{1,9},{2,10},{3,11},{4,12},{5,13},{6,14},{7,15},{8,0},{9,1},... | collective-permute-start | bytes 442376 | tf_op jit(solution)/shard_map/ppermute | solution.py:152
  202.8 10.3 %copy-start.7 = (bf16[1,768,1536]{2,1,0:T(8,128)(2,1)S(1)}, bf16[1,768,1536]{2,1,0:T(8,128)(2,1)}, u32[]{:S(2)}) copy-start(bf16[1,768,1536]{2,1,0:T(8,128)(2,1)} %param.11) | copy-start | bytes 7077892
  208.4 15.9 %collective-permute-start.31 = (bf16[48,1536]{1,0:T(8,128)(2,1)S(1)}, bf16[48,1536]{1,0:T(8,128)(2,1)S(1)}, u32[]{:S(2)}, u32[]{:S(2)}) collective-permute-start(bf16[48,1536]{1,0:T(8,128)(2,1)S(1)} %get-tuple-element.61), channel_id=1, source_target_pairs={{0,2},{1,3},{2,4},{3,5},{4,6},{5,7},{6,0},{7,1},{8,10},{9,11},{10,... | collective-permute-start | bytes 442376 | tf_op jit(solution)/shard_map/ppermute | solution.py:152
  224.3 5.5 %collective-permute-start.32 = (bf16[48,1536]{1,0:T(8,128)(2,1)S(1)}, bf16[48,1536]{1,0:T(8,128)(2,1)S(1)}, u32[]{:S(2)}, u32[]{:S(2)}) collective-permute-start(bf16[48,1536]{1,0:T(8,128)(2,1)S(1)} %get-tuple-element.61), channel_id=1, source_target_pairs={{0,4},{1,5},{2,6},{3,7},{4,0},{5,1},{6,2},{7,3},{8,12},{9,13},{10,... | collective-permute-start | bytes 442376 | tf_op jit(solution)/shard_map/ppermute | solution.py:152
  229.8 19.7 %collective-permute-start.33 = (bf16[48,1536]{1,0:T(8,128)(2,1)S(1)}, bf16[48,1536]{1,0:T(8,128)(2,1)S(1)}, u32[]{:S(2)}, u32[]{:S(2)}) collective-permute-start(bf16[48,1536]{1,0:T(8,128)(2,1)S(1)} %get-tuple-element.61), channel_id=1, source_target_pairs={{0,6},{1,7},{2,0},{3,1},{4,2},{5,3},{6,4},{7,5},{8,14},{9,15},{10,... | collective-permute-start | bytes 442376 | tf_op jit(solution)/shard_map/ppermute | solution.py:152
  229.8 29.7 %collective-permute-start.15 = (bf16[2,384,384]{2,1,0:T(8,128)(2,1)S(1)}, bf16[2,384,384]{2,1,0:T(8,128)(2,1)S(1)}, u32[]{:S(2)}, u32[]{:S(2)}) collective-permute-start(bf16[2,384,384]{2,1,0:T(8,128)(2,1)S(1)} %get-tuple-element.42), channel_id=1, source_target_pairs={{0,1},{1,2},{2,3},{3,4},{4,5},{5,6},{6,7},{7,8},{8,9},{9,10},{10,1... | collective-permute-start | bytes 1769480 | tf_op jit(solution)/shard_map/ppermute | solution.py:152
  240.3 19.3 %collective-permute-start.16 = (bf16[2,384,384]{2,1,0:T(8,128)(2,1)S(1)}, bf16[2,384,384]{2,1,0:T(8,128)(2,1)S(1)}, u32[]{:S(2)}, u32[]{:S(2)}) collective-permute-start(bf16[2,384,384]{2,1,0:T(8,128)(2,1)S(1)} %get-tuple-element.43), channel_id=1, source_target_pairs={{1,0},{2,1},{3,2},{4,3},{5,4},{6,5},{7,6},{8,7},{9,8},{10,9},{11,1... | collective-permute-start | bytes 1769480 | tf_op jit(solution)/shard_map/ppermute | solution.py:152
  242.2 19.8 %collective-permute-start.13 = (bf16[2,384,384]{2,1,0:T(8,128)(2,1)S(1)}, bf16[2,384,384]{2,1,0:T(8,128)(2,1)S(1)}, u32[]{:S(2)}, u32[]{:S(2)}) collective-permute-start(bf16[2,384,384]{2,1,0:T(8,128)(2,1)S(1)} %get-tuple-element.38), channel_id=1, source_target_pairs={{0,1},{1,2},{2,3},{3,4},{4,5},{5,6},{6,7},{7,8},{8,9},{9,10},{10,1... | collective-permute-start | bytes 1769480 | tf_op jit(solution)/shard_map/ppermute | solution.py:152
  249.5 14.8 %collective-permute-start.14 = (bf16[2,384,384]{2,1,0:T(8,128)(2,1)S(1)}, bf16[2,384,384]{2,1,0:T(8,128)(2,1)S(1)}, u32[]{:S(2)}, u32[]{:S(2)}) collective-permute-start(bf16[2,384,384]{2,1,0:T(8,128)(2,1)S(1)} %get-tuple-element.39), channel_id=1, source_target_pairs={{1,0},{2,1},{3,2},{4,3},{5,4},{6,5},{7,6},{8,7},{9,8},{10,9},{11,1... | collective-permute-start | bytes 1769480 | tf_op jit(solution)/shard_map/ppermute | solution.py:152
  251.5 15.3 %collective-permute-start.34 = (bf16[192,1536]{1,0:T(8,128)(2,1)S(1)}, bf16[192,1536]{1,0:T(8,128)(2,1)S(1)}, u32[]{:S(2)}, u32[]{:S(2)}) collective-permute-start(bf16[192,1536]{1,0:T(8,128)(2,1)S(1)} %bitcast.153), channel_id=1, source_target_pairs={{0,1},{1,0},{2,3},{3,2},{4,5},{5,4},{6,7},{7,6},{8,9},{9,8},{10,11... | collective-permute-start | bytes 1769480 | tf_op jit(solution)/shard_map/ppermute | solution.py:152
  (3 other events, 4.9 us)

commit v2 on v1

v2 whole, which is shorter than its diff:
```python
import functools
import math

import jax
import jax.numpy as jnp
from jax import lax
from jax.experimental import pallas as pl
from jax.experimental.pallas import tpu as pltpu
from jax.sharding import PartitionSpec as P

TILE = 384
HEAD = 128
LOG2E = math.log2(math.e)
SCALE = 1.0 / math.sqrt(HEAD)
F32 = jnp.float32
BF16 = jnp.bfloat16
NT = (((1,), (1,)), ((), ()))
NN = (((1,), (0,)), ((), ()))
TN = (((0,), (0,)), ((), ()))


def dot(a, b, dims):
    return lax.dot_general(a, b, dims, preferred_element_type=F32)


HEADS_AT = 7


def attend_kernel(slabs, *refs):
    meta, q, kb, ko, ka, vb, vo, va, near, away, o, norm = refs[:12]
    weights_in = refs[12 : 12 + 2 * slabs]
    dq, dko, dvo, low, high, kw, vw, dka, dva, gs = refs[13 + 2 * slabs :]
    step = pl.program_id(0)
    head = meta[HEADS_AT + step]
    per = gs.shape[0]
    for n in range(slabs):

        @pl.when(step == n * per)
        def _(n=n):
            made = dot(near[...], weights_in[2 * n][...], NT)
            made += dot(away[...], weights_in[2 * n + 1][...], NT)
            for m in range(per):
                gs[m] = made[:, m * HEAD : (m + 1) * HEAD].astype(BF16)

    g = gs.at[lax.rem(step, per)]
    kw[0] = kb[0]
    kw[1] = ko[:TILE]
    kw[2] = ko[TILE:]
    kw[3] = ka[0]
    vw[0] = vb[0]
    vw[1] = vo[:TILE]
    vw[2] = vo[TILE:]
    vw[3] = va[0]
    dka[...] = jnp.zeros_like(dka)
    dva[...] = jnp.zeros_like(dva)
    ones = jnp.ones((16, HEAD), BF16)
    for t in range(2):
        rows = slice(t * TILE, (t + 1) * TILE)
        qt = q[rows, :]
        gt = g[rows, :]
        prod = gt.astype(F32) * o[rows, :].astype(F32)
        coarse = prod.astype(BF16)
        fine = (prod - coarse.astype(F32)).astype(BF16)
        delta = (dot(ones, coarse, NT) + dot(ones, fine, NT))[0:1]
        shift = norm[pl.ds(head, 1), rows] * LOG2E
        total = None
        for j in range(3):
            slot = meta[t * 3 + j]
            k = kw[slot]
            weights = jnp.exp2(dot(k, qt, NT) * (SCALE * LOG2E) - shift)
            score_grad = (weights * (dot(vw[slot], gt, NT) - delta)).astype(BF16)
            dva[slot] += dot(weights.astype(BF16), gt, NN)
            dka[slot] += dot(score_grad, qt, NN)
            part = dot(k, score_grad, TN)
            total = part if total is None else total + part
        dq[rows, :] = (total * SCALE).T.astype(BF16)
    dko[...] = dka[1:3].reshape(2 * TILE, HEAD)
    dvo[...] = dva[1:3].reshape(2 * TILE, HEAD)
    low[0] = dka[0].astype(BF16)
    low[1] = dva[0].astype(BF16)
    high[0] = dka[3].astype(BF16)
    high[1] = dva[3].astype(BF16)


def attend(meta, q, k, v, before, after, grads, o, norm, slabs, dq_full):
    per = slabs[0][0].shape[0] // HEAD
    heads = per * len(slabs)
    half = slabs[0][0].shape[1]
    own = pl.BlockSpec((2 * TILE, HEAD), lambda i, m: (0, m[HEADS_AT + i]))
    rim_k = pl.BlockSpec((1, TILE, HEAD), lambda i, m: (0, 0, m[HEADS_AT + i]))
    rim_v = pl.BlockSpec((1, TILE, HEAD), lambda i, m: (1, 0, m[HEADS_AT + i]))
    local = pl.BlockSpec((2 * TILE, HEAD), lambda i, m: (0, i))
    local_rim = pl.BlockSpec((2, TILE, HEAD), lambda i, m: (0, 0, i))
    near = pl.BlockSpec((2 * TILE, half), lambda i, m: (0, m[6]))
    away = pl.BlockSpec((2 * TILE, half), lambda i, m: (0, 1 - m[6]))
    slab = pl.BlockSpec((per * HEAD, half), lambda i, m: (0, 0))
    whole = pl.BlockSpec(norm.shape, lambda i, m: (0, 0))
    anywhere = pl.BlockSpec(memory_space=pl.ANY)
    wide = jax.ShapeDtypeStruct((2 * TILE, heads * HEAD), F32)
    rims = jax.ShapeDtypeStruct((2, TILE, heads * HEAD), BF16)
    flops = heads * (6 * 5 * 2 * TILE * TILE * HEAD * 3 + 2 * 2 * TILE * 2 * half * HEAD)
    flat = [w for pair in slabs for w in pair]
    return pl.pallas_call(
        functools.partial(attend_kernel, len(slabs)),
        grid_spec=pltpu.PrefetchScalarGridSpec(
            num_scalar_prefetch=1,
            grid=(heads,),
            in_specs=[own, rim_k, own, rim_k, rim_v, own, rim_v, near, away, own, whole]
            + [slab] * len(flat)
            + [anywhere],
            out_specs=[own, local, local, local_rim, local_rim],
            scratch_shapes=[
                pltpu.VMEM((4, TILE, HEAD), BF16),
                pltpu.VMEM((4, TILE, HEAD), BF16),
                pltpu.VMEM((4, TILE, HEAD), F32),
                pltpu.VMEM((4, TILE, HEAD), F32),
                pltpu.VMEM((per, 2 * TILE, HEAD), BF16),
            ],
        ),
        out_shape=[jax.ShapeDtypeStruct(q.shape, BF16), wide, wide, rims, rims],
        input_output_aliases={12 + len(flat): 0},
        compiler_params=pltpu.CompilerParams(vmem_limit_bytes=40 << 20),
        cost_estimate=pl.CostEstimate(
            flops=flops, bytes_accessed=heads * 3_000_000, transcendentals=heads * 6 * TILE * TILE
        ),
    )(meta, q, before, k, after, before, v, after, grads, grads, o, norm, *flat, dq_full)


def combine_kernel(meta, dko, dvo, below, above, dk_in, dv_in, dk, dv):
    dk[:TILE] = ((dko[:TILE] + below[0].astype(F32)) * SCALE).astype(BF16)
    dk[TILE:] = ((dko[TILE:] + above[0].astype(F32)) * SCALE).astype(BF16)
    dv[:TILE] = (dvo[:TILE] + below[1].astype(F32)).astype(BF16)
    dv[TILE:] = (dvo[TILE:] + above[1].astype(F32)).astype(BF16)


def combine(meta, dko, dvo, below, above, dk_full, dv_full):
    width = dko.shape[1]
    own = pl.BlockSpec((2 * TILE, HEAD), lambda i, m: (0, i))
    rim = pl.BlockSpec((2, TILE, HEAD), lambda i, m: (0, 0, i))
    placed = pl.BlockSpec((2 * TILE, HEAD), lambda i, m: (0, m[HEADS_AT + i]))
    anywhere = pl.BlockSpec(memory_space=pl.ANY)
    full = jax.ShapeDtypeStruct(dk_full.shape, BF16)
    return pl.pallas_call(
        combine_kernel,
        grid_spec=pltpu.PrefetchScalarGridSpec(
            num_scalar_prefetch=1,
            grid=(width // HEAD,),
            in_specs=[own, own, rim, rim, anywhere, anywhere],
            out_specs=[placed, placed],
        ),
        out_shape=[full, full],
        input_output_aliases={5: 0, 6: 1},
        compiler_params=pltpu.CompilerParams(vmem_limit_bytes=16 << 20),
        cost_estimate=pl.CostEstimate(
            flops=4_000_000, bytes_accessed=width * 20_000, transcendentals=0
        ),
    )(meta, dko, dvo, below, above, dk_full, dv_full)


def product_kernel(which, a, b, *refs):
    out, turned = refs[-2:]

    @pl.when(pl.program_id(1) == 0)
    def _():
        turned[...] = a[...].T

    made = dot(turned[...], b[...], NN)
    zs, xs, ds, rows, columns = out.shape
    for d in range(ds):
        for z in range(zs):
            for x in range(xs):
                at = (d * zs + z) * rows
                part = made[at : at + rows, x * columns : (x + 1) * columns]
                if len(refs) == 3:
                    part = part + refs[0][z, x, d].astype(F32)
                out[z, x, d] = part.astype(BF16)


def product(which, a, b, n_z, n_x, n_dp, *added):
    tokens, width = a.shape
    half = b.shape[1] // 2
    rows, columns = width // n_dp // n_z, half // n_x
    shape = (n_z, n_x, n_dp, rows, columns)
    block = pl.BlockSpec((n_z, 2, 2, rows, columns), lambda i, j, m: (0, j, i, 0, 0))
    steps = n_x // 2
    return pl.pallas_call(
        product_kernel,
        grid_spec=pltpu.PrefetchScalarGridSpec(
            num_scalar_prefetch=1,
            grid=(n_dp // 2, steps),
            in_specs=[
                pl.BlockSpec((tokens, 2 * n_z * rows), lambda i, j, m: (0, i)),
                pl.BlockSpec((tokens, 2 * columns), lambda i, j, m: (0, m[0] * steps + j)),
            ]
            + [block] * len(added),
            out_specs=block,
            scratch_shapes=[pltpu.VMEM((2 * n_z * rows, tokens), BF16)],
        ),
        out_shape=jax.ShapeDtypeStruct(shape, BF16),
        compiler_params=pltpu.CompilerParams(vmem_limit_bytes=40 << 20),
        cost_estimate=pl.CostEstimate(
            flops=2 * 2 * tokens * width * half, bytes_accessed=20_000_000, transcendentals=0
        ),
    )(which, a, b, *added)


def body(query, key_states, value_states, attn_out, log_norm, out_grad, out_weight, tile_lists):
    grad_rows = out_grad[0]
    out_rows = attn_out[0]
    q, k, v = query[0], key_states[0], value_states[0]
    norm = log_norm[0]
    tokens, width = q.shape
    model = grad_rows.shape[1]
    n_dp = lax.axis_size("dp")
    n_seq = lax.axis_size("seq")
    dp = lax.axis_index("dp")
    seq = lax.axis_index("seq")
    y = dp // 2
    core = seq % 2
    n_y = n_dp // 2
    n_x = 4
    n_z = n_seq // 2 // n_x

    def over_dp(value, target):
        return lax.ppermute(value, "dp", [(i, target(i)) for i in range(n_dp)])

    def over_seq(value, target):
        pairs = [(i, target(i)) for i in range(n_seq)]
        return lax.ppermute(value, "seq", [(i, j) for i, j in pairs if 0 <= j < n_seq])

    def swap(value):
        return over_seq(value, lambda i: i ^ 1)

    def up(value):
        return over_dp(value, lambda i: (i + 2) % n_dp)

    def down(value):
        return over_dp(value, lambda i: (i - 2) % n_dp)

    half = model // 2
    mine = lax.dynamic_slice_in_dim(out_weight, core * half, half, 1)
    other = over_dp(mine, lambda i: i ^ 1)
    before = over_seq(jnp.stack([k[tokens - TILE :], v[tokens - TILE :]]), lambda i: i + 1)
    after = over_seq(jnp.stack([k[:TILE], v[:TILE]]), lambda i: i - 1)
    low_first = dp % 2 == 0
    pair0 = jnp.concatenate(
        [jnp.where(low_first, mine, other), jnp.where(low_first, other, mine)], axis=0
    )
    from_up = up(pair0)
    from_down = down(pair0)
    far = up(from_up)
    order = [[(pair0, y)], [(from_up, y + n_y - 1), (from_down, y + 1)], [(far, y + 2)]]

    first_tile = seq * 2 - 1
    slots = (lax.dynamic_slice_in_dim(tile_lists[0], seq * 2, 2, 0) - first_tile).reshape(-1)

    sent = product((1 - core)[None], out_rows, grad_rows, n_z, n_x, n_dp)
    chip_sum = product(core[None], out_rows, grad_rows, n_z, n_x, n_dp, swap(sent))
    chips = [[2 * i + c for i in range(n_seq // 2)] for c in range(2)]
    piece = chip_sum.shape[-2:]
    spread = lax.all_to_all(
        chip_sum.reshape(n_seq // 2, n_dp, *piece), "seq", 0, 0, axis_index_groups=chips
    )
    clip_sum = spread.astype(F32).sum(0).astype(BF16)

    per = width // n_y // HEAD
    dq = jnp.zeros((tokens, width), BF16)
    dk = jnp.zeros((tokens, width), BF16)
    dv = jnp.zeros((tokens, width), BF16)
    pending = []
    for group in order:
        slabs = [(slab, swap(slab)) for slab, _ in group]
        heads = [(at % n_y) * per + jnp.arange(per, dtype=jnp.int32) for _, at in group]
        meta = jnp.concatenate([slots, core[None], *heads]).astype(jnp.int32)
        dq, dko, dvo, low, high = attend(
            meta, q, k, v, before, after, grad_rows, out_rows, norm, slabs, dq
        )
        below = over_seq(high, lambda i: i + 1)
        above = over_seq(low, lambda i: i - 1)
        pending.append((meta, dko, dvo, below, above))

    met = lax.all_to_all(clip_sum, "dp", 0, 0)
    total = met.astype(F32).sum(0).astype(BF16)
    ready = lax.all_to_all(jnp.broadcast_to(total, (n_seq, *piece)), "seq", 0, 0)
    weight_grad = (
        ready.astype(F32)
        .reshape(n_z, n_x, 2, *piece)
        .transpose(0, 3, 2, 1, 4)
        .reshape(width // n_dp, model)
    )

    for item in pending:
        dk, dv = combine(*item, dk, dv)
    return (dq[None], dk[None], dv[None], weight_grad)


def solution(mesh):
    placed = (
        P("dp", "seq", None),
        P("dp", "seq", None),
        P("dp", "seq", None),
        P("dp", "seq", None),
        P("dp", None, "seq"),
        P("dp", "seq", None),
        P("dp", None),
        P("dp", None, None),
    )
    return jax.shard_map(
        body,
        mesh=mesh,
        in_specs=placed,
        out_specs=(P("dp", "seq", None), P("dp", "seq", None), P("dp", "seq", None), P("dp", None)),
        check_vma=False,
    )
```

time: 273 us -> 275 us (level)
  Pallas kernels: 54.7 us -> 90.6 us
  starting transfers between devices: 100 us -> 65.1 us
  matrix products: 29.2 us -> 0 us
  waiting for transfers between devices: 55.3 us -> 72.8 us
  local copies, waits for them, and re-layouts: 14.4 us -> 30.2 us
    ppermute x25 -> x13, starting transfers between devices: 75.3 us -> 38.3 us  [over_seq(): lax.ppermute(value, 'seq', [(i, j) for i, j in pairs if 0 <= j < n_seq])]
    ppermute x25 -> x13, waiting for transfers between devices: 11.2 us -> 47.8 us  [over_seq(): lax.ppermute(value, 'seq', [(i, j) for i, j in pairs if 0 <= j < n_seq])]
    pallas_call x4 -> x5, Pallas kernels: 44.9 us -> 78.5 us  [the longest x3 61.4 us: attend(): pl.pallas_call(functools.partial(attend_kernel, len(slabs)), grid_spec=pl...]
    dot_general x6 -> x0, matrix products: 29.2 us -> none  [dot(): return lax.dot_general(a, b, dims, preferred_element_type=F32)]
    all_to_all x0 -> x3, starting transfers between devices: none -> 22.1 us  [the longest x1 9.57 us: body(): lax.all_to_all(jnp.broadcast_to(total, (n_seq, *piece)), 'seq', 0, 0)]
    ppermute x10 -> x4, starting transfers between devices: 25.1 us -> 4.71 us  [over_dp(): return lax.ppermute(value, 'dp', [(i, target(i)) for i in range(n_dp)])]
    ppermute x10 -> x4, waiting for transfers between devices: 44.1 us -> 25.1 us  [over_dp(): return lax.ppermute(value, 'dp', [(i, target(i)) for i in range(n_dp)])]
    unnamed x35 -> x50, local copies, waits for them, and re-layouts: 1.04 us -> 16.7 us
  transfers between devices with their start and end apart: 35 -> 20, of which waited for: 12 -> 4; matrix products, arithmetic and copies ran while one was open for 20% -> 8% of each run, Pallas kernels for 20% -> 30%
where the time goes in v2:
time: 275 us; the launch traced here: 272 us
  Pallas kernels  90.6 us (33%)
  waiting for transfers between devices  72.8 us (26%)
  starting transfers between devices  65.1 us (24%)
  local copies, waits for them, and re-layouts  30.2 us (11%)
  other arithmetic  12 us (4%)
    pallas_call x3, Pallas kernels, attend(): pl.pallas_call(functools.partial(attend_kernel, len(slabs)), grid_spec=pl...  61.4 us
    ppermute x13, waiting for transfers between devices, over_seq(): lax.ppermute(value, 'seq', [(i, j) for i, j in pairs if 0 <= j < n_seq])  47.8 us
    ppermute x13, starting transfers between devices, over_seq(): lax.ppermute(value, 'seq', [(i, j) for i, j in pairs if 0 <= j < n_seq])  38.3 us
    ppermute x4, waiting for transfers between devices, over_dp(): return lax.ppermute(value, 'dp', [(i, target(i)) for i in range(n_dp)])  25.1 us
    pallas_call x2, Pallas kernels, product(): pl.pallas_call(product_kernel, grid_spec=pltpu.PrefetchScalarGridSpec(num...  17.1 us
    unnamed x50, local copies, waits for them, and re-layouts  16.7 us
    pallas_call x3, Pallas kernels, combine(): pl.pallas_call(combine_kernel, grid_spec=pltpu.PrefetchScalarGridSpec(num...  12.1 us
    all_to_all x1, starting transfers between devices, body(): lax.all_to_all(jnp.broadcast_to(total, (n_seq, *piece)), 'seq', 0, 0)  9.57 us
  transfers between devices with their start and end apart: 20, of which 4 were waited for; matrix products, arithmetic and copies ran while one was open for 8% of the time, Pallas kernels for 30%

profile of v2, /device:TPU:7, one launch (start us, length us, event | category | flops | bytes accessed | tf_op | source)
XLA Modules:
  0.0 271.8 jit_solution(5542156269603313566)
XLA Ops:
  0.7 2.3 copy-done.16
  3.0 1.7 copy-done.21
  4.7 7.9 %shard_map.117 = bf16[2,4,8,96,384]{4,3,2,1,0:T(8,128)(2,1)} custom-call(s32[1]{0:T(128)} %bitcast.9.which, bf16[768,1536]{1,0:T(8,128)(2,1)S(1)} %bitcast.39, bf16[768,3072]{1,0:T(8,128)(2,1)S(1)} %bitcast.31), custom_call_target="tpu_custom_call" | custom-call | flops 7247757312 | bytes 20000000 | tf_op jit(solution)/shard_map/pallas_call | solution.py:186
  14.1 1.6 collective-permute-start.2
  15.8 5.4 %collective-permute-done.16.refs_0_ = bf16[2,4,8,96,384]{4,3,2,1,0:T(8,128)(2,1)} collective-permute-done((bf16[2,4,8,96,384]{4,3,2,1,0:T(8,128)(2,1)}, bf16[2,4,8,96,384]{4,3,2,1,0:T(8,128)(2,1)}, u32[]{:S(2)}, u32[]{:S(2)}) %collective-permute-start.16) | collective-permute-done | bytes 4718624 | tf_op jit(solution)/shard_map/ppermute | solution.py:229
  21.2 2.3 copy-done.17
  23.5 9.2 %shard_map.118 = bf16[2,4,8,96,384]{4,3,2,1,0:T(8,128)(2,1)S(1)} custom-call(s32[1]{0:T(128)} %bitcast.which, bf16[768,1536]{1,0:T(8,128)(2,1)S(1)} %bitcast.40, bf16[768,3072]{1,0:T(8,128)(2,1)S(1)} %bitcast.32, bf16[2,4,8,96,384]{4,3,2,1,0:T(8,128)(2,1)} %collective-permute-done.16.refs_0_), custom_call_target="tpu_custom_call" | custom-call | flops 7247757312 | bytes 20000000 | tf_op jit(solution)/shard_map/pallas_call | solution.py:186
  32.7 2.2 copy-done.2
  34.9 7.7 %all-to-all-start = ((bf16[8,8,96,384]{3,2,1,0:T(8,128)(2,1)}), bf16[8,8,96,384]{3,2,1,0:T(8,128)(2,1)}, u32[]{:S(2)}, u32[]{:S(2)}) async-start(bf16[8,8,96,384]{3,2,1,0:T(8,128)(2,1)} %bitcast.18), calls=%async_computation | async-start | bytes 9437184 | tf_op jit(solution)/shard_map/all_to_all | solution.py:261
  42.6 2.2 fusion
  44.8 1.6 pad_maximum_fusion.1
  46.4 2.8 %collective-permute-start.1 = (bf16[2,384,1536]{2,1,0:T(8,128)(2,1)}, bf16[2,384,1536]{2,1,0:T(8,128)(2,1)}, u32[]{:S(2)}, u32[]{:S(2)}) collective-permute-start(bf16[2,384,1536]{2,1,0:T(8,128)(2,1)} %pad_maximum_fusion.1), channel_id=1, source_target_pairs={{1,0},{2,1},{3,2},{4,3},{5,4},{6,5},{7,6},{8,7},{9,8},{10,9},{11,1... | collective-permute-start | bytes 7077896 | tf_op jit(solution)/shard_map/ppermute | solution.py:229
  49.2 1.6 pad_maximum_fusion
  50.9 6.3 %collective-permute-start = (bf16[2,384,1536]{2,1,0:T(8,128)(2,1)}, bf16[2,384,1536]{2,1,0:T(8,128)(2,1)}, u32[]{:S(2)}, u32[]{:S(2)}) collective-permute-start(bf16[2,384,1536]{2,1,0:T(8,128)(2,1)} %pad_maximum_fusion), channel_id=1, source_target_pairs={{0,1},{1,2},{2,3},{3,4},{4,5},{5,6},{6,7},{7,8},{8,9},{9,10},{10,1... | collective-permute-start | bytes 7077896 | tf_op jit(solution)/shard_map/ppermute | solution.py:229
  57.2 1.3 broadcast_select_fusion.1
  58.6 1.4 collective-permute-start.3
  60.0 1.6 collective-permute-start.7
  61.9 22.6 %collective-permute-done.3.refs_12_ = bf16[384,1536]{1,0:T(8,128)(2,1)} collective-permute-done((bf16[384,1536]{1,0:T(8,128)(2,1)S(1)}, bf16[384,1536]{1,0:T(8,128)(2,1)}, u32[]{:S(2)}, u32[]{:S(2)}) %collective-permute-start.3) | collective-permute-done | bytes 1179680 | tf_op jit(solution)/shard_map/ppermute | solution.py:225
  84.6 2.5 collective-permute-done.7.refs_14_
  87.1 1.4 collective-permute-start.8
  89.3 42.3 %collective-permute-done.1.refs_4_.refs_7_ = bf16[2,384,1536]{2,1,0:T(8,128)(2,1)} collective-permute-done((bf16[2,384,1536]{2,1,0:T(8,128)(2,1)}, bf16[2,384,1536]{2,1,0:T(8,128)(2,1)}, u32[]{:S(2)}, u32[]{:S(2)}) %collective-permute-start.1) | collective-permute-done | bytes 2359328 | tf_op jit(solution)/shard_map/ppermute | solution.py:229
  131.7 1.6 broadcast_1_refs_14__dk_in_dv_in.2.clone.refs_14_
  133.2 16.0 %shard_map.111 = (bf16[768,1536]{1,0:T(8,128)(2,1)}, f32[768,384]{1,0:T(8,128)S(1)}, f32[768,384]{1,0:T(8,128)S(1)}, bf16[2,384,384]{2,1,0:T(8,128)(2,1)}, bf16[2,384,384]{2,1,0:T(8,128)(2,1)}) custom-call(s32[10]{0:T(128)S(1)} %get-tuple-element.52.refs_0_.meta, bf16[768,1536]{1,0:T(8,128)(2,1)S(1)} %bitcast.33, ...), custom_call_target="tpu_custom_call", output_to_operand_aliasing={{0}: (14, {})} | custom-call | flops 12004098048 | bytes 9000000 | tf_op jit(solution)/shard_map/pallas_call | solution.py:103
  150.3 1.0 copy-done.11
  151.3 1.9 collective-permute-start.14
  153.2 2.5 collective-permute-start.15
  156.5 4.0 %reduce_sum.24 = bf16[8,96,384]{2,1,0:T(8,128)(2,1)} reduce(bf16[8,8,96,384]{3,2,1,0:T(8,128)(2,1)} %all-to-all-done, bf16[]{:T(256)} %constant.76.clone.1), dimensions={0}, to_apply=%region_0.1 | reduce | flops 2064384 | bytes 5308418 | tf_op jit(solution)/shard_map/reduce_sum | solution.py:264
  160.4 4.9 %all-to-all-start.1 = ((bf16[8,96,384]{2,1,0:T(8,128)(2,1)}), bf16[8,96,384]{2,1,0:T(8,128)(2,1)}, u32[]{:S(2)}, u32[]{:S(2)}) async-start(bf16[8,96,384]{2,1,0:T(8,128)(2,1)} %reduce_sum.24), calls=%async_computation.1 | async-start | bytes 1179648 | tf_op jit(solution)/shard_map/all_to_all | solution.py:282
  165.3 29.0 %shard_map.112 = (bf16[768,1536]{1,0:T(8,128)(2,1)}, f32[768,768]{1,0:T(8,128)S(1)}, f32[768,768]{1,0:T(8,128)S(1)}, bf16[2,384,768]{2,1,0:T(8,128)(2,1)}, bf16[2,384,768]{2,1,0:T(8,128)(2,1)}) custom-call(s32[13]{0:T(128)S(1)} %pad_add_fusion.2.refs_0_.meta, bf16[768,1536]{1,0:T(8,128)(2,1)S(1)} %bitcast.34, ...), custom_call_target="tpu_custom_call", output_to_operand_aliasing={{0}: (16, {})} | custom-call | flops 24008196096 | bytes 18000000 | tf_op jit(solution)/shard_map/pallas_call | solution.py:103
  194.3 1.4 copy-done.5
  195.7 1.4 copy-done.7
  197.1 13.1 %collective-permute-start.12 = (bf16[2,384,768]{2,1,0:T(8,128)(2,1)}, bf16[2,384,768]{2,1,0:T(8,128)(2,1)S(1)}, u32[]{:S(2)}, u32[]{:S(2)}) collective-permute-start(bf16[2,384,768]{2,1,0:T(8,128)(2,1)} %get-tuple-element.34), channel_id=1, source_target_pairs={{0,1},{1,2},{2,3},{3,4},{4,5},{5,6},{6,7},{7,8},{8,9},{9,10},{10,1... | collective-permute-start | bytes 3538952 | tf_op jit(solution)/shard_map/ppermute | solution.py:229
  210.3 1.9 collective-permute-start.13
  212.2 1.8 reduce_sum.25
  214.0 2.0 broadcast_in_dim.26
  216.0 9.6 %all-to-all-start.2 = ((bf16[16,96,384]{2,1,0:T(8,128)(2,1)}), bf16[16,96,384]{2,1,0:T(8,128)(2,1)}, u32[]{:S(2)}, u32[]{:S(2)}) async-start(bf16[16,96,384]{2,1,0:T(8,128)(2,1)} %broadcast_in_dim.26), calls=%async_computation.2 | async-start | bytes 2359296 | tf_op jit(solution)/shard_map/all_to_all | solution.py:284
  226.4 1.7 copy-done.20
  228.0 16.4 %shard_map.113 = (bf16[768,1536]{1,0:T(8,128)(2,1)}, f32[768,384]{1,0:T(8,128)S(1)}, f32[768,384]{1,0:T(8,128)S(1)}, bf16[2,384,384]{2,1,0:T(8,128)(2,1)S(1)}, bf16[2,384,384]{2,1,0:T(8,128)(2,1)S(1)}) custom-call(s32[10]{0:T(128)S(1)} %get-tuple-element.53.refs_0_.meta, bf16[768,1536]{1,0:T(8,128)(2,1)S(1)} %bitcast.35, ...), custom_call_target="tpu_custom_call", output_to_operand_aliasing={{0}: (14, {})} | custom-call | flops 12004098048 | bytes 9000000 | tf_op jit(solution)/shard_map/pallas_call | solution.py:103
  244.4 4.8 %collective-permute-start.10 = (bf16[2,384,384]{2,1,0:T(8,128)(2,1)S(1)}, bf16[2,384,384]{2,1,0:T(8,128)(2,1)S(1)}, u32[]{:S(2)}, u32[]{:S(2)}) collective-permute-start(bf16[2,384,384]{2,1,0:T(8,128)(2,1)S(1)} %get-tuple-element.30), channel_id=1, source_target_pairs={{0,1},{1,2},{2,3},{3,4},{4,5},{5,6},{6,7},{7,8},{8,9},{9,10},{10,1... | collective-permute-start | bytes 1769480 | tf_op jit(solution)/shard_map/ppermute | solution.py:229
  249.2 2.1 collective-permute-start.11
  251.4 1.6 broadcast_1_refs_14__dk_in_dv_in.2.dk_in
  253.0 1.6 broadcast_1_refs_14__dk_in_dv_in.2.clone.1.dv_in
  254.5 4.3 %shard_map.114 = (bf16[768,1536]{1,0:T(8,128)(2,1)}, bf16[768,1536]{1,0:T(8,128)(2,1)}) custom-call(s32[10]{0:T(128)S(1)} %get-tuple-element.52.refs_0_.meta, f32[768,384]{1,0:T(8,128)S(1)} %copy-done.10, f32[768,384]{1,0:T(8,128)S(1)} %copy-done.12, ...), custom_call_target="tpu_custom_call", output_to_operand_aliasing={{0}: (5, {}), {1}: (6, {})} | custom-call | flops 4000000 | bytes 7680000 | tf_op jit(solution)/shard_map/pallas_call | solution.py:143
  258.9 5.4 %shard_map.115 = (bf16[768,1536]{1,0:T(8,128)(2,1)}, bf16[768,1536]{1,0:T(8,128)(2,1)}) custom-call(s32[13]{0:T(128)S(1)} %pad_add_fusion.2.refs_0_.meta, f32[768,768]{1,0:T(8,128)S(1)} %copy-done.6, f32[768,768]{1,0:T(8,128)S(1)} %copy-done.8, bf16[2,384,768]{2,1,0:T(8,128)(2,1)S(1)} %collective-permute-done.12.below, ...), custom_call_target="tpu_custom_call", output_to_operand_aliasing={{0}: (5, {}), {1}: (6, {})} | custom-call | flops 4000000 | bytes 15360000 | tf_op jit(solution)/shard_map/pallas_call | solution.py:143
  264.3 2.4 shard_map.116
  266.7 1.5 convert_bitcast_fusion
  268.2 1.5 copy.28
  269.8 2.0 reshape.39
  (72 shorter events, 5.5 us)
Async XLA Ops:
  0.6 60.9 %copy-start = (s32[1,32,3]{1,0,2:T(1,128)S(1)}, s32[1,32,3]{1,0,2:T(1,128)}, u32[]{:S(2)}) copy-start(s32[1,32,3]{1,0,2:T(1,128)} %param.15) | copy-start | bytes 1156
  0.7 2.3 copy-start.16
  3.0 1.7 copy-start.21
  4.7 8.6 %copy-start.23 = (bf16[192,3072]{1,0:T(8,128)(2,1)S(1)}, bf16[192,3072]{1,0:T(8,128)(2,1)}, u32[]{:S(2)}) copy-start(bf16[192,3072]{1,0:T(8,128)(2,1)} %param.14) | copy-start | bytes 3538948
  4.7 16.5 %copy-start.22 = (bf16[1,768,1536]{2,1,0:T(8,128)(2,1)S(1)}, bf16[1,768,1536]{2,1,0:T(8,128)(2,1)}, u32[]{:S(2)}) copy-start(bf16[1,768,1536]{2,1,0:T(8,128)(2,1)} %param.11) | copy-start | bytes 7077892
  12.6 8.6 %collective-permute-start.16 = (bf16[2,4,8,96,384]{4,3,2,1,0:T(8,128)(2,1)}, bf16[2,4,8,96,384]{4,3,2,1,0:T(8,128)(2,1)}, u32[]{:S(2)}, u32[]{:S(2)}) collective-permute-start(bf16[2,4,8,96,384]{4,3,2,1,0:T(8,128)(2,1)} %shard_map.117), channel_id=1, source_target_pairs={{0,1},{1,0},{2,3},{3,2},{4,5},{5,4},{6,7},{7,6},{8,9},{9,8},{10,11... | collective-permute-start | bytes 14155784 | tf_op jit(solution)/shard_map/ppermute | solution.py:229
  14.1 43.1 %collective-permute-start.2 = (bf16[192,1536]{1,0:T(8,128)(2,1)}, bf16[192,1536]{1,0:T(8,128)(2,1)}, u32[]{:S(2)}, u32[]{:S(2)}) collective-permute-start(bf16[192,1536]{1,0:T(8,128)(2,1)} %constant_dynamic-slice_fusion), channel_id=1, source_target_pairs={{0,16},{16,0},{32,48},{48,32},{64,80},{80,64},{96,112},{112,96},{1... | collective-permute-start | bytes 1769480 | tf_op jit(solution)/shard_map/ppermute | solution.py:225
  21.2 2.3 copy-start.17
  32.7 2.2 copy-start.2
  34.9 7.7 %copy-start.3 = (bf16[1,768,1536]{2,1,0:T(8,128)(2,1)S(1)}, bf16[1,768,1536]{2,1,0:T(8,128)(2,1)}, u32[]{:S(2)}) copy-start(bf16[1,768,1536]{2,1,0:T(8,128)(2,1)} %param.9) | copy-start | bytes 7077892
  34.9 121.6 %all-to-all-start = ((bf16[8,8,96,384]{3,2,1,0:T(8,128)(2,1)}), bf16[8,8,96,384]{3,2,1,0:T(8,128)(2,1)}, u32[]{:S(2)}, u32[]{:S(2)}) async-start(bf16[8,8,96,384]{3,2,1,0:T(8,128)(2,1)} %bitcast.18), calls=%async_computation | async-start | bytes 9437184 | tf_op jit(solution)/shard_map/all_to_all | solution.py:261
  46.4 85.3 %collective-permute-start.1 = (bf16[2,384,1536]{2,1,0:T(8,128)(2,1)}, bf16[2,384,1536]{2,1,0:T(8,128)(2,1)}, u32[]{:S(2)}, u32[]{:S(2)}) collective-permute-start(bf16[2,384,1536]{2,1,0:T(8,128)(2,1)} %pad_maximum_fusion.1), channel_id=1, source_target_pairs={{1,0},{2,1},{3,2},{4,3},{5,4},{6,5},{7,6},{8,7},{9,8},{10,9},{11,1... | collective-permute-start | bytes 7077896 | tf_op jit(solution)/shard_map/ppermute | solution.py:229
  50.9 80.8 %collective-permute-start = (bf16[2,384,1536]{2,1,0:T(8,128)(2,1)}, bf16[2,384,1536]{2,1,0:T(8,128)(2,1)}, u32[]{:S(2)}, u32[]{:S(2)}) collective-permute-start(bf16[2,384,1536]{2,1,0:T(8,128)(2,1)} %pad_maximum_fusion), channel_id=1, source_target_pairs={{0,1},{1,2},{2,3},{3,4},{4,5},{5,6},{6,7},{7,8},{8,9},{9,10},{10,1... | collective-permute-start | bytes 7077896 | tf_op jit(solution)/shard_map/ppermute | solution.py:229
  58.6 25.9 %collective-permute-start.3 = (bf16[384,1536]{1,0:T(8,128)(2,1)S(1)}, bf16[384,1536]{1,0:T(8,128)(2,1)}, u32[]{:S(2)}, u32[]{:S(2)}) collective-permute-start(bf16[384,1536]{1,0:T(8,128)(2,1)S(1)} %pad_maximum_fusion.2.refs_12_), channel_id=1, source_target_pairs={{0,32},{16,48},{32,64},{48,80},{64,96},{80,112},{96,0},{112,16},{1... | collective-permute-start | bytes 3538952 | tf_op jit(solution)/shard_map/ppermute | solution.py:225
  60.0 24.5 %collective-permute-start.9 = (bf16[384,1536]{1,0:T(8,128)(2,1)S(1)}, bf16[384,1536]{1,0:T(8,128)(2,1)}, u32[]{:S(2)}, u32[]{:S(2)}) collective-permute-start(bf16[384,1536]{1,0:T(8,128)(2,1)S(1)} %pad_maximum_fusion.2.refs_12_), channel_id=1, source_target_pairs={{0,1},{1,0},{2,3},{3,2},{4,5},{5,4},{6,7},{7,6},{8,9},{9,8},{10,11... | collective-permute-start | bytes 3538952 | tf_op jit(solution)/shard_map/ppermute | solution.py:229
  60.0 27.1 %collective-permute-start.7 = (bf16[384,1536]{1,0:T(8,128)(2,1)S(1)}, bf16[384,1536]{1,0:T(8,128)(2,1)}, u32[]{:S(2)}, u32[]{:S(2)}) collective-permute-start(bf16[384,1536]{1,0:T(8,128)(2,1)S(1)} %pad_maximum_fusion.2.refs_12_), channel_id=1, source_target_pairs={{0,96},{16,112},{32,0},{48,16},{64,32},{80,48},{96,64},{112,80},{1... | collective-permute-start | bytes 3538952 | tf_op jit(solution)/shard_map/ppermute | solution.py:225
  61.8 71.4 %copy-start.18 = (bf16[1,768,1536]{2,1,0:T(8,128)(2,1)S(1)}, bf16[1,768,1536]{2,1,0:T(8,128)(2,1)}, u32[]{:S(2)}) copy-start(bf16[1,768,1536]{2,1,0:T(8,128)(2,1)} %param.8) | copy-start | bytes 7077892
  84.5 80.8 %collective-permute-start.6 = (bf16[384,1536]{1,0:T(8,128)(2,1)}, bf16[384,1536]{1,0:T(8,128)(2,1)}, u32[]{:S(2)}, u32[]{:S(2)}) collective-permute-start(bf16[384,1536]{1,0:T(8,128)(2,1)} %collective-permute-done.3.refs_12_), channel_id=1, source_target_pairs={{0,1},{1,0},{2,3},{3,2},{4,5},{5,4},{6,7},{7,6},{8,9},{9,8},{10,11... | collective-permute-start | bytes 3538952 | tf_op jit(solution)/shard_map/ppermute | solution.py:229
  84.5 71.3 %collective-permute-start.4 = (bf16[384,1536]{1,0:T(8,128)(2,1)}, bf16[384,1536]{1,0:T(8,128)(2,1)}, u32[]{:S(2)}, u32[]{:S(2)}) collective-permute-start(bf16[384,1536]{1,0:T(8,128)(2,1)} %collective-permute-done.3.refs_12_), channel_id=1, source_target_pairs={{0,32},{16,48},{32,64},{48,80},{64,96},{80,112},{96,0},{112,16},{1... | collective-permute-start | bytes 3538952 | tf_op jit(solution)/shard_map/ppermute | solution.py:225
  87.1 78.2 %collective-permute-start.8 = (bf16[384,1536]{1,0:T(8,128)(2,1)}, bf16[384,1536]{1,0:T(8,128)(2,1)}, u32[]{:S(2)}, u32[]{:S(2)}) collective-permute-start(bf16[384,1536]{1,0:T(8,128)(2,1)} %collective-permute-done.7.refs_14_), channel_id=1, source_target_pairs={{0,1},{1,0},{2,3},{3,2},{4,5},{5,4},{6,7},{7,6},{8,9},{9,8},{10,11... | collective-permute-start | bytes 3538952 | tf_op jit(solution)/shard_map/ppermute | solution.py:229
  89.3 59.9 %copy-start.13 = (f32[1,12,768]{2,1,0:T(8,128)}, f32[1,12,768]{2,1,0:T(8,128)S(1)}, u32[]{:S(2)}) copy-start(f32[1,12,768]{2,1,0:T(8,128)S(1)} %copy.32) | copy-start | bytes 110596
  149.2 1.0 copy-start.9
  150.3 1.0 copy-start.11
  151.3 97.9 %collective-permute-start.14 = (bf16[2,384,384]{2,1,0:T(8,128)(2,1)}, bf16[2,384,384]{2,1,0:T(8,128)(2,1)}, u32[]{:S(2)}, u32[]{:S(2)}) collective-permute-start(bf16[2,384,384]{2,1,0:T(8,128)(2,1)} %get-tuple-element.38), channel_id=1, source_target_pairs={{0,1},{1,2},{2,3},{3,4},{4,5},{5,6},{6,7},{7,8},{8,9},{9,10},{10,1... | collective-permute-start | bytes 1769480 | tf_op jit(solution)/shard_map/ppermute | solution.py:229
  153.2 12.1 %copy-start.14 = (f32[1,12,768]{2,1,0:T(8,128)S(1)}, f32[1,12,768]{2,1,0:T(8,128)}, u32[]{:S(2)}) copy-start(f32[1,12,768]{2,1,0:T(8,128)} %copy-done.13) | copy-start | bytes 110596
  153.2 12.1 %copy-start.19 = (bf16[1,768,1536]{2,1,0:T(8,128)(2,1)S(1)}, bf16[1,768,1536]{2,1,0:T(8,128)(2,1)}, u32[]{:S(2)}) copy-start(bf16[1,768,1536]{2,1,0:T(8,128)(2,1)} %param.8) | copy-start | bytes 7077892
  153.2 98.2 %collective-permute-start.15 = (bf16[2,384,384]{2,1,0:T(8,128)(2,1)}, bf16[2,384,384]{2,1,0:T(8,128)(2,1)}, u32[]{:S(2)}, u32[]{:S(2)}) collective-permute-start(bf16[2,384,384]{2,1,0:T(8,128)(2,1)} %get-tuple-element.39), channel_id=1, source_target_pairs={{1,0},{2,1},{3,2},{4,3},{5,4},{6,5},{7,6},{8,7},{9,8},{10,9},{11,1... | collective-permute-start | bytes 1769480 | tf_op jit(solution)/shard_map/ppermute | solution.py:229
  155.8 69.7 %collective-permute-start.5 = (bf16[384,1536]{1,0:T(8,128)(2,1)}, bf16[384,1536]{1,0:T(8,128)(2,1)}, u32[]{:S(2)}, u32[]{:S(2)}) collective-permute-start(bf16[384,1536]{1,0:T(8,128)(2,1)} %collective-permute-done.4.refs_12_), channel_id=1, source_target_pairs={{0,1},{1,0},{2,3},{3,2},{4,5},{5,4},{6,7},{7,6},{8,9},{9,8},{10,11... | collective-permute-start | bytes 3538952 | tf_op jit(solution)/shard_map/ppermute | solution.py:229
  160.4 51.8 %all-to-all-start.1 = ((bf16[8,96,384]{2,1,0:T(8,128)(2,1)}), bf16[8,96,384]{2,1,0:T(8,128)(2,1)}, u32[]{:S(2)}, u32[]{:S(2)}) async-start(bf16[8,96,384]{2,1,0:T(8,128)(2,1)} %reduce_sum.24), calls=%async_computation.1 | async-start | bytes 1179648 | tf_op jit(solution)/shard_map/all_to_all | solution.py:282
  194.3 1.4 copy-start.5
  195.7 1.4 copy-start.7
  197.1 28.4 %copy-start.4 = (bf16[1,768,1536]{2,1,0:T(8,128)(2,1)S(1)}, bf16[1,768,1536]{2,1,0:T(8,128)(2,1)}, u32[]{:S(2)}) copy-start(bf16[1,768,1536]{2,1,0:T(8,128)(2,1)} %param.9) | copy-start | bytes 7077892
  197.1 61.7 %collective-permute-start.12 = (bf16[2,384,768]{2,1,0:T(8,128)(2,1)}, bf16[2,384,768]{2,1,0:T(8,128)(2,1)S(1)}, u32[]{:S(2)}, u32[]{:S(2)}) collective-permute-start(bf16[2,384,768]{2,1,0:T(8,128)(2,1)} %get-tuple-element.34), channel_id=1, source_target_pairs={{0,1},{1,2},{2,3},{3,4},{4,5},{5,6},{6,7},{7,8},{8,9},{9,10},{10,1... | collective-permute-start | bytes 3538952 | tf_op jit(solution)/shard_map/ppermute | solution.py:229
  210.3 48.6 %collective-permute-start.13 = (bf16[2,384,768]{2,1,0:T(8,128)(2,1)}, bf16[2,384,768]{2,1,0:T(8,128)(2,1)}, u32[]{:S(2)}, u32[]{:S(2)}) collective-permute-start(bf16[2,384,768]{2,1,0:T(8,128)(2,1)} %get-tuple-element.35), channel_id=1, source_target_pairs={{1,0},{2,1},{3,2},{4,3},{5,4},{6,5},{7,6},{8,7},{9,8},{10,9},{11,1... | collective-permute-start | bytes 3538952 | tf_op jit(solution)/shard_map/ppermute | solution.py:229
  216.0 50.8 %all-to-all-start.2 = ((bf16[16,96,384]{2,1,0:T(8,128)(2,1)}), bf16[16,96,384]{2,1,0:T(8,128)(2,1)}, u32[]{:S(2)}, u32[]{:S(2)}) async-start(bf16[16,96,384]{2,1,0:T(8,128)(2,1)} %broadcast_in_dim.26), calls=%async_computation.2 | async-start | bytes 2359296 | tf_op jit(solution)/shard_map/all_to_all | solution.py:284
  225.6 0.8 copy-start.15
  226.4 1.7 copy-start.20
  244.4 19.9 %collective-permute-start.10 = (bf16[2,384,384]{2,1,0:T(8,128)(2,1)S(1)}, bf16[2,384,384]{2,1,0:T(8,128)(2,1)S(1)}, u32[]{:S(2)}, u32[]{:S(2)}) collective-permute-start(bf16[2,384,384]{2,1,0:T(8,128)(2,1)S(1)} %get-tuple-element.30), channel_id=1, source_target_pairs={{0,1},{1,2},{2,3},{3,4},{4,5},{5,6},{6,7},{7,8},{8,9},{9,10},{10,1... | collective-permute-start | bytes 1769480 | tf_op jit(solution)/shard_map/ppermute | solution.py:229
  249.2 15.0 %collective-permute-start.11 = (bf16[2,384,384]{2,1,0:T(8,128)(2,1)S(1)}, bf16[2,384,384]{2,1,0:T(8,128)(2,1)S(1)}, u32[]{:S(2)}, u32[]{:S(2)}) collective-permute-start(bf16[2,384,384]{2,1,0:T(8,128)(2,1)S(1)} %get-tuple-element.31), channel_id=1, source_target_pairs={{1,0},{2,1},{3,2},{4,3},{5,4},{6,5},{7,6},{8,7},{9,8},{10,9},{11,1... | collective-permute-start | bytes 1769480 | tf_op jit(solution)/shard_map/ppermute | solution.py:229
  251.4 3.1 %copy-start.10 = (f32[768,384]{1,0:T(8,128)S(1)}, f32[768,384]{1,0:T(8,128)}, u32[]{:S(2)}) copy-start(f32[768,384]{1,0:T(8,128)} %copy-done.9) | copy-start | bytes 3538948
  251.4 3.1 %copy-start.12 = (f32[768,384]{1,0:T(8,128)S(1)}, f32[768,384]{1,0:T(8,128)}, u32[]{:S(2)}) copy-start(f32[768,384]{1,0:T(8,128)} %copy-done.11) | copy-start | bytes 3538948
  254.5 4.3 %copy-start.6 = (f32[768,768]{1,0:T(8,128)S(1)}, f32[768,768]{1,0:T(8,128)}, u32[]{:S(2)}) copy-start(f32[768,768]{1,0:T(8,128)} %copy-done.5) | copy-start | bytes 7077892
  254.5 4.3 %copy-start.8 = (f32[768,768]{1,0:T(8,128)S(1)}, f32[768,768]{1,0:T(8,128)}, u32[]{:S(2)}) copy-start(f32[768,768]{1,0:T(8,128)} %copy-done.7) | copy-start | bytes 7077892
  268.2 3.5 %copy-start.1 = (s32[1,32,3]{1,0,2:T(1,128)S(1)}, s32[1,32,3]{1,0,2:T(1,128)}, u32[]{:S(2)}) copy-start(s32[1,32,3]{1,0,2:T(1,128)} %param.15) | copy-start | bytes 1156

commit v3 on v2

--- a/solution.py
+++ b/solution.py
@@ -24,12 +24,13 @@
 
 
 HEADS_AT = 7
+VMEM = 62 << 20
 
 
 def attend_kernel(slabs, *refs):
     meta, q, kb, ko, ka, vb, vo, va, near, away, o, norm = refs[:12]
     weights_in = refs[12 : 12 + 2 * slabs]
-    dq, dko, dvo, low, high, kw, vw, dka, dva, gs = refs[13 + 2 * slabs :]
+    dq, dko, dvo, low, high, kw, vw, dka, dva, gs = refs[-10:]
     step = pl.program_id(0)
     head = meta[HEADS_AT + step]
     per = gs.shape[0]
@@ -98,8 +99,9 @@
     anywhere = pl.BlockSpec(memory_space=pl.ANY)
     wide = jax.ShapeDtypeStruct((2 * TILE, heads * HEAD), F32)
     rims = jax.ShapeDtypeStruct((2, TILE, heads * HEAD), BF16)
-    flops = heads * (6 * 5 * 2 * TILE * TILE * HEAD * 3 + 2 * 2 * TILE * 2 * half * HEAD)
+    flops = heads * (6 * 5 * 2 * TILE * TILE * HEAD + 2 * 2 * TILE * 2 * half * HEAD)
     flat = [w for pair in slabs for w in pair]
+    full = [] if dq_full is None else [dq_full]
     return pl.pallas_call(
         functools.partial(attend_kernel, len(slabs)),
         grid_spec=pltpu.PrefetchScalarGridSpec(
@@ -107,7 +109,7 @@
             grid=(heads,),
             in_specs=[own, rim_k, own, rim_k, rim_v, own, rim_v, near, away, own, whole]
             + [slab] * len(flat)
-            + [anywhere],
+            + [anywhere] * len(full),
             out_specs=[own, local, local, local_rim, local_rim],
             scratch_shapes=[
                 pltpu.VMEM((4, TILE, HEAD), BF16),
@@ -118,90 +120,153 @@
             ],
         ),
         out_shape=[jax.ShapeDtypeStruct(q.shape, BF16), wide, wide, rims, rims],
-        input_output_aliases={12 + len(flat): 0},
-        compiler_params=pltpu.CompilerParams(vmem_limit_bytes=40 << 20),
+        input_output_aliases={12 + len(flat): 0} if full else {},
+        compiler_params=pltpu.CompilerParams(vmem_limit_bytes=VMEM),
         cost_estimate=pl.CostEstimate(
-            flops=flops, bytes_accessed=heads * 3_000_000, transcendentals=heads * 6 * TILE * TILE
-        ),
-    )(meta, q, before, k, after, before, v, after, grads, grads, o, norm, *flat, dq_full)
-
-
-def combine_kernel(meta, dko, dvo, below, above, dk_in, dv_in, dk, dv):
-    dk[:TILE] = ((dko[:TILE] + below[0].astype(F32)) * SCALE).astype(BF16)
-    dk[TILE:] = ((dko[TILE:] + above[0].astype(F32)) * SCALE).astype(BF16)
-    dv[:TILE] = (dvo[:TILE] + below[1].astype(F32)).astype(BF16)
-    dv[TILE:] = (dvo[TILE:] + above[1].astype(F32)).astype(BF16)
-
-
-def combine(meta, dko, dvo, below, above, dk_full, dv_full):
-    width = dko.shape[1]
-    own = pl.BlockSpec((2 * TILE, HEAD), lambda i, m: (0, i))
-    rim = pl.BlockSpec((2, TILE, HEAD), lambda i, m: (0, 0, i))
-    placed = pl.BlockSpec((2 * TILE, HEAD), lambda i, m: (0, m[HEADS_AT + i]))
+            flops=flops, bytes_accessed=heads * 2_000_000, transcendentals=heads * 6 * TILE * TILE
+        ),
+    )(meta, q, before, k, after, before, v, after, grads, grads, o, norm, *flat, *full)
+
+
+def combine_kernel(edges, meta, *refs):
+    dk, dv = refs[-2:]
+    step = pl.program_id(0)
+    for n, (start, stop) in enumerate(edges):
+        dko, dvo, below, above = refs[4 * n : 4 * n + 4]
+
+        @pl.when((step >= start) & (step < stop))
+        def _(dko=dko, dvo=dvo, below=below, above=above):
+            dk[:TILE] = ((dko[:TILE] + below[0].astype(F32)) * SCALE).astype(BF16)
+            dk[TILE:] = ((dko[TILE:] + above[0].astype(F32)) * SCALE).astype(BF16)
+            dv[:TILE] = (dvo[:TILE] + below[1].astype(F32)).astype(BF16)
+            dv[TILE:] = (dvo[TILE:] + above[1].astype(F32)).astype(BF16)
+
+
+def combine(blocks, groups, *filled):
+    edges, in_specs, flat, start = [], [], [], 0
+    wide = min(group[0].shape[1] for group in groups)
+    width = blocks[1] * wide
     anywhere = pl.BlockSpec(memory_space=pl.ANY)
-    full = jax.ShapeDtypeStruct(dk_full.shape, BF16)
-    return pl.pallas_call(
-        combine_kernel,
+    for group in groups:
+        count = group[0].shape[1] // wide
+
+        def at(i, start=start, count=count):
+            return jnp.clip(i - start, 0, count - 1)
+
+        own = pl.BlockSpec((2 * TILE, wide), lambda i, m, at=at: (0, at(i)))
+        rim = pl.BlockSpec((2, TILE, wide), lambda i, m, at=at: (0, 0, at(i)))
+        in_specs += [own, own, rim, rim]
+        flat += group
+        edges.append((start, start + count))
+        start += count
+    placed = pl.BlockSpec((2 * TILE, wide), lambda i, m: (0, m[i]))
+    return pl.pallas_call(
+        functools.partial(combine_kernel, edges),
         grid_spec=pltpu.PrefetchScalarGridSpec(
             num_scalar_prefetch=1,
-            grid=(width // HEAD,),
-            in_specs=[own, own, rim, rim, anywhere, anywhere],
+            grid=(start,),
+            in_specs=in_specs + [anywhere] * len(filled),
             out_specs=[placed, placed],
         ),
-        out_shape=[full, full],
-        input_output_aliases={5: 0, 6: 1},
-        compiler_params=pltpu.CompilerParams(vmem_limit_bytes=16 << 20),
+        out_shape=[jax.ShapeDtypeStruct((2 * TILE, width), BF16)] * 2,
+        input_output_aliases={1 + len(flat) + n: n for n in range(len(filled))},
+        compiler_params=pltpu.CompilerParams(vmem_limit_bytes=VMEM),
         cost_estimate=pl.CostEstimate(
-            flops=4_000_000, bytes_accessed=width * 20_000, transcendentals=0
-        ),
-    )(meta, dko, dvo, below, above, dk_full, dv_full)
+            flops=4_000_000, bytes_accessed=20_000_000, transcendentals=0
+        ),
+    )(blocks[0], *flat, *filled)
 
 
 def product_kernel(which, a, b, *refs):
-    out, turned = refs[-2:]
-
-    @pl.when(pl.program_id(1) == 0)
-    def _():
-        turned[...] = a[...].T
-
-    made = dot(turned[...], b[...], NN)
+    out = refs[-1]
+    added = refs[:-1]
     zs, xs, ds, rows, columns = out.shape
-    for d in range(ds):
-        for z in range(zs):
-            for x in range(xs):
-                at = (d * zs + z) * rows
-                part = made[at : at + rows, x * columns : (x + 1) * columns]
-                if len(refs) == 3:
-                    part = part + refs[0][z, x, d].astype(F32)
-                out[z, x, d] = part.astype(BF16)
-
-
-def product(which, a, b, n_z, n_x, n_dp, *added):
+    turned = a[...].T
+    for half in range(xs // 2):
+        wide = 2 * columns
+        made = dot(turned, b[:, half * wide : (half + 1) * wide], NN)
+        for d in range(ds):
+            for z in range(zs):
+                for n in range(2):
+                    at = (d * zs + z) * rows
+                    part = made[at : at + rows, n * columns : (n + 1) * columns]
+                    if added:
+                        part = part + added[half][z, n, d].astype(F32)
+                    out[z, 2 * half + n, d] = part.astype(BF16)
+
+
+def product(which, a, b, n_z, n_x, n_dp, parts, *added):
     tokens, width = a.shape
-    half = b.shape[1] // 2
-    rows, columns = width // n_dp // n_z, half // n_x
-    shape = (n_z, n_x, n_dp, rows, columns)
-    block = pl.BlockSpec((n_z, 2, 2, rows, columns), lambda i, j, m: (0, j, i, 0, 0))
-    steps = n_x // 2
+    wide = b.shape[1] // 2 // parts
+    rows, columns = width // n_dp // n_z, b.shape[1] // 2 // n_x
+    shape = (n_z, n_x // parts, n_dp, rows, columns)
+    block = pl.BlockSpec((n_z, n_x // parts, 2, rows, columns), lambda i, m: (0, 0, i, 0, 0))
+    piece = pl.BlockSpec((n_z, 2, 2, rows, columns), lambda i, m: (0, 0, i, 0, 0))
     return pl.pallas_call(
         product_kernel,
         grid_spec=pltpu.PrefetchScalarGridSpec(
             num_scalar_prefetch=1,
-            grid=(n_dp // 2, steps),
+            grid=(n_dp // 2,),
             in_specs=[
-                pl.BlockSpec((tokens, 2 * n_z * rows), lambda i, j, m: (0, i)),
-                pl.BlockSpec((tokens, 2 * columns), lambda i, j, m: (0, m[0] * steps + j)),
+                pl.BlockSpec((tokens, 2 * n_z * rows), lambda i, m: (0, i)),
+                pl.BlockSpec((tokens, wide), lambda i, m: (0, m[0])),
             ]
-            + [block] * len(added),
+            + [piece] * len(added),
             out_specs=block,
-            scratch_shapes=[pltpu.VMEM((2 * n_z * rows, tokens), BF16)],
         ),
         out_shape=jax.ShapeDtypeStruct(shape, BF16),
-        compiler_params=pltpu.CompilerParams(vmem_limit_bytes=40 << 20),
+        compiler_params=pltpu.CompilerParams(vmem_limit_bytes=VMEM),
         cost_estimate=pl.CostEstimate(
-            flops=2 * 2 * tokens * width * half, bytes_accessed=20_000_000, transcendentals=0
+            flops=tokens * width * wide // 16, bytes_accessed=400_000, transcendentals=0
         ),
     )(which, a, b, *added)
+
+
+def lay_kernel(pieces, out):
+    n_x = pieces.shape[0] // 2
+    columns = pieces.shape[2]
+    for x in range(n_x):
+        for c in range(2):
+            at = (c * n_x + x) * columns
+            out[:, at : at + columns] = pieces[2 * x + c].astype(F32)
+
+
+def lay_out(pieces, n_z):
+    count, rows, columns = pieces.shape
+    wide = count // n_z * columns
+    return pl.pallas_call(
+        lay_kernel,
+        grid=(n_z,),
+        in_specs=[pl.BlockSpec((count // n_z, rows, columns), lambda i: (i, 0, 0))],
+        out_specs=pl.BlockSpec((rows, wide), lambda i: (i, 0)),
+        out_shape=jax.ShapeDtypeStruct((n_z * rows, wide), F32),
+        compiler_params=pltpu.CompilerParams(vmem_limit_bytes=VMEM),
+    )(pieces)
+
+
+def pack_kernel(kf, kl, vf, vl, last, first):
+    last[0] = kl[...]
+    last[1] = vl[...]
+    first[0] = kf[...]
+    first[1] = vf[...]
+
+
+def pack(k, v):
+    steps = 3
+    columns = k.shape[1] // steps
+    end = k.shape[0] // TILE - 1
+    head = pl.BlockSpec((TILE, columns), lambda i: (0, i))
+    tail = pl.BlockSpec((TILE, columns), lambda i: (end, i))
+    rim = pl.BlockSpec((2, TILE, columns), lambda i: (0, 0, i))
+    shape = jax.ShapeDtypeStruct((2, TILE, k.shape[1]), BF16)
+    return pl.pallas_call(
+        pack_kernel,
+        grid=(steps,),
+        in_specs=[head, tail, head, tail],
+        out_specs=[rim, rim],
+        out_shape=[shape, shape],
+        compiler_params=pltpu.CompilerParams(vmem_limit_bytes=VMEM),
+    )(k, k, v, v)
 
 
 def body(query, key_states, value_states, attn_out, log_norm, out_grad, out_weight, tile_lists):
@@ -239,58 +304,70 @@
 
     half = model // 2
     mine = lax.dynamic_slice_in_dim(out_weight, core * half, half, 1)
+    last, first = pack(k, v)
+    mine, last, first, left = lax.optimization_barrier((mine, last, first, out_rows))
+    before = over_seq(last, lambda i: i + 1)
+    after = over_seq(first, lambda i: i - 1)
     other = over_dp(mine, lambda i: i ^ 1)
-    before = over_seq(jnp.stack([k[tokens - TILE :], v[tokens - TILE :]]), lambda i: i + 1)
-    after = over_seq(jnp.stack([k[:TILE], v[:TILE]]), lambda i: i - 1)
+
+    first_tile = seq * 2 - 1
+    slots = (lax.dynamic_slice_in_dim(tile_lists[0], seq * 2, 2, 0) - first_tile).reshape(-1)
+
+    send = 2 * (1 - core)
+    sent0 = product(send[None], left, grad_rows, n_z, n_x, n_dp, 2)
+    left, other = lax.optimization_barrier((left, other))
+    sent1 = product((send + 1)[None], left, grad_rows, n_z, n_x, n_dp, 2)
     low_first = dp % 2 == 0
     pair0 = jnp.concatenate(
         [jnp.where(low_first, mine, other), jnp.where(low_first, other, mine)], axis=0
     )
     from_up = up(pair0)
     from_down = down(pair0)
-    far = up(from_up)
-    order = [[(pair0, y)], [(from_up, y + n_y - 1), (from_down, y + 1)], [(far, y + 2)]]
-
-    first_tile = seq * 2 - 1
-    slots = (lax.dynamic_slice_in_dim(tile_lists[0], seq * 2, 2, 0) - first_tile).reshape(-1)
-
-    sent = product((1 - core)[None], out_rows, grad_rows, n_z, n_x, n_dp)
-    chip_sum = product(core[None], out_rows, grad_rows, n_z, n_x, n_dp, swap(sent))
+    across0 = swap(pair0)
+    met0, met1, before, after = lax.optimization_barrier((swap(sent0), swap(sent1), before, after))
+    chip_sum = product(core[None], out_rows, grad_rows, n_z, n_x, n_dp, 1, met0, met1)
+    chip_sum, across0 = lax.optimization_barrier((chip_sum, across0))
     chips = [[2 * i + c for i in range(n_seq // 2)] for c in range(2)]
     piece = chip_sum.shape[-2:]
     spread = lax.all_to_all(
         chip_sum.reshape(n_seq // 2, n_dp, *piece), "seq", 0, 0, axis_index_groups=chips
     )
-    clip_sum = spread.astype(F32).sum(0).astype(BF16)
 
     per = width // n_y // HEAD
-    dq = jnp.zeros((tokens, width), BF16)
-    dk = jnp.zeros((tokens, width), BF16)
-    dv = jnp.zeros((tokens, width), BF16)
     pending = []
-    for group in order:
-        slabs = [(slab, swap(slab)) for slab, _ in group]
-        heads = [(at % n_y) * per + jnp.arange(per, dtype=jnp.int32) for _, at in group]
-        meta = jnp.concatenate([slots, core[None], *heads]).astype(jnp.int32)
+
+    def attend_group(ats, slabs, dq):
+        heads = [(at % n_y) * per + jnp.arange(per, dtype=jnp.int32) for at in ats]
+        heads = jnp.concatenate(heads).astype(jnp.int32)
+        meta = jnp.concatenate([slots, core[None], heads]).astype(jnp.int32)
         dq, dko, dvo, low, high = attend(
             meta, q, k, v, before, after, grad_rows, out_rows, norm, slabs, dq
         )
         below = over_seq(high, lambda i: i + 1)
         above = over_seq(low, lambda i: i - 1)
-        pending.append((meta, dko, dvo, below, above))
+        pending.append([dko, dvo, below, above])
+        return dq
+
+    dq = attend_group([y], [(pair0, across0)], None)
+    from_up, from_down, dq = lax.optimization_barrier((from_up, from_down, dq))
+    far = up(from_up)
+    dq = attend_group(
+        [y + n_y - 1, y + 1], [(from_up, swap(from_up)), (from_down, swap(from_down))], dq
+    )
+    spread, far, dq = lax.optimization_barrier((spread, far, dq))
+    clip_sum = spread.astype(F32).sum(0).astype(BF16)
+    dq = attend_group([y + 2], [(far, swap(far))], dq)
 
     met = lax.all_to_all(clip_sum, "dp", 0, 0)
+    met, dq, *rims = lax.optimization_barrier((met, dq, *pending[0][2:], *pending[1][2:]))
+    pending[0][2:], pending[1][2:] = rims[:2], rims[2:]
     total = met.astype(F32).sum(0).astype(BF16)
     ready = lax.all_to_all(jnp.broadcast_to(total, (n_seq, *piece)), "seq", 0, 0)
-    weight_grad = (
-        ready.astype(F32)
-        .reshape(n_z, n_x, 2, *piece)
-        .transpose(0, 3, 2, 1, 4)
-        .reshape(width // n_dp, model)
-    )
-
-    for item in pending:
-        dk, dv = combine(*item, dk, dv)
+    weight_grad = lay_out(ready, n_z)
+
+    blocks = jnp.stack([y, (y + n_y - 1) % n_y, (y + 1) % n_y, (y + 2) % n_y]).astype(jnp.int32)
+    filled = combine((blocks[:3], n_y), pending[:2])
+    dk, dv = combine((blocks[3:], n_y), pending[2:], *filled)
     return (dq[None], dk[None], dv[None], weight_grad)
 
 

time: 275 us -> 212 us (0.77)
  local copies, waits for them, and re-layouts: 30.2 us -> 3.45 us
  waiting for transfers between devices: 72.8 us -> 49.1 us
  starting transfers between devices: 65.1 us -> 49.8 us
  Pallas kernels: 90.6 us -> 101 us
  other arithmetic: 12 us -> 6.17 us
    ppermute x4, waiting for transfers between devices: 25.1 us -> 9.19 us  [over_dp(): return lax.ppermute(value, 'dp', [(i, target(i)) for i in range(n_dp)])]
    unnamed x50 -> x18, local copies, waits for them, and re-layouts: 16.7 us -> 2 us
    ppermute x13 -> x14, waiting for transfers between devices: 47.8 us -> 37.1 us  [over_seq(): lax.ppermute(value, 'seq', [(i, j) for i, j in pairs if 0 <= j < n_seq])]
    ppermute x13 -> x14, starting transfers between devices: 38.3 us -> 29.3 us  [over_seq(): lax.ppermute(value, 'seq', [(i, j) for i, j in pairs if 0 <= j < n_seq])]
    pallas_call x3 -> x4, Pallas kernels: 12.1 us -> 19.1 us  [the longest x2 11.2 us: combine(): pl.pallas_call(functools.partial(combine_kernel, edges), grid_spec=pltpu....]
    another operation x3 -> x0, local copies, waits for them, and re-layouts: 4.68 us -> none
    reshape x2 -> x0, local copies, waits for them, and re-layouts: 3.51 us -> none  [body(): weight_grad = ready.astype(F32).reshape(n_z, n_x, 2, *piece).transpose(0,...]
    all_to_all x1, starting transfers between devices: 7.66 us -> 4.69 us  [body(): lax.all_to_all(chip_sum.reshape(n_seq // 2, n_dp, *piece), 'seq', 0, 0, a...]
  transfers between devices with their start and end apart: 20 -> 21, of which waited for: 4 -> 9; matrix products, arithmetic and copies ran while one was open for 8% -> 3% of each run, Pallas kernels for 30% -> 44%
where the time goes in v3:
time: 212 us; the launch traced here: 211 us
  Pallas kernels  101 us (48%)
  starting transfers between devices  49.8 us (23%)
  waiting for transfers between devices  49.1 us (23%)
  other arithmetic  6.17 us (3%)
  local copies, waits for them, and re-layouts  3.45 us (2%)
    pallas_call x3, Pallas kernels, attend(): pl.pallas_call(functools.partial(attend_kernel, len(slabs)), grid_spec=pl...  62.4 us
    ppermute x14, waiting for transfers between devices, over_seq(): lax.ppermute(value, 'seq', [(i, j) for i, j in pairs if 0 <= j < n_seq])  37.1 us
    ppermute x14, starting transfers between devices, over_seq(): lax.ppermute(value, 'seq', [(i, j) for i, j in pairs if 0 <= j < n_seq])  29.3 us
    pallas_call x3, Pallas kernels, product(): pl.pallas_call(product_kernel, grid_spec=pltpu.PrefetchScalarGridSpec(num...  20 us
    pallas_call x2, Pallas kernels, combine(): pl.pallas_call(functools.partial(combine_kernel, edges), grid_spec=pltpu....  11.2 us
    ppermute x4, waiting for transfers between devices, over_dp(): return lax.ppermute(value, 'dp', [(i, target(i)) for i in range(n_dp)])  9.19 us
    all_to_all x1, starting transfers between devices, body(): lax.all_to_all(jnp.broadcast_to(total, (n_seq, *piece)), 'seq', 0, 0)  7.51 us
    pallas_call x1, Pallas kernels, pack(): pl.pallas_call(pack_kernel, grid=(steps,), in_specs=[head, tail, head, ta...  5.34 us
  transfers between devices with their start and end apart: 21, of which 9 were waited for; matrix products, arithmetic and copies ran while one was open for 3% of the time, Pallas kernels for 44%

profile of v3, /device:TPU:7, one launch (start us, length us, event | category | flops | bytes accessed | tf_op | source)
XLA Modules:
  0.0 210.9 jit_solution(16340117248723103675)
XLA Ops:
  0.7 1.2 copy-done
  2.0 5.3 %shard_map.111 = (bf16[2,384,1536]{2,1,0:T(8,128)(2,1)}, bf16[2,384,1536]{2,1,0:T(8,128)(2,1)}) custom-call(bf16[768,1536]{1,0:T(8,128)(2,1)} %bitcast.34, bf16[768,1536]{1,0:T(8,128)(2,1)} %bitcast.35, bf16[768,1536]{1,0:T(8,128)(2,1)} %bitcast.39, bf16[768,1536]{1,0:T(8,128)(2,1)} %bitcast.40), custom_call_target="tpu_custom_call" | custom-call | tf_op jit(solution)/shard_map/pallas_call | solution.py:262
  7.3 1.6 collective-permute-start.1
  8.9 5.6 %shard_map.112 = bf16[2,2,8,96,384]{4,3,2,1,0:T(8,128)(2,1)} custom-call(s32[1]{0:T(128)} %bitcast.3.which, bf16[768,1536]{1,0:T(8,128)(2,1)} %bitcast.28, bf16[768,3072]{1,0:T(8,128)(2,1)} %bitcast.19), custom_call_target="tpu_custom_call" | custom-call | flops 56623104 | bytes 400000 | tf_op jit(solution)/shard_map/pallas_call | solution.py:205
  14.6 1.0 collective-permute-start
  15.5 5.0 %collective-permute-start.3 = (bf16[2,384,1536]{2,1,0:T(8,128)(2,1)}, bf16[2,384,1536]{2,1,0:T(8,128)(2,1)}, u32[]{:S(2)}, u32[]{:S(2)}) collective-permute-start(bf16[2,384,1536]{2,1,0:T(8,128)(2,1)} %get-tuple-element.54), channel_id=1, source_target_pairs={{0,1},{1,2},{2,3},{3,4},{4,5},{5,6},{6,7},{7,8},{8,9},{9,10},{10,1... | collective-permute-start | bytes 7077896 | tf_op jit(solution)/shard_map/ppermute | solution.py:294
  20.5 1.9 collective-permute-start.4
  22.5 5.7 %shard_map.113 = bf16[2,2,8,96,384]{4,3,2,1,0:T(8,128)(2,1)} custom-call(s32[1]{0:T(128)} %bitcast.6.which, bf16[768,1536]{1,0:T(8,128)(2,1)} %bitcast.29, bf16[768,3072]{1,0:T(8,128)(2,1)} %bitcast.20), custom_call_target="tpu_custom_call" | custom-call | flops 56623104 | bytes 400000 | tf_op jit(solution)/shard_map/pallas_call | solution.py:205
  28.1 0.7 collective-permute-start.2
  28.8 0.1 broadcast_select_fusion.1
  28.9 0.1 pad_maximum_fusion.refs_12_
  29.0 0.1 collective-permute-start.5
  29.1 17.5 %collective-permute-done.3.refs_2_.refs_5_ = bf16[2,384,1536]{2,1,0:T(8,128)(2,1)} collective-permute-done((bf16[2,384,1536]{2,1,0:T(8,128)(2,1)}, bf16[2,384,1536]{2,1,0:T(8,128)(2,1)}, u32[]{:S(2)}, u32[]{:S(2)}) %collective-permute-start.3) | collective-permute-done | bytes 2359328 | tf_op jit(solution)/shard_map/ppermute | solution.py:294
  46.6 8.0 %collective-permute-done.4.refs_4_.refs_7_ = bf16[2,384,1536]{2,1,0:T(8,128)(2,1)} collective-permute-done((bf16[2,384,1536]{2,1,0:T(8,128)(2,1)}, bf16[2,384,1536]{2,1,0:T(8,128)(2,1)}, u32[]{:S(2)}, u32[]{:S(2)}) %collective-permute-start.4) | collective-permute-done | bytes 2359328 | tf_op jit(solution)/shard_map/ppermute | solution.py:294
  54.6 8.7 %shard_map.114 = bf16[2,4,8,96,384]{4,3,2,1,0:T(8,128)(2,1)} custom-call(s32[1]{0:T(128)} %bitcast.which, bf16[768,1536]{1,0:T(8,128)(2,1)} %bitcast.30, bf16[768,3072]{1,0:T(8,128)(2,1)} %bitcast.21, bf16[2,2,8,96,384]{4,3,2,1,0:T(8,128)(2,1)} %collective-permute-done.refs_0_, bf16[2,2,8,96,384]{4,3,2,1,0:T(8,128)(2,1)} %collective-permute-done.2.refs_1_), custom_call_target="tpu_custom_call" | custom-call | flops 113246208 | bytes 400000 | tf_op jit(solution)/shard_map/pallas_call | solution.py:205
  63.3 4.7 %all-to-all-start = ((bf16[8,8,96,384]{3,2,1,0:T(8,128)(2,1)}), bf16[8,8,96,384]{3,2,1,0:T(8,128)(2,1)}, u32[]{:S(2)}, u32[]{:S(2)}) async-start(bf16[8,8,96,384]{3,2,1,0:T(8,128)(2,1)} %bitcast.44), calls=%async_computation | async-start | bytes 9437184 | tf_op jit(solution)/shard_map/all_to_all | solution.py:332
  68.0 2.8 %collective-permute-start.7 = (bf16[384,1536]{1,0:T(8,128)(2,1)S(1)}, bf16[384,1536]{1,0:T(8,128)(2,1)}, u32[]{:S(2)}, u32[]{:S(2)}) collective-permute-start(bf16[384,1536]{1,0:T(8,128)(2,1)S(1)} %pad_maximum_fusion.refs_12_), channel_id=1, source_target_pairs={{0,96},{16,112},{32,0},{48,16},{64,32},{80,48},{96,64},{112,80},{1... | collective-permute-start | bytes 3538952 | tf_op jit(solution)/shard_map/ppermute | solution.py:290
  70.9 0.1 copy.19
  71.0 0.1 sub.28
  71.1 0.6 copy.21
  71.7 0.7 pad_add_fusion.3
  72.4 16.7 %shard_map.115 = (bf16[768,1536]{1,0:T(8,128)(2,1)}, f32[768,384]{1,0:T(8,128)}, f32[768,384]{1,0:T(8,128)}, bf16[2,384,384]{2,1,0:T(8,128)(2,1)}, bf16[2,384,384]{2,1,0:T(8,128)(2,1)}) custom-call(s32[10]{0:T(128)} %get-tuple-element.97.refs_0_, bf16[768,1536]{1,0:T(8,128)(2,1)} %bitcast.45, bf16[2,384,1536]{2,1,0:T(8,128)(2,1)} %collective-permute-done.3.refs_2_.refs_5_, ...), custom_call_target="tpu_custom_call" | custom-call | flops 5209325568 | bytes 6000000 | tf_op jit(solution)/shard_map/pallas_call | solution.py:105
  89.1 5.4 %collective-permute-done.7.refs_14_ = bf16[384,1536]{1,0:T(8,128)(2,1)} collective-permute-done((bf16[384,1536]{1,0:T(8,128)(2,1)S(1)}, bf16[384,1536]{1,0:T(8,128)(2,1)}, u32[]{:S(2)}, u32[]{:S(2)}) %collective-permute-start.7) | collective-permute-done | bytes 1179680 | tf_op jit(solution)/shard_map/ppermute | solution.py:290
  94.5 3.8 %collective-permute-done.6.refs_12_ = bf16[384,1536]{1,0:T(8,128)(2,1)} collective-permute-done((bf16[384,1536]{1,0:T(8,128)(2,1)S(1)}, bf16[384,1536]{1,0:T(8,128)(2,1)}, u32[]{:S(2)}, u32[]{:S(2)}) %collective-permute-start.6) | collective-permute-done | bytes 1179680 | tf_op jit(solution)/shard_map/ppermute | solution.py:290
  98.3 0.5 collective-permute-start.9
  98.8 0.6 pad_add_fusion.2.refs_0_
  99.4 2.1 collective-permute-done.10.refs_15_
  101.5 1.7 collective-permute-done.9.refs_13_
  103.2 28.9 %shard_map.116 = (bf16[768,1536]{1,0:T(8,128)(2,1)}, f32[768,768]{1,0:T(8,128)}, f32[768,768]{1,0:T(8,128)}, bf16[2,384,768]{2,1,0:T(8,128)(2,1)}, bf16[2,384,768]{2,1,0:T(8,128)(2,1)}) custom-call(s32[13]{0:T(128)} %pad_add_fusion.2.refs_0_, bf16[768,1536]{1,0:T(8,128)(2,1)} %bitcast.46, ...), custom_call_target="tpu_custom_call", output_to_operand_aliasing={{0}: (16, {})} | custom-call | flops 10418651136 | bytes 12000000 | tf_op jit(solution)/shard_map/pallas_call | solution.py:105
  132.1 2.8 %all-to-all-done = bf16[8,8,96,384]{3,2,1,0:T(8,128)(2,1)} async-done(((bf16[8,8,96,384]{3,2,1,0:T(8,128)(2,1)}), bf16[8,8,96,384]{3,2,1,0:T(8,128)(2,1)}, u32[]{:S(2)}, u32[]{:S(2)}) %all-to-all-start) | async-done | bytes 4718624 | tf_op jit(solution)/shard_map/all_to_all | solution.py:332
  134.9 2.3 %collective-permute-start.14 = (bf16[2,384,768]{2,1,0:T(8,128)(2,1)}, bf16[2,384,768]{2,1,0:T(8,128)(2,1)}, u32[]{:S(2)}, u32[]{:S(2)}) collective-permute-start(bf16[2,384,768]{2,1,0:T(8,128)(2,1)} %get-tuple-element.74), channel_id=1, source_target_pairs={{0,1},{1,2},{2,3},{3,4},{4,5},{5,6},{6,7},{7,8},{8,9},{9,10},{10,1... | collective-permute-start | bytes 3538952 | tf_op jit(solution)/shard_map/ppermute | solution.py:294
  137.2 2.1 collective-permute-start.15
  139.3 7.1 %collective-permute-start.12 = (bf16[2,384,384]{2,1,0:T(8,128)(2,1)}, bf16[2,384,384]{2,1,0:T(8,128)(2,1)S(1)}, u32[]{:S(2)}, u32[]{:S(2)}) collective-permute-start(bf16[2,384,384]{2,1,0:T(8,128)(2,1)} %get-tuple-element.72), channel_id=1, source_target_pairs={{0,1},{1,2},{2,3},{3,4},{4,5},{5,6},{6,7},{7,8},{8,9},{9,10},{10,1... | collective-permute-start | bytes 1769480 | tf_op jit(solution)/shard_map/ppermute | solution.py:294
  146.4 1.9 collective-permute-start.13
  148.3 4.1 %reduce_sum.24 = bf16[8,96,384]{2,1,0:T(8,128)(2,1)} reduce(bf16[8,8,96,384]{3,2,1,0:T(8,128)(2,1)} %all-to-all-done, bf16[]{:T(256)} %constant.81.clone.1), dimensions={0}, to_apply=%region_0.1 | reduce | flops 2064384 | bytes 5308418 | tf_op jit(solution)/shard_map/reduce_sum | solution.py:358
  152.4 3.8 %all-to-all-start.1 = ((bf16[8,96,384]{2,1,0:T(8,128)(2,1)}), bf16[8,96,384]{2,1,0:T(8,128)(2,1)S(1)}, u32[]{:S(2)}, u32[]{:S(2)}) async-start(bf16[8,96,384]{2,1,0:T(8,128)(2,1)} %reduce_sum.24), calls=%async_computation.1 | async-start | bytes 1179648 | tf_op jit(solution)/shard_map/all_to_all | solution.py:361
  156.2 16.8 %shard_map.117 = (bf16[768,1536]{1,0:T(8,128)(2,1)}, f32[768,384]{1,0:T(8,128)}, f32[768,384]{1,0:T(8,128)}, bf16[2,384,384]{2,1,0:T(8,128)(2,1)}, bf16[2,384,384]{2,1,0:T(8,128)(2,1)}) custom-call(s32[10]{0:T(128)} %get-tuple-element.96.refs_0_, bf16[768,1536]{1,0:T(8,128)(2,1)} %bitcast.47, ...), custom_call_target="tpu_custom_call", output_to_operand_aliasing={{0}: (14, {})} | custom-call | flops 5209325568 | bytes 6000000 | tf_op jit(solution)/shard_map/pallas_call | solution.py:105
  173.0 0.1 reduce_sum.25
  173.1 1.2 broadcast_in_dim.30
  174.4 7.5 %all-to-all-start.2 = ((bf16[16,96,384]{2,1,0:T(8,128)(2,1)}), bf16[16,96,384]{2,1,0:T(8,128)(2,1)}, u32[]{:S(2)}, u32[]{:S(2)}) async-start(bf16[16,96,384]{2,1,0:T(8,128)(2,1)} %broadcast_in_dim.30), calls=%async_computation.2 | async-start | bytes 2359296 | tf_op jit(solution)/shard_map/all_to_all | solution.py:365
  181.9 4.8 %collective-permute-start.16 = (bf16[2,384,384]{2,1,0:T(8,128)(2,1)}, bf16[2,384,384]{2,1,0:T(8,128)(2,1)S(1)}, u32[]{:S(2)}, u32[]{:S(2)}) collective-permute-start(bf16[2,384,384]{2,1,0:T(8,128)(2,1)} %get-tuple-element.79), channel_id=1, source_target_pairs={{0,1},{1,2},{2,3},{3,4},{4,5},{5,6},{6,7},{7,8},{8,9},{9,10},{10,1... | collective-permute-start | bytes 1769480 | tf_op jit(solution)/shard_map/ppermute | solution.py:294
  186.8 1.9 collective-permute-start.17
  188.7 0.6 pad_add_fusion.4.meta
  189.3 8.0 %shard_map.118 = (bf16[768,1536]{1,0:T(8,128)(2,1)}, bf16[768,1536]{1,0:T(8,128)(2,1)}) custom-call(s32[3]{0:T(128)} %pad_add_fusion.4.meta, f32[768,384]{1,0:T(8,128)} %get-tuple-element.81.refs_0_, f32[768,384]{1,0:T(8,128)} %get-tuple-element.82.refs_1_, bf16[2,384,384]{2,1,0:T(8,128)(2,1)} %copy-done.4, bf16[2,384,384]{2,1,0:T(8,128)(2,1)} %copy-done.5, ...), custom_call_target="tpu_custom_call" | custom-call | flops 4000000 | bytes 20000000 | tf_op jit(solution)/shard_map/pallas_call | solution.py:163
  197.3 4.4 %collective-permute-done.16.refs_2_ = bf16[2,384,384]{2,1,0:T(8,128)(2,1)S(1)} collective-permute-done((bf16[2,384,384]{2,1,0:T(8,128)(2,1)}, bf16[2,384,384]{2,1,0:T(8,128)(2,1)S(1)}, u32[]{:S(2)}, u32[]{:S(2)}) %collective-permute-start.16) | collective-permute-done | bytes 589856 | tf_op jit(solution)/shard_map/ppermute | solution.py:294
  201.7 3.5 %collective-permute-done.17.refs_3_ = bf16[2,384,384]{2,1,0:T(8,128)(2,1)} collective-permute-done((bf16[2,384,384]{2,1,0:T(8,128)(2,1)}, bf16[2,384,384]{2,1,0:T(8,128)(2,1)}, u32[]{:S(2)}, u32[]{:S(2)}) %collective-permute-start.17) | collective-permute-done | bytes 589856 | tf_op jit(solution)/shard_map/ppermute | solution.py:294
  205.2 3.2 %shard_map.119 = (bf16[768,1536]{1,0:T(8,128)(2,1)}, bf16[768,1536]{1,0:T(8,128)(2,1)}) custom-call(s32[1]{0:T(128)} %bitcast.10.meta, f32[768,384]{1,0:T(8,128)} %get-tuple-element.77.refs_0_, f32[768,384]{1,0:T(8,128)} %get-tuple-element.78.refs_1_, bf16[2,384,384]{2,1,0:T(8,128)(2,1)} %copy-done.3, ...), custom_call_target="tpu_custom_call", output_to_operand_aliasing={{0}: (5, {}), {1}: (6, {})} | custom-call | flops 4000000 | bytes 20000000 | tf_op jit(solution)/shard_map/pallas_call | solution.py:163
  208.4 2.5 %shard_map.120 = f32[192,3072]{1,0:T(8,128)} custom-call(bf16[16,96,384]{2,1,0:T(8,128)(2,1)} %all-to-all-done.2.pieces), custom_call_target="tpu_custom_call" | custom-call | tf_op jit(solution)/shard_map/pallas_call | solution.py:237
  (36 shorter events, 0.2 us)
Async XLA Ops:
  0.6 1.3 copy-start
  7.3 15.2 %collective-permute-start.1 = (bf16[192,1536]{1,0:T(8,128)(2,1)S(1)}, bf16[192,1536]{1,0:T(8,128)(2,1)S(1)}, u32[]{:S(2)}, u32[]{:S(2)}) collective-permute-start(bf16[192,1536]{1,0:T(8,128)(2,1)S(1)} %constant_dynamic-slice_fusion.1), channel_id=1, source_target_pairs={{0,16},{16,0},{32,48},{48,32},{64,80},{80,64},{96,112},{112,96},{1... | collective-permute-start | bytes 1769480 | tf_op jit(solution)/shard_map/ppermute | solution.py:290
  14.6 14.6 %collective-permute-start = (bf16[2,2,8,96,384]{4,3,2,1,0:T(8,128)(2,1)}, bf16[2,2,8,96,384]{4,3,2,1,0:T(8,128)(2,1)}, u32[]{:S(2)}, u32[]{:S(2)}) collective-permute-start(bf16[2,2,8,96,384]{4,3,2,1,0:T(8,128)(2,1)} %shard_map.112), channel_id=1, source_target_pairs={{0,1},{1,0},{2,3},{3,2},{4,5},{5,4},{6,7},{7,6},{8,9},{9,8},{10,11... | collective-permute-start | bytes 7077896 | tf_op jit(solution)/shard_map/ppermute | solution.py:294
  15.5 31.1 %collective-permute-start.3 = (bf16[2,384,1536]{2,1,0:T(8,128)(2,1)}, bf16[2,384,1536]{2,1,0:T(8,128)(2,1)}, u32[]{:S(2)}, u32[]{:S(2)}) collective-permute-start(bf16[2,384,1536]{2,1,0:T(8,128)(2,1)} %get-tuple-element.54), channel_id=1, source_target_pairs={{0,1},{1,2},{2,3},{3,4},{4,5},{5,6},{6,7},{7,8},{8,9},{9,10},{10,1... | collective-permute-start | bytes 7077896 | tf_op jit(solution)/shard_map/ppermute | solution.py:294
  20.5 34.1 %collective-permute-start.4 = (bf16[2,384,1536]{2,1,0:T(8,128)(2,1)}, bf16[2,384,1536]{2,1,0:T(8,128)(2,1)}, u32[]{:S(2)}, u32[]{:S(2)}) collective-permute-start(bf16[2,384,1536]{2,1,0:T(8,128)(2,1)} %get-tuple-element.55), channel_id=1, source_target_pairs={{1,0},{2,1},{3,2},{4,3},{5,4},{6,5},{7,6},{8,7},{9,8},{10,9},{11,1... | collective-permute-start | bytes 7077896 | tf_op jit(solution)/shard_map/ppermute | solution.py:294
  28.1 26.5 %collective-permute-start.2 = (bf16[2,2,8,96,384]{4,3,2,1,0:T(8,128)(2,1)}, bf16[2,2,8,96,384]{4,3,2,1,0:T(8,128)(2,1)}, u32[]{:S(2)}, u32[]{:S(2)}) collective-permute-start(bf16[2,2,8,96,384]{4,3,2,1,0:T(8,128)(2,1)} %shard_map.113), channel_id=1, source_target_pairs={{0,1},{1,0},{2,3},{3,2},{4,5},{5,4},{6,7},{7,6},{8,9},{9,8},{10,11... | collective-permute-start | bytes 7077896 | tf_op jit(solution)/shard_map/ppermute | solution.py:294
  29.0 41.8 %copy-start.2 = (bf16[384,1536]{1,0:T(8,128)(2,1)}, bf16[384,1536]{1,0:T(8,128)(2,1)S(1)}, u32[]{:S(2)}) copy-start(bf16[384,1536]{1,0:T(8,128)(2,1)S(1)} %pad_maximum_fusion.refs_12_) | copy-start | bytes 3538948
  29.0 34.3 %collective-permute-start.5 = (bf16[384,1536]{1,0:T(8,128)(2,1)S(1)}, bf16[384,1536]{1,0:T(8,128)(2,1)}, u32[]{:S(2)}, u32[]{:S(2)}) collective-permute-start(bf16[384,1536]{1,0:T(8,128)(2,1)S(1)} %pad_maximum_fusion.refs_12_), channel_id=1, source_target_pairs={{0,1},{1,0},{2,3},{3,2},{4,5},{5,4},{6,7},{7,6},{8,9},{9,8},{10,11... | collective-permute-start | bytes 3538952 | tf_op jit(solution)/shard_map/ppermute | solution.py:294
  63.3 7.5 %copy-start.7 = (s32[1,32,3]{1,0,2:T(1,128)S(1)}, s32[1,32,3]{1,0,2:T(1,128)}, u32[]{:S(2)}) copy-start(s32[1,32,3]{1,0,2:T(1,128)} %param.15) | copy-start | bytes 1156
  63.3 7.8 %copy-start.6 = (f32[1,12,768]{2,0,1:T(1,128)S(1)}, f32[1,12,768]{2,0,1:T(1,128)}, u32[]{:S(2)}) copy-start(f32[1,12,768]{2,0,1:T(1,128)} %param.12) | copy-start | bytes 110596
  63.3 71.6 %all-to-all-start = ((bf16[8,8,96,384]{3,2,1,0:T(8,128)(2,1)}), bf16[8,8,96,384]{3,2,1,0:T(8,128)(2,1)}, u32[]{:S(2)}, u32[]{:S(2)}) async-start(bf16[8,8,96,384]{3,2,1,0:T(8,128)(2,1)} %bitcast.44), calls=%async_computation | async-start | bytes 9437184 | tf_op jit(solution)/shard_map/all_to_all | solution.py:332
  68.0 26.5 %collective-permute-start.7 = (bf16[384,1536]{1,0:T(8,128)(2,1)S(1)}, bf16[384,1536]{1,0:T(8,128)(2,1)}, u32[]{:S(2)}, u32[]{:S(2)}) collective-permute-start(bf16[384,1536]{1,0:T(8,128)(2,1)S(1)} %pad_maximum_fusion.refs_12_), channel_id=1, source_target_pairs={{0,96},{16,112},{32,0},{48,16},{64,32},{80,48},{96,64},{112,80},{1... | collective-permute-start | bytes 3538952 | tf_op jit(solution)/shard_map/ppermute | solution.py:290
  70.8 27.5 %collective-permute-start.6 = (bf16[384,1536]{1,0:T(8,128)(2,1)S(1)}, bf16[384,1536]{1,0:T(8,128)(2,1)}, u32[]{:S(2)}, u32[]{:S(2)}) collective-permute-start(bf16[384,1536]{1,0:T(8,128)(2,1)S(1)} %pad_maximum_fusion.refs_12_), channel_id=1, source_target_pairs={{0,32},{16,48},{32,64},{48,80},{64,96},{80,112},{96,0},{112,16},{1... | collective-permute-start | bytes 3538952 | tf_op jit(solution)/shard_map/ppermute | solution.py:290
  98.3 3.2 %collective-permute-start.10 = (bf16[384,1536]{1,0:T(8,128)(2,1)}, bf16[384,1536]{1,0:T(8,128)(2,1)}, u32[]{:S(2)}, u32[]{:S(2)}) collective-permute-start(bf16[384,1536]{1,0:T(8,128)(2,1)} %collective-permute-done.7.refs_14_), channel_id=1, source_target_pairs={{0,1},{1,0},{2,3},{3,2},{4,5},{5,4},{6,7},{7,6},{8,9},{9,8},{10,11... | collective-permute-start | bytes 3538952 | tf_op jit(solution)/shard_map/ppermute | solution.py:294
  98.3 4.9 %collective-permute-start.9 = (bf16[384,1536]{1,0:T(8,128)(2,1)}, bf16[384,1536]{1,0:T(8,128)(2,1)}, u32[]{:S(2)}, u32[]{:S(2)}) collective-permute-start(bf16[384,1536]{1,0:T(8,128)(2,1)} %collective-permute-done.6.refs_12_), channel_id=1, source_target_pairs={{0,1},{1,0},{2,3},{3,2},{4,5},{5,4},{6,7},{7,6},{8,9},{9,8},{10,11... | collective-permute-start | bytes 3538952 | tf_op jit(solution)/shard_map/ppermute | solution.py:294
  98.8 33.3 %collective-permute-start.8 = (bf16[384,1536]{1,0:T(8,128)(2,1)}, bf16[384,1536]{1,0:T(8,128)(2,1)}, u32[]{:S(2)}, u32[]{:S(2)}) collective-permute-start(bf16[384,1536]{1,0:T(8,128)(2,1)} %collective-permute-done.6.refs_12_), channel_id=1, source_target_pairs={{0,32},{16,48},{32,64},{48,80},{64,96},{80,112},{96,0},{112,16},{1... | collective-permute-start | bytes 3538952 | tf_op jit(solution)/shard_map/ppermute | solution.py:290
  134.9 21.3 %collective-permute-start.11 = (bf16[384,1536]{1,0:T(8,128)(2,1)}, bf16[384,1536]{1,0:T(8,128)(2,1)}, u32[]{:S(2)}, u32[]{:S(2)}) collective-permute-start(bf16[384,1536]{1,0:T(8,128)(2,1)} %collective-permute-done.8.refs_12_), channel_id=1, source_target_pairs={{0,1},{1,0},{2,3},{3,2},{4,5},{5,4},{6,7},{7,6},{8,9},{9,8},{10,11... | collective-permute-start | bytes 3538952 | tf_op jit(solution)/shard_map/ppermute | solution.py:294
  134.9 38.1 %collective-permute-start.14 = (bf16[2,384,768]{2,1,0:T(8,128)(2,1)}, bf16[2,384,768]{2,1,0:T(8,128)(2,1)}, u32[]{:S(2)}, u32[]{:S(2)}) collective-permute-start(bf16[2,384,768]{2,1,0:T(8,128)(2,1)} %get-tuple-element.74), channel_id=1, source_target_pairs={{0,1},{1,2},{2,3},{3,4},{4,5},{5,6},{6,7},{7,8},{8,9},{9,10},{10,1... | collective-permute-start | bytes 3538952 | tf_op jit(solution)/shard_map/ppermute | solution.py:294
  137.2 35.9 %collective-permute-start.15 = (bf16[2,384,768]{2,1,0:T(8,128)(2,1)}, bf16[2,384,768]{2,1,0:T(8,128)(2,1)}, u32[]{:S(2)}, u32[]{:S(2)}) collective-permute-start(bf16[2,384,768]{2,1,0:T(8,128)(2,1)} %get-tuple-element.75), channel_id=1, source_target_pairs={{1,0},{2,1},{3,2},{4,3},{5,4},{6,5},{7,6},{8,7},{9,8},{10,9},{11,1... | collective-permute-start | bytes 3538952 | tf_op jit(solution)/shard_map/ppermute | solution.py:294
  139.3 33.7 %collective-permute-start.12 = (bf16[2,384,384]{2,1,0:T(8,128)(2,1)}, bf16[2,384,384]{2,1,0:T(8,128)(2,1)S(1)}, u32[]{:S(2)}, u32[]{:S(2)}) collective-permute-start(bf16[2,384,384]{2,1,0:T(8,128)(2,1)} %get-tuple-element.72), channel_id=1, source_target_pairs={{0,1},{1,2},{2,3},{3,4},{4,5},{5,6},{6,7},{7,8},{8,9},{9,10},{10,1... | collective-permute-start | bytes 1769480 | tf_op jit(solution)/shard_map/ppermute | solution.py:294
  146.4 26.6 %collective-permute-start.13 = (bf16[2,384,384]{2,1,0:T(8,128)(2,1)}, bf16[2,384,384]{2,1,0:T(8,128)(2,1)S(1)}, u32[]{:S(2)}, u32[]{:S(2)}) collective-permute-start(bf16[2,384,384]{2,1,0:T(8,128)(2,1)} %get-tuple-element.73), channel_id=1, source_target_pairs={{1,0},{2,1},{3,2},{4,3},{5,4},{6,5},{7,6},{8,7},{9,8},{10,9},{11,1... | collective-permute-start | bytes 1769480 | tf_op jit(solution)/shard_map/ppermute | solution.py:294
  152.4 20.7 %all-to-all-start.1 = ((bf16[8,96,384]{2,1,0:T(8,128)(2,1)}), bf16[8,96,384]{2,1,0:T(8,128)(2,1)S(1)}, u32[]{:S(2)}, u32[]{:S(2)}) async-start(bf16[8,96,384]{2,1,0:T(8,128)(2,1)} %reduce_sum.24), calls=%async_computation.1 | async-start | bytes 1179648 | tf_op jit(solution)/shard_map/all_to_all | solution.py:361
  173.0 16.3 %copy-start.4 = (bf16[2,384,384]{2,1,0:T(8,128)(2,1)}, bf16[2,384,384]{2,1,0:T(8,128)(2,1)S(1)}, u32[]{:S(2)}) copy-start(bf16[2,384,384]{2,1,0:T(8,128)(2,1)S(1)} %collective-permute-done.12.refs_2_) | copy-start | bytes 1769476
  173.0 8.9 %copy-start.5 = (bf16[2,384,384]{2,1,0:T(8,128)(2,1)}, bf16[2,384,384]{2,1,0:T(8,128)(2,1)S(1)}, u32[]{:S(2)}) copy-start(bf16[2,384,384]{2,1,0:T(8,128)(2,1)S(1)} %collective-permute-done.13.refs_3_) | copy-start | bytes 1769476
  174.4 34.0 %all-to-all-start.2 = ((bf16[16,96,384]{2,1,0:T(8,128)(2,1)}), bf16[16,96,384]{2,1,0:T(8,128)(2,1)}, u32[]{:S(2)}, u32[]{:S(2)}) async-start(bf16[16,96,384]{2,1,0:T(8,128)(2,1)} %broadcast_in_dim.30), calls=%async_computation.2 | async-start | bytes 2359296 | tf_op jit(solution)/shard_map/all_to_all | solution.py:365
  181.9 19.8 %collective-permute-start.16 = (bf16[2,384,384]{2,1,0:T(8,128)(2,1)}, bf16[2,384,384]{2,1,0:T(8,128)(2,1)S(1)}, u32[]{:S(2)}, u32[]{:S(2)}) collective-permute-start(bf16[2,384,384]{2,1,0:T(8,128)(2,1)} %get-tuple-element.79), channel_id=1, source_target_pairs={{0,1},{1,2},{2,3},{3,4},{4,5},{5,6},{6,7},{7,8},{8,9},{9,10},{10,1... | collective-permute-start | bytes 1769480 | tf_op jit(solution)/shard_map/ppermute | solution.py:294
  186.8 18.4 %collective-permute-start.17 = (bf16[2,384,384]{2,1,0:T(8,128)(2,1)}, bf16[2,384,384]{2,1,0:T(8,128)(2,1)}, u32[]{:S(2)}, u32[]{:S(2)}) collective-permute-start(bf16[2,384,384]{2,1,0:T(8,128)(2,1)} %get-tuple-element.80), channel_id=1, source_target_pairs={{1,0},{2,1},{3,2},{4,3},{5,4},{6,5},{7,6},{8,7},{9,8},{10,9},{11,1... | collective-permute-start | bytes 1769480 | tf_op jit(solution)/shard_map/ppermute | solution.py:294
  201.7 3.5 %copy-start.3 = (bf16[2,384,384]{2,1,0:T(8,128)(2,1)}, bf16[2,384,384]{2,1,0:T(8,128)(2,1)S(1)}, u32[]{:S(2)}) copy-start(bf16[2,384,384]{2,1,0:T(8,128)(2,1)S(1)} %collective-permute-done.16.refs_2_) | copy-start | bytes 1769476
  205.2 5.8 %copy-start.1 = (bf16[192,3072]{1,0:T(8,128)(2,1)S(1)}, bf16[192,3072]{1,0:T(8,128)(2,1)}, u32[]{:S(2)}) copy-start(bf16[192,3072]{1,0:T(8,128)(2,1)} %param.14) | copy-start | bytes 3538948

commit v4 on v3

--- a/solution.py
+++ b/solution.py
@@ -28,22 +28,27 @@
 
 
 def attend_kernel(slabs, *refs):
-    meta, q, kb, ko, ka, vb, vo, va, near, away, o, norm = refs[:12]
-    weights_in = refs[12 : 12 + 2 * slabs]
-    dq, dko, dvo, low, high, kw, vw, dka, dva, gs = refs[-10:]
+    meta, q, kb, ko, ka, vb, vo, va, o, norm = refs[:10]
     step = pl.program_id(0)
     head = meta[HEADS_AT + step]
-    per = gs.shape[0]
-    for n in range(slabs):
-
-        @pl.when(step == n * per)
-        def _(n=n):
-            made = dot(near[...], weights_in[2 * n][...], NT)
-            made += dot(away[...], weights_in[2 * n + 1][...], NT)
-            for m in range(per):
-                gs[m] = made[:, m * HEAD : (m + 1) * HEAD].astype(BF16)
-
-    g = gs.at[lax.rem(step, per)]
+    if slabs:
+        near, away = refs[10:12]
+        weights_in = refs[12 : 12 + 2 * slabs]
+        dq, dko, dvo, low, high, kw, vw, dka, dva, gs = refs[-10:]
+        per = gs.shape[0]
+        for n in range(slabs):
+
+            @pl.when(step == n * per)
+            def _(n=n):
+                made = dot(near[...], weights_in[2 * n][...], NT)
+                made += dot(away[...], weights_in[2 * n + 1][...], NT)
+                for m in range(per):
+                    gs[m] = made[:, m * HEAD : (m + 1) * HEAD].astype(BF16)
+
+        g = gs.at[lax.rem(step, per)]
+    else:
+        g = refs[10]
+        dq, dko, dvo, low, high, kw, vw, dka, dva = refs[-9:]
     kw[0] = kb[0]
     kw[1] = ko[:TILE]
     kw[2] = ko[TILE:]
@@ -83,49 +88,55 @@
     high[1] = dva[3].astype(BF16)
 
 
-def attend(meta, q, k, v, before, after, grads, o, norm, slabs, dq_full):
-    per = slabs[0][0].shape[0] // HEAD
-    heads = per * len(slabs)
-    half = slabs[0][0].shape[1]
+def attend(meta, q, k, v, before, after, o, norm, g, slabs, grads, width, start, filled):
+    heads = meta.shape[0] - HEADS_AT
     own = pl.BlockSpec((2 * TILE, HEAD), lambda i, m: (0, m[HEADS_AT + i]))
     rim_k = pl.BlockSpec((1, TILE, HEAD), lambda i, m: (0, 0, m[HEADS_AT + i]))
     rim_v = pl.BlockSpec((1, TILE, HEAD), lambda i, m: (1, 0, m[HEADS_AT + i]))
-    local = pl.BlockSpec((2 * TILE, HEAD), lambda i, m: (0, i))
-    local_rim = pl.BlockSpec((2, TILE, HEAD), lambda i, m: (0, 0, i))
-    near = pl.BlockSpec((2 * TILE, half), lambda i, m: (0, m[6]))
-    away = pl.BlockSpec((2 * TILE, half), lambda i, m: (0, 1 - m[6]))
-    slab = pl.BlockSpec((per * HEAD, half), lambda i, m: (0, 0))
+    local = pl.BlockSpec((2 * TILE, HEAD), lambda i, m: (0, i + start))
+    local_rim = pl.BlockSpec((2, TILE, HEAD), lambda i, m: (0, 0, i + start))
     whole = pl.BlockSpec(norm.shape, lambda i, m: (0, 0))
     anywhere = pl.BlockSpec(memory_space=pl.ANY)
-    wide = jax.ShapeDtypeStruct((2 * TILE, heads * HEAD), F32)
-    rims = jax.ShapeDtypeStruct((2, TILE, heads * HEAD), BF16)
-    flops = heads * (6 * 5 * 2 * TILE * TILE * HEAD + 2 * 2 * TILE * 2 * half * HEAD)
-    flat = [w for pair in slabs for w in pair]
-    full = [] if dq_full is None else [dq_full]
+    wide = jax.ShapeDtypeStruct((2 * TILE, width), F32)
+    rims = jax.ShapeDtypeStruct((2, TILE, width), BF16)
+    in_specs = [own, rim_k, own, rim_k, rim_v, own, rim_v, own, whole]
+    operands = [q, before, k, after, before, v, after, o, norm]
+    scratch = [
+        pltpu.VMEM((4, TILE, HEAD), BF16),
+        pltpu.VMEM((4, TILE, HEAD), BF16),
+        pltpu.VMEM((4, TILE, HEAD), F32),
+        pltpu.VMEM((4, TILE, HEAD), F32),
+    ]
+    flops = heads * 6 * 5 * 2 * TILE * TILE * HEAD
+    if slabs:
+        rows, half = slabs[0][0].shape
+        in_specs += [
+            pl.BlockSpec((2 * TILE, half), lambda i, m: (0, m[6])),
+            pl.BlockSpec((2 * TILE, half), lambda i, m: (0, 1 - m[6])),
+        ]
+        in_specs += [pl.BlockSpec((rows, half), lambda i, m: (0, 0))] * (2 * len(slabs))
+        operands += [grads, grads, *(w for pair in slabs for w in pair)]
+        scratch.append(pltpu.VMEM((rows // HEAD, 2 * TILE, HEAD), BF16))
+        flops += heads * 2 * 2 * TILE * 2 * half * HEAD
+    else:
+        in_specs.append(pl.BlockSpec((2 * TILE, HEAD), lambda i, m: (0, i)))
+        operands.append(g)
     return pl.pallas_call(
         functools.partial(attend_kernel, len(slabs)),
         grid_spec=pltpu.PrefetchScalarGridSpec(
             num_scalar_prefetch=1,
             grid=(heads,),
-            in_specs=[own, rim_k, own, rim_k, rim_v, own, rim_v, near, away, own, whole]
-            + [slab] * len(flat)
-            + [anywhere] * len(full),
+            in_specs=in_specs + [anywhere] * len(filled),
             out_specs=[own, local, local, local_rim, local_rim],
-            scratch_shapes=[
-                pltpu.VMEM((4, TILE, HEAD), BF16),
-                pltpu.VMEM((4, TILE, HEAD), BF16),
-                pltpu.VMEM((4, TILE, HEAD), F32),
-                pltpu.VMEM((4, TILE, HEAD), F32),
-                pltpu.VMEM((per, 2 * TILE, HEAD), BF16),
-            ],
+            scratch_shapes=scratch,
         ),
         out_shape=[jax.ShapeDtypeStruct(q.shape, BF16), wide, wide, rims, rims],
-        input_output_aliases={12 + len(flat): 0} if full else {},
+        input_output_aliases={1 + len(operands) + n: n for n in range(len(filled))},
         compiler_params=pltpu.CompilerParams(vmem_limit_bytes=VMEM),
         cost_estimate=pl.CostEstimate(
             flops=flops, bytes_accessed=heads * 2_000_000, transcendentals=heads * 6 * TILE * TILE
         ),
-    )(meta, q, before, k, after, before, v, after, grads, grads, o, norm, *flat, *full)
+    )(meta, *operands, *filled)
 
 
 def combine_kernel(edges, meta, *refs):
@@ -144,7 +155,7 @@
 
 def combine(blocks, groups, *filled):
     edges, in_specs, flat, start = [], [], [], 0
-    wide = min(group[0].shape[1] for group in groups)
+    wide = blocks[2]
     width = blocks[1] * wide
     anywhere = pl.BlockSpec(memory_space=pl.ANY)
     for group in groups:
@@ -324,9 +335,15 @@
     from_up = up(pair0)
     from_down = down(pair0)
     across0 = swap(pair0)
-    met0, met1, before, after = lax.optimization_barrier((swap(sent0), swap(sent1), before, after))
+    rows_here = jnp.concatenate(
+        [jnp.where(core == 0, pair0, across0), jnp.where(core == 0, across0, pair0)], axis=1
+    )
+    g0 = dot(grad_rows, rows_here, NT).astype(BF16)
+    met0, met1, before, after, g0 = lax.optimization_barrier(
+        (swap(sent0), swap(sent1), before, after, g0)
+    )
     chip_sum = product(core[None], out_rows, grad_rows, n_z, n_x, n_dp, 1, met0, met1)
-    chip_sum, across0 = lax.optimization_barrier((chip_sum, across0))
+    chip_sum, g0, from_up, from_down = lax.optimization_barrier((chip_sum, g0, from_up, from_down))
     chips = [[2 * i + c for i in range(n_seq // 2)] for c in range(2)]
     piece = chip_sum.shape[-2:]
     spread = lax.all_to_all(
@@ -334,40 +351,46 @@
     )
 
     per = width // n_y // HEAD
-    pending = []
-
-    def attend_group(ats, slabs, dq):
+
+    def attend_group(ats, g, slabs, width, start, filled):
         heads = [(at % n_y) * per + jnp.arange(per, dtype=jnp.int32) for at in ats]
-        heads = jnp.concatenate(heads).astype(jnp.int32)
-        meta = jnp.concatenate([slots, core[None], heads]).astype(jnp.int32)
-        dq, dko, dvo, low, high = attend(
-            meta, q, k, v, before, after, grad_rows, out_rows, norm, slabs, dq
+        meta = jnp.concatenate([slots, core[None], *heads]).astype(jnp.int32)
+        return attend(
+            meta, q, k, v, before, after, out_rows, norm, g, slabs, grad_rows, width, start, filled
         )
-        below = over_seq(high, lambda i: i + 1)
-        above = over_seq(low, lambda i: i - 1)
-        pending.append([dko, dvo, below, above])
-        return dq
-
-    dq = attend_group([y], [(pair0, across0)], None)
-    from_up, from_down, dq = lax.optimization_barrier((from_up, from_down, dq))
+
+    def rims_of(low, high):
+        return [over_seq(high, lambda i: i + 1), over_seq(low, lambda i: i - 1)]
+
+    three = width // n_y
     far = up(from_up)
-    dq = attend_group(
-        [y + n_y - 1, y + 1], [(from_up, swap(from_up)), (from_down, swap(from_down))], dq
-    )
+    across_up, across_down = swap(from_up), swap(from_down)
+    begun = attend_group([y], g0, [], 3 * three, 0, [])
+    most = attend_group(
+        [y + n_y - 1, y + 1],
+        None,
+        [(from_up, across_up), (from_down, across_down)],
+        3 * three,
+        per,
+        begun,
+    )
+    dq, dko, dvo, low, high = most
     spread, far, dq = lax.optimization_barrier((spread, far, dq))
+    rims = rims_of(low, high)
     clip_sum = spread.astype(F32).sum(0).astype(BF16)
-    dq = attend_group([y + 2], [(far, swap(far))], dq)
+    dq, *rest = attend_group([y + 2], None, [(far, swap(far))], three, 0, [dq])
+    pending = [[dko, dvo, *rims], [*rest[:2], *rims_of(*rest[2:])]]
 
     met = lax.all_to_all(clip_sum, "dp", 0, 0)
-    met, dq, *rims = lax.optimization_barrier((met, dq, *pending[0][2:], *pending[1][2:]))
-    pending[0][2:], pending[1][2:] = rims[:2], rims[2:]
+    met, dq, *rims = lax.optimization_barrier((met, dq, *pending[0][2:]))
+    pending[0][2:] = rims
     total = met.astype(F32).sum(0).astype(BF16)
     ready = lax.all_to_all(jnp.broadcast_to(total, (n_seq, *piece)), "seq", 0, 0)
     weight_grad = lay_out(ready, n_z)
 
     blocks = jnp.stack([y, (y + n_y - 1) % n_y, (y + 1) % n_y, (y + 2) % n_y]).astype(jnp.int32)
-    filled = combine((blocks[:3], n_y), pending[:2])
-    dk, dv = combine((blocks[3:], n_y), pending[2:], *filled)
+    filled = combine((blocks[:3], n_y, three), pending[:1])
+    dk, dv = combine((blocks[3:], n_y, three), pending[1:], *filled)
     return (dq[None], dk[None], dv[None], weight_grad)
 
 

time: 212 us -> 205 us (0.967)
  waiting for transfers between devices: 49.1 us -> 37.8 us
  matrix products: 0 us -> 5.77 us
  Pallas kernels: 101 us -> 95.9 us
  other arithmetic: 6.17 us -> 8.62 us
    ppermute x14 -> x12, waiting for transfers between devices: 37.1 us -> 24.1 us  [over_seq(): lax.ppermute(value, 'seq', [(i, j) for i, j in pairs if 0 <= j < n_seq])]
    all_to_all x1, waiting for transfers between devices: 2.81 us -> 13 us  [body(): lax.all_to_all(chip_sum.reshape(n_seq // 2, n_dp, *piece), 'seq', 0, 0, a...]
    ppermute x4, waiting for transfers between devices: 9.19 us -> 0.68 us  [over_dp(): return lax.ppermute(value, 'dp', [(i, target(i)) for i in range(n_dp)])]
    dot_general x0 -> x1, matrix products: none -> 5.77 us  [dot(): return lax.dot_general(a, b, dims, preferred_element_type=F32)]
    pallas_call x3, Pallas kernels: 62.4 us -> 57.5 us  [attend(): pl.pallas_call(functools.partial(attend_kernel, len(slabs)), grid_spec=pl...]
    all_to_all x1, starting transfers between devices: 4.69 us -> 7.5 us  [body(): lax.all_to_all(chip_sum.reshape(n_seq // 2, n_dp, *piece), 'seq', 0, 0, a...]
    ppermute x14 -> x12, starting transfers between devices: 29.3 us -> 26.7 us  [over_seq(): lax.ppermute(value, 'seq', [(i, j) for i, j in pairs if 0 <= j < n_seq])]
  transfers between devices with their start and end apart: 21 -> 19, of which waited for: 9 -> 8; matrix products, arithmetic and copies ran while one was open for 3% -> 7% of each run, Pallas kernels for 44% -> 43%
where the time goes in v4:
time: 205 us; the launch traced here: 204 us
  Pallas kernels  95.9 us (47%)
  starting transfers between devices  50.9 us (25%)
  waiting for transfers between devices  37.8 us (18%)
  other arithmetic  8.62 us (4%)
  matrix products  5.77 us (3%)
  local copies, waits for them, and re-layouts  4.3 us (2%)
    pallas_call x3, Pallas kernels, attend(): pl.pallas_call(functools.partial(attend_kernel, len(slabs)), grid_spec=pl...  57.5 us
    ppermute x12, starting transfers between devices, over_seq(): lax.ppermute(value, 'seq', [(i, j) for i, j in pairs if 0 <= j < n_seq])  26.7 us
    ppermute x12, waiting for transfers between devices, over_seq(): lax.ppermute(value, 'seq', [(i, j) for i, j in pairs if 0 <= j < n_seq])  24.1 us
    pallas_call x3, Pallas kernels, product(): pl.pallas_call(product_kernel, grid_spec=pltpu.PrefetchScalarGridSpec(num...  20.1 us
    all_to_all x1, waiting for transfers between devices, body(): lax.all_to_all(chip_sum.reshape(n_seq // 2, n_dp, *piece), 'seq', 0, 0, a...  13 us
    pallas_call x2, Pallas kernels, combine(): pl.pallas_call(functools.partial(combine_kernel, edges), grid_spec=pltpu....  10.4 us
    all_to_all x1, starting transfers between devices, body(): lax.all_to_all(chip_sum.reshape(n_seq // 2, n_dp, *piece), 'seq', 0, 0, a...  7.5 us
    all_to_all x1, starting transfers between devices, body(): lax.all_to_all(jnp.broadcast_to(total, (n_seq, *piece)), 'seq', 0, 0)  7.27 us
  transfers between devices with their start and end apart: 19, of which 8 were waited for; matrix products, arithmetic and copies ran while one was open for 7% of the time, Pallas kernels for 43%

profile of v4, /device:TPU:7, one launch (start us, length us, event | category | flops | bytes accessed | tf_op | source)
XLA Modules:
  0.0 204.1 jit_solution(10201793403358394731)
XLA Ops:
  0.7 1.2 copy-done
  2.0 5.3 %shard_map.111 = (bf16[2,384,1536]{2,1,0:T(8,128)(2,1)}, bf16[2,384,1536]{2,1,0:T(8,128)(2,1)}) custom-call(bf16[768,1536]{1,0:T(8,128)(2,1)} %bitcast.36, bf16[768,1536]{1,0:T(8,128)(2,1)} %bitcast.37, bf16[768,1536]{1,0:T(8,128)(2,1)} %bitcast.41, bf16[768,1536]{1,0:T(8,128)(2,1)} %bitcast.42), custom_call_target="tpu_custom_call" | custom-call | tf_op jit(solution)/shard_map/pallas_call | solution.py:273
  7.3 1.6 collective-permute-start.1
  8.9 5.6 %shard_map.112 = bf16[2,2,8,96,384]{4,3,2,1,0:T(8,128)(2,1)} custom-call(s32[1]{0:T(128)} %bitcast.3.which, bf16[768,1536]{1,0:T(8,128)(2,1)} %bitcast.30, bf16[768,3072]{1,0:T(8,128)(2,1)} %bitcast.23), custom_call_target="tpu_custom_call" | custom-call | flops 56623104 | bytes 400000 | tf_op jit(solution)/shard_map/pallas_call | solution.py:216
  14.6 1.0 collective-permute-start
  15.5 5.0 %collective-permute-start.3 = (bf16[2,384,1536]{2,1,0:T(8,128)(2,1)}, bf16[2,384,1536]{2,1,0:T(8,128)(2,1)}, u32[]{:S(2)}, u32[]{:S(2)}) collective-permute-start(bf16[2,384,1536]{2,1,0:T(8,128)(2,1)} %get-tuple-element.52), channel_id=1, source_target_pairs={{0,1},{1,2},{2,3},{3,4},{4,5},{5,6},{6,7},{7,8},{8,9},{9,10},{10,1... | collective-permute-start | bytes 7077896 | tf_op jit(solution)/shard_map/ppermute | solution.py:305
  20.5 1.9 collective-permute-start.4
  22.5 5.9 %shard_map.113 = bf16[2,2,8,96,384]{4,3,2,1,0:T(8,128)(2,1)} custom-call(s32[1]{0:T(128)} %bitcast.6.which, bf16[768,1536]{1,0:T(8,128)(2,1)} %bitcast.31, bf16[768,3072]{1,0:T(8,128)(2,1)} %bitcast.24), custom_call_target="tpu_custom_call" | custom-call | flops 56623104 | bytes 400000 | tf_op jit(solution)/shard_map/pallas_call | solution.py:216
  28.4 0.7 collective-permute-start.2
  29.1 1.1 broadcast_select_fusion.3
  30.2 1.1 pad_maximum_fusion
  31.3 3.8 %collective-permute-done.5 = bf16[384,1536]{1,0:T(8,128)(2,1)S(1)} collective-permute-done((bf16[384,1536]{1,0:T(8,128)(2,1)}, bf16[384,1536]{1,0:T(8,128)(2,1)S(1)}, u32[]{:S(2)}, u32[]{:S(2)}) %collective-permute-start.5) | collective-permute-done | bytes 1179680 | tf_op jit(solution)/shard_map/ppermute | solution.py:305
  35.1 1.3 collective-permute-start.6
  36.4 1.4 collective-permute-start.7
  37.9 0.4 broadcast_select_fusion.1
  38.3 5.8 %fusion.7.refs_10_ = bf16[768,384]{1,0:T(8,128)(2,1)} fusion(bf16[384,1536]{1,0:T(8,128)(2,1)S(1)} %get-tuple-element.91, bf16[384,1536]{1,0:T(8,128)(2,1)S(1)} %get-tuple-element.90, bf16[1,768,3072]{2,1,0:T(8,128)(2,1)} %param.13), kind=kOutput, calls=%fused_computation.5 | convolution fusion | flops 1816952832 | bytes 7667712 | tf_op jit(solution)/shard_map/dot_general | solution.py:23
  44.0 2.6 %collective-permute-done.3.refs_2_.refs_5_ = bf16[2,384,1536]{2,1,0:T(8,128)(2,1)} collective-permute-done((bf16[2,384,1536]{2,1,0:T(8,128)(2,1)}, bf16[2,384,1536]{2,1,0:T(8,128)(2,1)}, u32[]{:S(2)}, u32[]{:S(2)}) %collective-permute-start.3) | collective-permute-done | bytes 2359328 | tf_op jit(solution)/shard_map/ppermute | solution.py:305
  46.6 8.0 %collective-permute-done.4.refs_4_.refs_7_ = bf16[2,384,1536]{2,1,0:T(8,128)(2,1)} collective-permute-done((bf16[2,384,1536]{2,1,0:T(8,128)(2,1)}, bf16[2,384,1536]{2,1,0:T(8,128)(2,1)}, u32[]{:S(2)}, u32[]{:S(2)}) %collective-permute-start.4) | collective-permute-done | bytes 2359328 | tf_op jit(solution)/shard_map/ppermute | solution.py:305
  54.6 8.6 %shard_map.114 = bf16[2,4,8,96,384]{4,3,2,1,0:T(8,128)(2,1)} custom-call(s32[1]{0:T(128)} %bitcast.which, bf16[768,1536]{1,0:T(8,128)(2,1)} %bitcast.32, bf16[768,3072]{1,0:T(8,128)(2,1)} %bitcast.25, bf16[2,2,8,96,384]{4,3,2,1,0:T(8,128)(2,1)} %collective-permute-done.refs_0_, bf16[2,2,8,96,384]{4,3,2,1,0:T(8,128)(2,1)} %collective-permute-done.2.refs_1_), custom_call_target="tpu_custom_call" | custom-call | flops 113246208 | bytes 400000 | tf_op jit(solution)/shard_map/pallas_call | solution.py:216
  63.3 0.7 collective-permute-done.6.refs_12_
  64.0 7.5 %all-to-all-start = ((bf16[8,8,96,384]{3,2,1,0:T(8,128)(2,1)}), bf16[8,8,96,384]{3,2,1,0:T(8,128)(2,1)}, u32[]{:S(2)}, u32[]{:S(2)}) async-start(bf16[8,8,96,384]{3,2,1,0:T(8,128)(2,1)} %bitcast.49), calls=%async_computation | async-start | bytes 9437184 | tf_op jit(solution)/shard_map/all_to_all | solution.py:349
  71.5 1.7 collective-permute-start.10
  73.2 0.1 copy.26
  73.4 0.6 copy.28
  74.1 0.6 pad_add_fusion.refs_0_
  74.7 0.7 pad_add_fusion.3
  75.3 1.3 collective-permute-start.8
  76.6 11.8 %shard_map.115 = (bf16[768,1536]{1,0:T(8,128)(2,1)}, f32[768,1152]{1,0:T(8,128)}, f32[768,1152]{1,0:T(8,128)}, bf16[2,384,1152]{2,1,0:T(8,128)(2,1)}, bf16[2,384,1152]{2,1,0:T(8,128)(2,1)}) custom-call(s32[10]{0:T(128)} %get-tuple-element.95.refs_0_, bf16[768,1536]{1,0:T(8,128)(2,1)} %bitcast.46, ...), custom_call_target="tpu_custom_call" | custom-call | flops 3397386240 | bytes 6000000 | tf_op jit(solution)/shard_map/pallas_call | solution.py:124
  88.5 1.0 copy-done.2
  89.5 28.9 %shard_map.116 = (bf16[768,1536]{1,0:T(8,128)(2,1)}, f32[768,1152]{1,0:T(8,128)}, f32[768,1152]{1,0:T(8,128)}, bf16[2,384,1152]{2,1,0:T(8,128)(2,1)}, bf16[2,384,1152]{2,1,0:T(8,128)(2,1)}) custom-call(s32[13]{0:T(128)} %pad_add_fusion.refs_0_, ...), custom_call_target="tpu_custom_call", output_to_operand_aliasing={{0}: (16, {}), {1}: (17, {}), {2}: (18, {}), {3}: (19, {}),... | custom-call | flops 10418651136 | bytes 12000000 | tf_op jit(solution)/shard_map/pallas_call | solution.py:124
  118.4 5.3 %collective-permute-start.12 = (bf16[2,384,1152]{2,1,0:T(8,128)(2,1)}, bf16[2,384,1152]{2,1,0:T(8,128)(2,1)}, u32[]{:S(2)}, u32[]{:S(2)}) collective-permute-start(bf16[2,384,1152]{2,1,0:T(8,128)(2,1)} %get-tuple-element.74), channel_id=1, source_target_pairs={{0,1},{1,2},{2,3},{3,4},{4,5},{5,6},{6,7},{7,8},{8,9},{9,10},{10,1... | collective-permute-start | bytes 5308424 | tf_op jit(solution)/shard_map/ppermute | solution.py:305
  123.7 1.9 collective-permute-start.13
  125.6 13.0 %all-to-all-done = bf16[8,8,96,384]{3,2,1,0:T(8,128)(2,1)} async-done(((bf16[8,8,96,384]{3,2,1,0:T(8,128)(2,1)}), bf16[8,8,96,384]{3,2,1,0:T(8,128)(2,1)}, u32[]{:S(2)}, u32[]{:S(2)}) %all-to-all-start) | async-done | bytes 4718624 | tf_op jit(solution)/shard_map/all_to_all | solution.py:349
  138.6 2.4 %collective-permute-start.11 = (bf16[384,1536]{1,0:T(8,128)(2,1)}, bf16[384,1536]{1,0:T(8,128)(2,1)}, u32[]{:S(2)}, u32[]{:S(2)}) collective-permute-start(bf16[384,1536]{1,0:T(8,128)(2,1)} %collective-permute-done.8.refs_12_), channel_id=1, source_target_pairs={{0,1},{1,0},{2,3},{3,2},{4,5},{5,4},{6,7},{7,6},{8,9},{9,8},{10,11... | collective-permute-start | bytes 3538952 | tf_op jit(solution)/shard_map/ppermute | solution.py:305
  141.0 4.0 %reduce_sum.24 = bf16[8,96,384]{2,1,0:T(8,128)(2,1)} reduce(bf16[8,8,96,384]{3,2,1,0:T(8,128)(2,1)} %all-to-all-done, bf16[]{:T(256)} %constant.81.clone.1), dimensions={0}, to_apply=%region_0.1 | reduce | flops 2064384 | bytes 5308418 | tf_op jit(solution)/shard_map/reduce_sum | solution.py:380
  145.0 3.8 %all-to-all-start.1 = ((bf16[8,96,384]{2,1,0:T(8,128)(2,1)}), bf16[8,96,384]{2,1,0:T(8,128)(2,1)S(1)}, u32[]{:S(2)}, u32[]{:S(2)}) async-start(bf16[8,96,384]{2,1,0:T(8,128)(2,1)} %reduce_sum.24), calls=%async_computation.1 | async-start | bytes 1179648 | tf_op jit(solution)/shard_map/all_to_all | solution.py:384
  148.8 16.8 %shard_map.117 = (bf16[768,1536]{1,0:T(8,128)(2,1)}, f32[768,384]{1,0:T(8,128)}, f32[768,384]{1,0:T(8,128)}, bf16[2,384,384]{2,1,0:T(8,128)(2,1)}, bf16[2,384,384]{2,1,0:T(8,128)(2,1)}) custom-call(s32[10]{0:T(128)} %get-tuple-element.94.refs_0_, bf16[768,1536]{1,0:T(8,128)(2,1)} %bitcast.48, ...), custom_call_target="tpu_custom_call", output_to_operand_aliasing={{0}: (14, {})} | custom-call | flops 5209325568 | bytes 6000000 | tf_op jit(solution)/shard_map/pallas_call | solution.py:124
  165.6 1.1 collective-permute-done.13.refs_3_
  166.7 1.1 broadcast_in_dim.30
  167.9 7.3 %all-to-all-start.2 = ((bf16[16,96,384]{2,1,0:T(8,128)(2,1)}), bf16[16,96,384]{2,1,0:T(8,128)(2,1)}, u32[]{:S(2)}, u32[]{:S(2)}) async-start(bf16[16,96,384]{2,1,0:T(8,128)(2,1)} %broadcast_in_dim.30), calls=%async_computation.2 | async-start | bytes 2359296 | tf_op jit(solution)/shard_map/all_to_all | solution.py:388
  175.1 4.8 %collective-permute-start.14 = (bf16[2,384,384]{2,1,0:T(8,128)(2,1)}, bf16[2,384,384]{2,1,0:T(8,128)(2,1)S(1)}, u32[]{:S(2)}, u32[]{:S(2)}) collective-permute-start(bf16[2,384,384]{2,1,0:T(8,128)(2,1)} %get-tuple-element.79), channel_id=1, source_target_pairs={{0,1},{1,2},{2,3},{3,4},{4,5},{5,6},{6,7},{7,8},{8,9},{9,10},{10,1... | collective-permute-start | bytes 1769480 | tf_op jit(solution)/shard_map/ppermute | solution.py:305
  180.0 1.9 collective-permute-start.15
  181.9 0.6 pad_add_fusion.4.meta
  182.5 7.2 %shard_map.118 = (bf16[768,1536]{1,0:T(8,128)(2,1)}, bf16[768,1536]{1,0:T(8,128)(2,1)}) custom-call(s32[3]{0:T(128)} %pad_add_fusion.4.meta, f32[768,1152]{1,0:T(8,128)} %get-tuple-element.81.refs_0_, f32[768,1152]{1,0:T(8,128)} %get-tuple-element.82.refs_1_, bf16[2,384,1152]{2,1,0:T(8,128)(2,1)} %collective-permute-done.12.refs_2_, ...), custom_call_target="tpu_custom_call" | custom-call | flops 4000000 | bytes 20000000 | tf_op jit(solution)/shard_map/pallas_call | solution.py:174
  189.7 5.2 %collective-permute-done.14.refs_2_ = bf16[2,384,384]{2,1,0:T(8,128)(2,1)S(1)} collective-permute-done((bf16[2,384,384]{2,1,0:T(8,128)(2,1)}, bf16[2,384,384]{2,1,0:T(8,128)(2,1)S(1)}, u32[]{:S(2)}, u32[]{:S(2)}) %collective-permute-start.14) | collective-permute-done | bytes 589856 | tf_op jit(solution)/shard_map/ppermute | solution.py:305
  194.9 3.5 %collective-permute-done.15.refs_3_ = bf16[2,384,384]{2,1,0:T(8,128)(2,1)} collective-permute-done((bf16[2,384,384]{2,1,0:T(8,128)(2,1)}, bf16[2,384,384]{2,1,0:T(8,128)(2,1)}, u32[]{:S(2)}, u32[]{:S(2)}) %collective-permute-start.15) | collective-permute-done | bytes 589856 | tf_op jit(solution)/shard_map/ppermute | solution.py:305
  198.4 3.2 %shard_map.119 = (bf16[768,1536]{1,0:T(8,128)(2,1)}, bf16[768,1536]{1,0:T(8,128)(2,1)}) custom-call(s32[1]{0:T(128)} %bitcast.11.meta, f32[768,384]{1,0:T(8,128)} %get-tuple-element.77.refs_0_, f32[768,384]{1,0:T(8,128)} %get-tuple-element.78.refs_1_, bf16[2,384,384]{2,1,0:T(8,128)(2,1)} %copy-done.3, ...), custom_call_target="tpu_custom_call", output_to_operand_aliasing={{0}: (5, {}), {1}: (6, {})} | custom-call | flops 4000000 | bytes 20000000 | tf_op jit(solution)/shard_map/pallas_call | solution.py:174
  201.6 2.5 %shard_map.120 = f32[192,3072]{1,0:T(8,128)} custom-call(bf16[16,96,384]{2,1,0:T(8,128)(2,1)} %all-to-all-done.2.pieces), custom_call_target="tpu_custom_call" | custom-call | tf_op jit(solution)/shard_map/pallas_call | solution.py:248
  (32 shorter events, 0.4 us)
Async XLA Ops:
  0.6 1.3 copy-start
  7.3 15.2 %collective-permute-start.1 = (bf16[192,1536]{1,0:T(8,128)(2,1)S(1)}, bf16[192,1536]{1,0:T(8,128)(2,1)S(1)}, u32[]{:S(2)}, u32[]{:S(2)}) collective-permute-start(bf16[192,1536]{1,0:T(8,128)(2,1)S(1)} %constant_dynamic-slice_fusion.1), channel_id=1, source_target_pairs={{0,16},{16,0},{32,48},{48,32},{64,80},{80,64},{96,112},{112,96},{1... | collective-permute-start | bytes 1769480 | tf_op jit(solution)/shard_map/ppermute | solution.py:301
  14.6 21.8 %collective-permute-start = (bf16[2,2,8,96,384]{4,3,2,1,0:T(8,128)(2,1)}, bf16[2,2,8,96,384]{4,3,2,1,0:T(8,128)(2,1)}, u32[]{:S(2)}, u32[]{:S(2)}) collective-permute-start(bf16[2,2,8,96,384]{4,3,2,1,0:T(8,128)(2,1)} %shard_map.112), channel_id=1, source_target_pairs={{0,1},{1,0},{2,3},{3,2},{4,5},{5,4},{6,7},{7,6},{8,9},{9,8},{10,11... | collective-permute-start | bytes 7077896 | tf_op jit(solution)/shard_map/ppermute | solution.py:305
  15.5 31.1 %collective-permute-start.3 = (bf16[2,384,1536]{2,1,0:T(8,128)(2,1)}, bf16[2,384,1536]{2,1,0:T(8,128)(2,1)}, u32[]{:S(2)}, u32[]{:S(2)}) collective-permute-start(bf16[2,384,1536]{2,1,0:T(8,128)(2,1)} %get-tuple-element.52), channel_id=1, source_target_pairs={{0,1},{1,2},{2,3},{3,4},{4,5},{5,6},{6,7},{7,8},{8,9},{9,10},{10,1... | collective-permute-start | bytes 7077896 | tf_op jit(solution)/shard_map/ppermute | solution.py:305
  20.5 34.1 %collective-permute-start.4 = (bf16[2,384,1536]{2,1,0:T(8,128)(2,1)}, bf16[2,384,1536]{2,1,0:T(8,128)(2,1)}, u32[]{:S(2)}, u32[]{:S(2)}) collective-permute-start(bf16[2,384,1536]{2,1,0:T(8,128)(2,1)} %get-tuple-element.53), channel_id=1, source_target_pairs={{1,0},{2,1},{3,2},{4,3},{5,4},{6,5},{7,6},{8,7},{9,8},{10,9},{11,1... | collective-permute-start | bytes 7077896 | tf_op jit(solution)/shard_map/ppermute | solution.py:305
  22.5 5.9 %copy-start.4 = (bf16[192,1536]{1,0:T(8,128)(2,1)}, bf16[192,1536]{1,0:T(8,128)(2,1)S(1)}, u32[]{:S(2)}) copy-start(bf16[192,1536]{1,0:T(8,128)(2,1)S(1)} %collective-permute-done.1) | copy-start | bytes 1769476
  28.4 26.3 %collective-permute-start.2 = (bf16[2,2,8,96,384]{4,3,2,1,0:T(8,128)(2,1)}, bf16[2,2,8,96,384]{4,3,2,1,0:T(8,128)(2,1)}, u32[]{:S(2)}, u32[]{:S(2)}) collective-permute-start(bf16[2,2,8,96,384]{4,3,2,1,0:T(8,128)(2,1)} %shard_map.113), channel_id=1, source_target_pairs={{0,1},{1,0},{2,3},{3,2},{4,5},{5,4},{6,7},{7,6},{8,9},{9,8},{10,11... | collective-permute-start | bytes 7077896 | tf_op jit(solution)/shard_map/ppermute | solution.py:305
  31.3 3.8 %collective-permute-start.5 = (bf16[384,1536]{1,0:T(8,128)(2,1)}, bf16[384,1536]{1,0:T(8,128)(2,1)S(1)}, u32[]{:S(2)}, u32[]{:S(2)}) collective-permute-start(bf16[384,1536]{1,0:T(8,128)(2,1)} %pad_maximum_fusion), channel_id=1, source_target_pairs={{0,1},{1,0},{2,3},{3,2},{4,5},{5,4},{6,7},{7,6},{8,9},{9,8},{10,11... | collective-permute-start | bytes 3538952 | tf_op jit(solution)/shard_map/ppermute | solution.py:305
  35.1 28.8 %collective-permute-start.6 = (bf16[384,1536]{1,0:T(8,128)(2,1)}, bf16[384,1536]{1,0:T(8,128)(2,1)}, u32[]{:S(2)}, u32[]{:S(2)}) collective-permute-start(bf16[384,1536]{1,0:T(8,128)(2,1)} %pad_maximum_fusion), channel_id=1, source_target_pairs={{0,32},{16,48},{32,64},{48,80},{64,96},{80,112},{96,0},{112,16},{1... | collective-permute-start | bytes 3538952 | tf_op jit(solution)/shard_map/ppermute | solution.py:301
  36.4 27.5 %collective-permute-start.7 = (bf16[384,1536]{1,0:T(8,128)(2,1)}, bf16[384,1536]{1,0:T(8,128)(2,1)}, u32[]{:S(2)}, u32[]{:S(2)}) collective-permute-start(bf16[384,1536]{1,0:T(8,128)(2,1)} %pad_maximum_fusion), channel_id=1, source_target_pairs={{0,96},{16,112},{32,0},{48,16},{64,32},{80,48},{96,64},{112,80},{1... | collective-permute-start | bytes 3538952 | tf_op jit(solution)/shard_map/ppermute | solution.py:301
  63.9 9.2 %copy-start.6 = (s32[1,32,3]{1,0,2:T(1,128)S(1)}, s32[1,32,3]{1,0,2:T(1,128)}, u32[]{:S(2)}) copy-start(s32[1,32,3]{1,0,2:T(1,128)} %param.15) | copy-start | bytes 1156
  64.0 9.5 %copy-start.5 = (f32[1,12,768]{2,0,1:T(1,128)S(1)}, f32[1,12,768]{2,0,1:T(1,128)}, u32[]{:S(2)}) copy-start(f32[1,12,768]{2,0,1:T(1,128)} %param.12) | copy-start | bytes 110596
  64.0 74.7 %all-to-all-start = ((bf16[8,8,96,384]{3,2,1,0:T(8,128)(2,1)}), bf16[8,8,96,384]{3,2,1,0:T(8,128)(2,1)}, u32[]{:S(2)}, u32[]{:S(2)}) async-start(bf16[8,8,96,384]{3,2,1,0:T(8,128)(2,1)} %bitcast.49), calls=%async_computation | async-start | bytes 9437184 | tf_op jit(solution)/shard_map/all_to_all | solution.py:349
  71.5 17.0 %collective-permute-start.10 = (bf16[384,1536]{1,0:T(8,128)(2,1)}, bf16[384,1536]{1,0:T(8,128)(2,1)S(1)}, u32[]{:S(2)}, u32[]{:S(2)}) collective-permute-start(bf16[384,1536]{1,0:T(8,128)(2,1)} %collective-permute-done.7.refs_14_), channel_id=1, source_target_pairs={{0,1},{1,0},{2,3},{3,2},{4,5},{5,4},{6,7},{7,6},{8,9},{9,8},{10,11... | collective-permute-start | bytes 3538952 | tf_op jit(solution)/shard_map/ppermute | solution.py:305
  73.2 15.3 %collective-permute-start.9 = (bf16[384,1536]{1,0:T(8,128)(2,1)}, bf16[384,1536]{1,0:T(8,128)(2,1)}, u32[]{:S(2)}, u32[]{:S(2)}) collective-permute-start(bf16[384,1536]{1,0:T(8,128)(2,1)} %collective-permute-done.6.refs_12_), channel_id=1, source_target_pairs={{0,1},{1,0},{2,3},{3,2},{4,5},{5,4},{6,7},{7,6},{8,9},{9,8},{10,11... | collective-permute-start | bytes 3538952 | tf_op jit(solution)/shard_map/ppermute | solution.py:305
  75.3 50.3 %collective-permute-start.8 = (bf16[384,1536]{1,0:T(8,128)(2,1)}, bf16[384,1536]{1,0:T(8,128)(2,1)}, u32[]{:S(2)}, u32[]{:S(2)}) collective-permute-start(bf16[384,1536]{1,0:T(8,128)(2,1)} %collective-permute-done.6.refs_12_), channel_id=1, source_target_pairs={{0,32},{16,48},{32,64},{48,80},{64,96},{80,112},{96,0},{112,16},{1... | collective-permute-start | bytes 3538952 | tf_op jit(solution)/shard_map/ppermute | solution.py:301
  88.5 1.0 copy-start.2
  118.4 47.2 %collective-permute-start.12 = (bf16[2,384,1152]{2,1,0:T(8,128)(2,1)}, bf16[2,384,1152]{2,1,0:T(8,128)(2,1)}, u32[]{:S(2)}, u32[]{:S(2)}) collective-permute-start(bf16[2,384,1152]{2,1,0:T(8,128)(2,1)} %get-tuple-element.74), channel_id=1, source_target_pairs={{0,1},{1,2},{2,3},{3,4},{4,5},{5,6},{6,7},{7,8},{8,9},{9,10},{10,1... | collective-permute-start | bytes 5308424 | tf_op jit(solution)/shard_map/ppermute | solution.py:305
  123.7 43.0 %collective-permute-start.13 = (bf16[2,384,1152]{2,1,0:T(8,128)(2,1)}, bf16[2,384,1152]{2,1,0:T(8,128)(2,1)}, u32[]{:S(2)}, u32[]{:S(2)}) collective-permute-start(bf16[2,384,1152]{2,1,0:T(8,128)(2,1)} %get-tuple-element.75), channel_id=1, source_target_pairs={{1,0},{2,1},{3,2},{4,3},{5,4},{6,5},{7,6},{8,7},{9,8},{10,9},{11,1... | collective-permute-start | bytes 5308424 | tf_op jit(solution)/shard_map/ppermute | solution.py:305
  138.6 10.1 %collective-permute-start.11 = (bf16[384,1536]{1,0:T(8,128)(2,1)}, bf16[384,1536]{1,0:T(8,128)(2,1)}, u32[]{:S(2)}, u32[]{:S(2)}) collective-permute-start(bf16[384,1536]{1,0:T(8,128)(2,1)} %collective-permute-done.8.refs_12_), channel_id=1, source_target_pairs={{0,1},{1,0},{2,3},{3,2},{4,5},{5,4},{6,7},{7,6},{8,9},{9,8},{10,11... | collective-permute-start | bytes 3538952 | tf_op jit(solution)/shard_map/ppermute | solution.py:305
  145.0 21.6 %all-to-all-start.1 = ((bf16[8,96,384]{2,1,0:T(8,128)(2,1)}), bf16[8,96,384]{2,1,0:T(8,128)(2,1)S(1)}, u32[]{:S(2)}, u32[]{:S(2)}) async-start(bf16[8,96,384]{2,1,0:T(8,128)(2,1)} %reduce_sum.24), calls=%async_computation.1 | async-start | bytes 1179648 | tf_op jit(solution)/shard_map/all_to_all | solution.py:384
  167.9 33.7 %all-to-all-start.2 = ((bf16[16,96,384]{2,1,0:T(8,128)(2,1)}), bf16[16,96,384]{2,1,0:T(8,128)(2,1)}, u32[]{:S(2)}, u32[]{:S(2)}) async-start(bf16[16,96,384]{2,1,0:T(8,128)(2,1)} %broadcast_in_dim.30), calls=%async_computation.2 | async-start | bytes 2359296 | tf_op jit(solution)/shard_map/all_to_all | solution.py:388
  175.1 19.8 %collective-permute-start.14 = (bf16[2,384,384]{2,1,0:T(8,128)(2,1)}, bf16[2,384,384]{2,1,0:T(8,128)(2,1)S(1)}, u32[]{:S(2)}, u32[]{:S(2)}) collective-permute-start(bf16[2,384,384]{2,1,0:T(8,128)(2,1)} %get-tuple-element.79), channel_id=1, source_target_pairs={{0,1},{1,2},{2,3},{3,4},{4,5},{5,6},{6,7},{7,8},{8,9},{9,10},{10,1... | collective-permute-start | bytes 1769480 | tf_op jit(solution)/shard_map/ppermute | solution.py:305
  180.0 18.4 %collective-permute-start.15 = (bf16[2,384,384]{2,1,0:T(8,128)(2,1)}, bf16[2,384,384]{2,1,0:T(8,128)(2,1)}, u32[]{:S(2)}, u32[]{:S(2)}) collective-permute-start(bf16[2,384,384]{2,1,0:T(8,128)(2,1)} %get-tuple-element.80), channel_id=1, source_target_pairs={{1,0},{2,1},{3,2},{4,3},{5,4},{6,5},{7,6},{8,7},{9,8},{10,9},{11,1... | collective-permute-start | bytes 1769480 | tf_op jit(solution)/shard_map/ppermute | solution.py:305
  194.9 3.5 %copy-start.3 = (bf16[2,384,384]{2,1,0:T(8,128)(2,1)}, bf16[2,384,384]{2,1,0:T(8,128)(2,1)S(1)}, u32[]{:S(2)}) copy-start(bf16[2,384,384]{2,1,0:T(8,128)(2,1)S(1)} %collective-permute-done.14.refs_2_) | copy-start | bytes 1769476
  198.4 5.8 %copy-start.1 = (bf16[192,3072]{1,0:T(8,128)(2,1)S(1)}, bf16[192,3072]{1,0:T(8,128)(2,1)}, u32[]{:S(2)}) copy-start(bf16[192,3072]{1,0:T(8,128)(2,1)} %param.14) | copy-start | bytes 3538948

commit v5 on v4

--- a/solution.py
+++ b/solution.py
@@ -343,7 +343,7 @@
         (swap(sent0), swap(sent1), before, after, g0)
     )
     chip_sum = product(core[None], out_rows, grad_rows, n_z, n_x, n_dp, 1, met0, met1)
-    chip_sum, g0, from_up, from_down = lax.optimization_barrier((chip_sum, g0, from_up, from_down))
+    chip_sum, g0 = lax.optimization_barrier((chip_sum, g0))
     chips = [[2 * i + c for i in range(n_seq // 2)] for c in range(2)]
     piece = chip_sum.shape[-2:]
     spread = lax.all_to_all(
@@ -363,9 +363,10 @@
         return [over_seq(high, lambda i: i + 1), over_seq(low, lambda i: i - 1)]
 
     three = width // n_y
+    begun = attend_group([y], g0, [], 3 * three, 0, [])
+    from_up, from_down, *begun = lax.optimization_barrier((from_up, from_down, *begun))
     far = up(from_up)
     across_up, across_down = swap(from_up), swap(from_down)
-    begun = attend_group([y], g0, [], 3 * three, 0, [])
     most = attend_group(
         [y + n_y - 1, y + 1],
         None,

time: 205 us -> 207 us (level)
  waiting for transfers between devices: 37.8 us -> 50.2 us
  starting transfers between devices: 50.9 us -> 41.2 us
    ppermute x4, waiting for transfers between devices: 0.68 us -> 14.4 us  [over_dp(): return lax.ppermute(value, 'dp', [(i, target(i)) for i in range(n_dp)])]
    all_to_all x1, waiting for transfers between devices: 13 us -> 0.01 us  [body(): lax.all_to_all(chip_sum.reshape(n_seq // 2, n_dp, *piece), 'seq', 0, 0, a...]
    ppermute x12, waiting for transfers between devices: 24.1 us -> 35.8 us  [over_seq(): lax.ppermute(value, 'seq', [(i, j) for i, j in pairs if 0 <= j < n_seq])]
    ppermute x12, starting transfers between devices: 26.7 us -> 22.5 us  [over_seq(): lax.ppermute(value, 'seq', [(i, j) for i, j in pairs if 0 <= j < n_seq])]
    all_to_all x1, starting transfers between devices: 7.5 us -> 4.66 us  [body(): lax.all_to_all(chip_sum.reshape(n_seq // 2, n_dp, *piece), 'seq', 0, 0, a...]
  transfers between devices with their start and end apart: 19 -> 19, of which waited for: 8 -> 9; matrix products, arithmetic and copies ran while one was open for 7% -> 7% of each run, Pallas kernels for 43% -> 39%
where the time goes in v5:
time: 207 us; the launch traced here: 206 us
  Pallas kernels  95.8 us (46%)
  waiting for transfers between devices  50.2 us (24%)
  starting transfers between devices  41.2 us (20%)
  other arithmetic  8.64 us (4%)
  matrix products  5.76 us (3%)
  local copies, waits for them, and re-layouts  3.3 us (2%)
    pallas_call x3, Pallas kernels, attend(): pl.pallas_call(functools.partial(attend_kernel, len(slabs)), grid_spec=pl...  57.4 us
    ppermute x12, waiting for transfers between devices, over_seq(): lax.ppermute(value, 'seq', [(i, j) for i, j in pairs if 0 <= j < n_seq])  35.8 us
    ppermute x12, starting transfers between devices, over_seq(): lax.ppermute(value, 'seq', [(i, j) for i, j in pairs if 0 <= j < n_seq])  22.5 us
    pallas_call x3, Pallas kernels, product(): pl.pallas_call(product_kernel, grid_spec=pltpu.PrefetchScalarGridSpec(num...  20.1 us
    ppermute x4, waiting for transfers between devices, over_dp(): return lax.ppermute(value, 'dp', [(i, target(i)) for i in range(n_dp)])  14.4 us
    pallas_call x2, Pallas kernels, combine(): pl.pallas_call(functools.partial(combine_kernel, edges), grid_spec=pltpu....  10.4 us
    all_to_all x1, starting transfers between devices, body(): lax.all_to_all(jnp.broadcast_to(total, (n_seq, *piece)), 'seq', 0, 0)  6.06 us
    dot_general x1, matrix products, dot(): return lax.dot_general(a, b, dims, preferred_element_type=F32)  5.76 us
  transfers between devices with their start and end apart: 19, of which 9 were waited for; matrix products, arithmetic and copies ran while one was open for 7% of the time, Pallas kernels for 39%

profile of v5, /device:TPU:7, one launch (start us, length us, event | category | flops | bytes accessed | tf_op | source)
XLA Modules:
  0.0 205.8 jit_solution(5311547743419083838)
XLA Ops:
  0.7 1.2 copy-done
  2.0 5.3 %shard_map.111 = (bf16[2,384,1536]{2,1,0:T(8,128)(2,1)}, bf16[2,384,1536]{2,1,0:T(8,128)(2,1)}) custom-call(bf16[768,1536]{1,0:T(8,128)(2,1)} %bitcast.36, bf16[768,1536]{1,0:T(8,128)(2,1)} %bitcast.37, bf16[768,1536]{1,0:T(8,128)(2,1)} %bitcast.41, bf16[768,1536]{1,0:T(8,128)(2,1)} %bitcast.42), custom_call_target="tpu_custom_call" | custom-call | tf_op jit(solution)/shard_map/pallas_call | solution.py:273
  7.3 1.6 collective-permute-start.1
  8.9 5.6 %shard_map.112 = bf16[2,2,8,96,384]{4,3,2,1,0:T(8,128)(2,1)} custom-call(s32[1]{0:T(128)} %bitcast.3.which, bf16[768,1536]{1,0:T(8,128)(2,1)} %bitcast.30, bf16[768,3072]{1,0:T(8,128)(2,1)} %bitcast.23), custom_call_target="tpu_custom_call" | custom-call | flops 56623104 | bytes 400000 | tf_op jit(solution)/shard_map/pallas_call | solution.py:216
  14.6 1.0 collective-permute-start
  15.5 5.0 %collective-permute-start.3 = (bf16[2,384,1536]{2,1,0:T(8,128)(2,1)}, bf16[2,384,1536]{2,1,0:T(8,128)(2,1)}, u32[]{:S(2)}, u32[]{:S(2)}) collective-permute-start(bf16[2,384,1536]{2,1,0:T(8,128)(2,1)} %get-tuple-element.57), channel_id=1, source_target_pairs={{0,1},{1,2},{2,3},{3,4},{4,5},{5,6},{6,7},{7,8},{8,9},{9,10},{10,1... | collective-permute-start | bytes 7077896 | tf_op jit(solution)/shard_map/ppermute | solution.py:305
  20.5 1.9 collective-permute-start.4
  22.5 5.9 %shard_map.113 = bf16[2,2,8,96,384]{4,3,2,1,0:T(8,128)(2,1)} custom-call(s32[1]{0:T(128)} %bitcast.6.which, bf16[768,1536]{1,0:T(8,128)(2,1)} %bitcast.31, bf16[768,3072]{1,0:T(8,128)(2,1)} %bitcast.24), custom_call_target="tpu_custom_call" | custom-call | flops 56623104 | bytes 400000 | tf_op jit(solution)/shard_map/pallas_call | solution.py:216
  28.4 0.7 collective-permute-start.2
  29.1 1.1 broadcast_select_fusion.3
  30.2 1.1 pad_maximum_fusion
  31.3 3.8 %collective-permute-done.5 = bf16[384,1536]{1,0:T(8,128)(2,1)S(1)} collective-permute-done((bf16[384,1536]{1,0:T(8,128)(2,1)}, bf16[384,1536]{1,0:T(8,128)(2,1)S(1)}, u32[]{:S(2)}, u32[]{:S(2)}) %collective-permute-start.5) | collective-permute-done | bytes 1179680 | tf_op jit(solution)/shard_map/ppermute | solution.py:305
  35.1 0.4 broadcast_select_fusion.1
  35.5 5.8 %fusion.7.refs_10_ = bf16[768,384]{1,0:T(8,128)(2,1)} fusion(bf16[384,1536]{1,0:T(8,128)(2,1)S(1)} %get-tuple-element.101, bf16[384,1536]{1,0:T(8,128)(2,1)S(1)} %get-tuple-element.100, bf16[1,768,3072]{2,1,0:T(8,128)(2,1)} %param.13), kind=kOutput, calls=%fused_computation.5 | convolution fusion | flops 1816952832 | bytes 7667712 | tf_op jit(solution)/shard_map/dot_general | solution.py:23
  41.3 5.3 %collective-permute-done.3.refs_2_.refs_5_ = bf16[2,384,1536]{2,1,0:T(8,128)(2,1)} collective-permute-done((bf16[2,384,1536]{2,1,0:T(8,128)(2,1)}, bf16[2,384,1536]{2,1,0:T(8,128)(2,1)}, u32[]{:S(2)}, u32[]{:S(2)}) %collective-permute-start.3) | collective-permute-done | bytes 2359328 | tf_op jit(solution)/shard_map/ppermute | solution.py:305
  46.6 8.0 %collective-permute-done.4.refs_4_.refs_7_ = bf16[2,384,1536]{2,1,0:T(8,128)(2,1)} collective-permute-done((bf16[2,384,1536]{2,1,0:T(8,128)(2,1)}, bf16[2,384,1536]{2,1,0:T(8,128)(2,1)}, u32[]{:S(2)}, u32[]{:S(2)}) %collective-permute-start.4) | collective-permute-done | bytes 2359328 | tf_op jit(solution)/shard_map/ppermute | solution.py:305
  54.6 8.6 %shard_map.114 = bf16[2,4,8,96,384]{4,3,2,1,0:T(8,128)(2,1)} custom-call(s32[1]{0:T(128)} %bitcast.which, bf16[768,1536]{1,0:T(8,128)(2,1)} %bitcast.32, bf16[768,3072]{1,0:T(8,128)(2,1)} %bitcast.25, bf16[2,2,8,96,384]{4,3,2,1,0:T(8,128)(2,1)} %collective-permute-done.refs_0_, bf16[2,2,8,96,384]{4,3,2,1,0:T(8,128)(2,1)} %collective-permute-done.2.refs_1_), custom_call_target="tpu_custom_call" | custom-call | flops 113246208 | bytes 400000 | tf_op jit(solution)/shard_map/pallas_call | solution.py:216
  63.3 4.7 %all-to-all-start = ((bf16[8,8,96,384]{3,2,1,0:T(8,128)(2,1)}), bf16[8,8,96,384]{3,2,1,0:T(8,128)(2,1)}, u32[]{:S(2)}, u32[]{:S(2)}) async-start(bf16[8,8,96,384]{3,2,1,0:T(8,128)(2,1)} %bitcast.49), calls=%async_computation | async-start | bytes 9437184 | tf_op jit(solution)/shard_map/all_to_all | solution.py:349
  67.9 2.8 %collective-permute-start.7 = (bf16[384,1536]{1,0:T(8,128)(2,1)}, bf16[384,1536]{1,0:T(8,128)(2,1)}, u32[]{:S(2)}, u32[]{:S(2)}) collective-permute-start(bf16[384,1536]{1,0:T(8,128)(2,1)} %pad_maximum_fusion), channel_id=1, source_target_pairs={{0,96},{16,112},{32,0},{48,16},{64,32},{80,48},{96,64},{112,80},{1... | collective-permute-start | bytes 3538952 | tf_op jit(solution)/shard_map/ppermute | solution.py:301
  70.8 0.1 copy.26
  70.9 0.1 sub.28
  71.0 0.6 copy.28
  71.6 0.6 pad_add_fusion.3
  72.3 11.8 %shard_map.115 = (bf16[768,1536]{1,0:T(8,128)(2,1)}, f32[768,1152]{1,0:T(8,128)}, f32[768,1152]{1,0:T(8,128)}, bf16[2,384,1152]{2,1,0:T(8,128)(2,1)}, bf16[2,384,1152]{2,1,0:T(8,128)(2,1)}) custom-call(s32[10]{0:T(128)} %get-tuple-element.105.refs_0_, bf16[768,1536]{1,0:T(8,128)(2,1)} %bitcast.46, ...), custom_call_target="tpu_custom_call" | custom-call | flops 3397386240 | bytes 6000000 | tf_op jit(solution)/shard_map/pallas_call | solution.py:124
  84.1 10.7 %collective-permute-done.7.refs_14_ = bf16[384,1536]{1,0:T(8,128)(2,1)} collective-permute-done((bf16[384,1536]{1,0:T(8,128)(2,1)}, bf16[384,1536]{1,0:T(8,128)(2,1)}, u32[]{:S(2)}, u32[]{:S(2)}) %collective-permute-start.7) | collective-permute-done | bytes 1179680 | tf_op jit(solution)/shard_map/ppermute | solution.py:301
  94.8 3.7 %collective-permute-done.6.refs_12_ = bf16[384,1536]{1,0:T(8,128)(2,1)S(1)} collective-permute-done((bf16[384,1536]{1,0:T(8,128)(2,1)}, bf16[384,1536]{1,0:T(8,128)(2,1)S(1)}, u32[]{:S(2)}, u32[]{:S(2)}) %collective-permute-start.6) | collective-permute-done | bytes 1179680 | tf_op jit(solution)/shard_map/ppermute | solution.py:301
  98.5 0.5 collective-permute-start.9
  99.0 0.7 pad_add_fusion.2.refs_0_
  99.7 3.6 %collective-permute-done.10.refs_15_ = bf16[384,1536]{1,0:T(8,128)(2,1)} collective-permute-done((bf16[384,1536]{1,0:T(8,128)(2,1)}, bf16[384,1536]{1,0:T(8,128)(2,1)}, u32[]{:S(2)}, u32[]{:S(2)}) %collective-permute-start.10) | collective-permute-done | bytes 1179680 | tf_op jit(solution)/shard_map/ppermute | solution.py:305
  103.3 28.9 %shard_map.116 = (bf16[768,1536]{1,0:T(8,128)(2,1)}, f32[768,1152]{1,0:T(8,128)}, f32[768,1152]{1,0:T(8,128)}, bf16[2,384,1152]{2,1,0:T(8,128)(2,1)}, bf16[2,384,1152]{2,1,0:T(8,128)(2,1)}) custom-call(s32[13]{0:T(128)} %pad_add_fusion.2.refs_0_, ...), custom_call_target="tpu_custom_call", output_to_operand_aliasing={{0}: (16, {}), {1}: (17, {}), {2}: (18, {}), {3}: (19, {}),... | custom-call | flops 10418651136 | bytes 12000000 | tf_op jit(solution)/shard_map/pallas_call | solution.py:124
  132.2 4.6 %collective-permute-start.12 = (bf16[2,384,1152]{2,1,0:T(8,128)(2,1)}, bf16[2,384,1152]{2,1,0:T(8,128)(2,1)}, u32[]{:S(2)}, u32[]{:S(2)}) collective-permute-start(bf16[2,384,1152]{2,1,0:T(8,128)(2,1)} %get-tuple-element.84), channel_id=1, source_target_pairs={{0,1},{1,2},{2,3},{3,4},{4,5},{5,6},{6,7},{7,8},{8,9},{9,10},{10,1... | collective-permute-start | bytes 5308424 | tf_op jit(solution)/shard_map/ppermute | solution.py:305
  136.9 1.9 collective-permute-start.13
  138.8 0.1 collective-permute-start.11
  138.9 4.0 %reduce_sum.24 = bf16[8,96,384]{2,1,0:T(8,128)(2,1)} reduce(bf16[8,8,96,384]{3,2,1,0:T(8,128)(2,1)} %all-to-all-done, bf16[]{:T(256)} %constant.81.clone.1), dimensions={0}, to_apply=%region_0.1 | reduce | flops 2064384 | bytes 5308418 | tf_op jit(solution)/shard_map/reduce_sum | solution.py:381
  142.9 3.5 %all-to-all-start.1 = ((bf16[8,96,384]{2,1,0:T(8,128)(2,1)}), bf16[8,96,384]{2,1,0:T(8,128)(2,1)S(1)}, u32[]{:S(2)}, u32[]{:S(2)}) async-start(bf16[8,96,384]{2,1,0:T(8,128)(2,1)} %reduce_sum.24), calls=%async_computation.1 | async-start | bytes 1179648 | tf_op jit(solution)/shard_map/all_to_all | solution.py:385
  146.4 16.7 %shard_map.117 = (bf16[768,1536]{1,0:T(8,128)(2,1)}, f32[768,384]{1,0:T(8,128)}, f32[768,384]{1,0:T(8,128)}, bf16[2,384,384]{2,1,0:T(8,128)(2,1)}, bf16[2,384,384]{2,1,0:T(8,128)(2,1)}) custom-call(s32[10]{0:T(128)} %get-tuple-element.104.refs_0_, bf16[768,1536]{1,0:T(8,128)(2,1)} %bitcast.48, ...), custom_call_target="tpu_custom_call", output_to_operand_aliasing={{0}: (14, {})} | custom-call | flops 5209325568 | bytes 6000000 | tf_op jit(solution)/shard_map/pallas_call | solution.py:124
  163.2 6.3 %collective-permute-done.13.refs_3_ = bf16[2,384,1152]{2,1,0:T(8,128)(2,1)} collective-permute-done((bf16[2,384,1152]{2,1,0:T(8,128)(2,1)}, bf16[2,384,1152]{2,1,0:T(8,128)(2,1)}, u32[]{:S(2)}, u32[]{:S(2)}) %collective-permute-start.13) | collective-permute-done | bytes 1769504 | tf_op jit(solution)/shard_map/ppermute | solution.py:305
  169.5 0.1 reduce_sum.25
  169.6 1.1 broadcast_in_dim.30
  170.7 6.1 %all-to-all-start.2 = ((bf16[16,96,384]{2,1,0:T(8,128)(2,1)}), bf16[16,96,384]{2,1,0:T(8,128)(2,1)}, u32[]{:S(2)}, u32[]{:S(2)}) async-start(bf16[16,96,384]{2,1,0:T(8,128)(2,1)} %broadcast_in_dim.30), calls=%async_computation.2 | async-start | bytes 2359296 | tf_op jit(solution)/shard_map/all_to_all | solution.py:389
  176.7 4.8 %collective-permute-start.14 = (bf16[2,384,384]{2,1,0:T(8,128)(2,1)}, bf16[2,384,384]{2,1,0:T(8,128)(2,1)S(1)}, u32[]{:S(2)}, u32[]{:S(2)}) collective-permute-start(bf16[2,384,384]{2,1,0:T(8,128)(2,1)} %get-tuple-element.89), channel_id=1, source_target_pairs={{0,1},{1,2},{2,3},{3,4},{4,5},{5,6},{6,7},{7,8},{8,9},{9,10},{10,1... | collective-permute-start | bytes 1769480 | tf_op jit(solution)/shard_map/ppermute | solution.py:305
  181.6 1.9 collective-permute-start.15
  183.5 0.6 pad_add_fusion.4.meta
  184.1 7.2 %shard_map.118 = (bf16[768,1536]{1,0:T(8,128)(2,1)}, bf16[768,1536]{1,0:T(8,128)(2,1)}) custom-call(s32[3]{0:T(128)} %pad_add_fusion.4.meta, f32[768,1152]{1,0:T(8,128)} %get-tuple-element.91.refs_0_, f32[768,1152]{1,0:T(8,128)} %get-tuple-element.92.refs_1_, bf16[2,384,1152]{2,1,0:T(8,128)(2,1)} %collective-permute-done.12.refs_2_, ...), custom_call_target="tpu_custom_call" | custom-call | flops 4000000 | bytes 20000000 | tf_op jit(solution)/shard_map/pallas_call | solution.py:174
  191.3 5.2 %collective-permute-done.14.refs_2_ = bf16[2,384,384]{2,1,0:T(8,128)(2,1)S(1)} collective-permute-done((bf16[2,384,384]{2,1,0:T(8,128)(2,1)}, bf16[2,384,384]{2,1,0:T(8,128)(2,1)S(1)}, u32[]{:S(2)}, u32[]{:S(2)}) %collective-permute-start.14) | collective-permute-done | bytes 589856 | tf_op jit(solution)/shard_map/ppermute | solution.py:305
  196.5 3.5 %collective-permute-done.15.refs_3_ = bf16[2,384,384]{2,1,0:T(8,128)(2,1)} collective-permute-done((bf16[2,384,384]{2,1,0:T(8,128)(2,1)}, bf16[2,384,384]{2,1,0:T(8,128)(2,1)}, u32[]{:S(2)}, u32[]{:S(2)}) %collective-permute-start.15) | collective-permute-done | bytes 589856 | tf_op jit(solution)/shard_map/ppermute | solution.py:305
  200.0 3.2 %shard_map.119 = (bf16[768,1536]{1,0:T(8,128)(2,1)}, bf16[768,1536]{1,0:T(8,128)(2,1)}) custom-call(s32[1]{0:T(128)} %bitcast.11.meta, f32[768,384]{1,0:T(8,128)} %get-tuple-element.87.refs_0_, f32[768,384]{1,0:T(8,128)} %get-tuple-element.88.refs_1_, bf16[2,384,384]{2,1,0:T(8,128)(2,1)} %copy-done.3, ...), custom_call_target="tpu_custom_call", output_to_operand_aliasing={{0}: (5, {}), {1}: (6, {})} | custom-call | flops 4000000 | bytes 20000000 | tf_op jit(solution)/shard_map/pallas_call | solution.py:174
  203.2 2.5 %shard_map.120 = f32[192,3072]{1,0:T(8,128)} custom-call(bf16[16,96,384]{2,1,0:T(8,128)(2,1)} %all-to-all-done.2.pieces), custom_call_target="tpu_custom_call" | custom-call | tf_op jit(solution)/shard_map/pallas_call | solution.py:248
  (32 shorter events, 0.2 us)
Async XLA Ops:
  0.6 1.3 copy-start
  7.3 15.2 %collective-permute-start.1 = (bf16[192,1536]{1,0:T(8,128)(2,1)S(1)}, bf16[192,1536]{1,0:T(8,128)(2,1)S(1)}, u32[]{:S(2)}, u32[]{:S(2)}) collective-permute-start(bf16[192,1536]{1,0:T(8,128)(2,1)S(1)} %constant_dynamic-slice_fusion.1), channel_id=1, source_target_pairs={{0,16},{16,0},{32,48},{48,32},{64,80},{80,64},{96,112},{112,96},{1... | collective-permute-start | bytes 1769480 | tf_op jit(solution)/shard_map/ppermute | solution.py:301
  14.6 26.7 %collective-permute-start = (bf16[2,2,8,96,384]{4,3,2,1,0:T(8,128)(2,1)}, bf16[2,2,8,96,384]{4,3,2,1,0:T(8,128)(2,1)}, u32[]{:S(2)}, u32[]{:S(2)}) collective-permute-start(bf16[2,2,8,96,384]{4,3,2,1,0:T(8,128)(2,1)} %shard_map.112), channel_id=1, source_target_pairs={{0,1},{1,0},{2,3},{3,2},{4,5},{5,4},{6,7},{7,6},{8,9},{9,8},{10,11... | collective-permute-start | bytes 7077896 | tf_op jit(solution)/shard_map/ppermute | solution.py:305
  15.5 31.1 %collective-permute-start.3 = (bf16[2,384,1536]{2,1,0:T(8,128)(2,1)}, bf16[2,384,1536]{2,1,0:T(8,128)(2,1)}, u32[]{:S(2)}, u32[]{:S(2)}) collective-permute-start(bf16[2,384,1536]{2,1,0:T(8,128)(2,1)} %get-tuple-element.57), channel_id=1, source_target_pairs={{0,1},{1,2},{2,3},{3,4},{4,5},{5,6},{6,7},{7,8},{8,9},{9,10},{10,1... | collective-permute-start | bytes 7077896 | tf_op jit(solution)/shard_map/ppermute | solution.py:305
  20.5 34.1 %collective-permute-start.4 = (bf16[2,384,1536]{2,1,0:T(8,128)(2,1)}, bf16[2,384,1536]{2,1,0:T(8,128)(2,1)}, u32[]{:S(2)}, u32[]{:S(2)}) collective-permute-start(bf16[2,384,1536]{2,1,0:T(8,128)(2,1)} %get-tuple-element.58), channel_id=1, source_target_pairs={{1,0},{2,1},{3,2},{4,3},{5,4},{6,5},{7,6},{8,7},{9,8},{10,9},{11,1... | collective-permute-start | bytes 7077896 | tf_op jit(solution)/shard_map/ppermute | solution.py:305
  22.5 5.9 %copy-start.4 = (bf16[192,1536]{1,0:T(8,128)(2,1)}, bf16[192,1536]{1,0:T(8,128)(2,1)S(1)}, u32[]{:S(2)}) copy-start(bf16[192,1536]{1,0:T(8,128)(2,1)S(1)} %collective-permute-done.1) | copy-start | bytes 1769476
  28.4 26.3 %collective-permute-start.2 = (bf16[2,2,8,96,384]{4,3,2,1,0:T(8,128)(2,1)}, bf16[2,2,8,96,384]{4,3,2,1,0:T(8,128)(2,1)}, u32[]{:S(2)}, u32[]{:S(2)}) collective-permute-start(bf16[2,2,8,96,384]{4,3,2,1,0:T(8,128)(2,1)} %shard_map.113), channel_id=1, source_target_pairs={{0,1},{1,0},{2,3},{3,2},{4,5},{5,4},{6,7},{7,6},{8,9},{9,8},{10,11... | collective-permute-start | bytes 7077896 | tf_op jit(solution)/shard_map/ppermute | solution.py:305
  31.3 3.8 %collective-permute-start.5 = (bf16[384,1536]{1,0:T(8,128)(2,1)}, bf16[384,1536]{1,0:T(8,128)(2,1)S(1)}, u32[]{:S(2)}, u32[]{:S(2)}) collective-permute-start(bf16[384,1536]{1,0:T(8,128)(2,1)} %pad_maximum_fusion), channel_id=1, source_target_pairs={{0,1},{1,0},{2,3},{3,2},{4,5},{5,4},{6,7},{7,6},{8,9},{9,8},{10,11... | collective-permute-start | bytes 3538952 | tf_op jit(solution)/shard_map/ppermute | solution.py:305
  63.3 7.5 %copy-start.6 = (s32[1,32,3]{1,0,2:T(1,128)S(1)}, s32[1,32,3]{1,0,2:T(1,128)}, u32[]{:S(2)}) copy-start(s32[1,32,3]{1,0,2:T(1,128)} %param.15) | copy-start | bytes 1156
  63.3 7.7 %copy-start.5 = (f32[1,12,768]{2,0,1:T(1,128)S(1)}, f32[1,12,768]{2,0,1:T(1,128)}, u32[]{:S(2)}) copy-start(f32[1,12,768]{2,0,1:T(1,128)} %param.12) | copy-start | bytes 110596
  63.3 75.5 %all-to-all-start = ((bf16[8,8,96,384]{3,2,1,0:T(8,128)(2,1)}), bf16[8,8,96,384]{3,2,1,0:T(8,128)(2,1)}, u32[]{:S(2)}, u32[]{:S(2)}) async-start(bf16[8,8,96,384]{3,2,1,0:T(8,128)(2,1)} %bitcast.49), calls=%async_computation | async-start | bytes 9437184 | tf_op jit(solution)/shard_map/all_to_all | solution.py:349
  67.9 26.8 %collective-permute-start.7 = (bf16[384,1536]{1,0:T(8,128)(2,1)}, bf16[384,1536]{1,0:T(8,128)(2,1)}, u32[]{:S(2)}, u32[]{:S(2)}) collective-permute-start(bf16[384,1536]{1,0:T(8,128)(2,1)} %pad_maximum_fusion), channel_id=1, source_target_pairs={{0,96},{16,112},{32,0},{48,16},{64,32},{80,48},{96,64},{112,80},{1... | collective-permute-start | bytes 3538952 | tf_op jit(solution)/shard_map/ppermute | solution.py:301
  70.8 27.7 %collective-permute-start.6 = (bf16[384,1536]{1,0:T(8,128)(2,1)}, bf16[384,1536]{1,0:T(8,128)(2,1)S(1)}, u32[]{:S(2)}, u32[]{:S(2)}) collective-permute-start(bf16[384,1536]{1,0:T(8,128)(2,1)} %pad_maximum_fusion), channel_id=1, source_target_pairs={{0,32},{16,48},{32,64},{48,80},{64,96},{80,112},{96,0},{112,16},{1... | collective-permute-start | bytes 3538952 | tf_op jit(solution)/shard_map/ppermute | solution.py:301
  98.5 4.8 %copy-start.2 = (bf16[384,1536]{1,0:T(8,128)(2,1)}, bf16[384,1536]{1,0:T(8,128)(2,1)S(1)}, u32[]{:S(2)}) copy-start(bf16[384,1536]{1,0:T(8,128)(2,1)S(1)} %collective-permute-done.6.refs_12_) | copy-start | bytes 3538948
  98.5 4.8 %collective-permute-start.10 = (bf16[384,1536]{1,0:T(8,128)(2,1)}, bf16[384,1536]{1,0:T(8,128)(2,1)}, u32[]{:S(2)}, u32[]{:S(2)}) collective-permute-start(bf16[384,1536]{1,0:T(8,128)(2,1)} %collective-permute-done.7.refs_14_), channel_id=1, source_target_pairs={{0,1},{1,0},{2,3},{3,2},{4,5},{5,4},{6,7},{7,6},{8,9},{9,8},{10,11... | collective-permute-start | bytes 3538952 | tf_op jit(solution)/shard_map/ppermute | solution.py:305
  98.5 4.8 %collective-permute-start.9 = (bf16[384,1536]{1,0:T(8,128)(2,1)S(1)}, bf16[384,1536]{1,0:T(8,128)(2,1)}, u32[]{:S(2)}, u32[]{:S(2)}) collective-permute-start(bf16[384,1536]{1,0:T(8,128)(2,1)S(1)} %collective-permute-done.6.refs_12_), channel_id=1, source_target_pairs={{0,1},{1,0},{2,3},{3,2},{4,5},{5,4},{6,7},{7,6},{8,9},{9,8},{10,11... | collective-permute-start | bytes 3538952 | tf_op jit(solution)/shard_map/ppermute | solution.py:305
  99.0 39.8 %collective-permute-start.8 = (bf16[384,1536]{1,0:T(8,128)(2,1)S(1)}, bf16[384,1536]{1,0:T(8,128)(2,1)}, u32[]{:S(2)}, u32[]{:S(2)}) collective-permute-start(bf16[384,1536]{1,0:T(8,128)(2,1)S(1)} %collective-permute-done.6.refs_12_), channel_id=1, source_target_pairs={{0,32},{16,48},{32,64},{48,80},{64,96},{80,112},{96,0},{112,16},{1... | collective-permute-start | bytes 3538952 | tf_op jit(solution)/shard_map/ppermute | solution.py:301
  132.2 30.9 %collective-permute-start.12 = (bf16[2,384,1152]{2,1,0:T(8,128)(2,1)}, bf16[2,384,1152]{2,1,0:T(8,128)(2,1)}, u32[]{:S(2)}, u32[]{:S(2)}) collective-permute-start(bf16[2,384,1152]{2,1,0:T(8,128)(2,1)} %get-tuple-element.84), channel_id=1, source_target_pairs={{0,1},{1,2},{2,3},{3,4},{4,5},{5,6},{6,7},{7,8},{8,9},{9,10},{10,1... | collective-permute-start | bytes 5308424 | tf_op jit(solution)/shard_map/ppermute | solution.py:305
  136.9 32.6 %collective-permute-start.13 = (bf16[2,384,1152]{2,1,0:T(8,128)(2,1)}, bf16[2,384,1152]{2,1,0:T(8,128)(2,1)}, u32[]{:S(2)}, u32[]{:S(2)}) collective-permute-start(bf16[2,384,1152]{2,1,0:T(8,128)(2,1)} %get-tuple-element.85), channel_id=1, source_target_pairs={{1,0},{2,1},{3,2},{4,3},{5,4},{6,5},{7,6},{8,7},{9,8},{10,9},{11,1... | collective-permute-start | bytes 5308424 | tf_op jit(solution)/shard_map/ppermute | solution.py:305
  138.8 7.6 %collective-permute-start.11 = (bf16[384,1536]{1,0:T(8,128)(2,1)}, bf16[384,1536]{1,0:T(8,128)(2,1)}, u32[]{:S(2)}, u32[]{:S(2)}) collective-permute-start(bf16[384,1536]{1,0:T(8,128)(2,1)} %collective-permute-done.8.refs_12_), channel_id=1, source_target_pairs={{0,1},{1,0},{2,3},{3,2},{4,5},{5,4},{6,7},{7,6},{8,9},{9,8},{10,11... | collective-permute-start | bytes 3538952 | tf_op jit(solution)/shard_map/ppermute | solution.py:305
  142.9 26.6 %all-to-all-start.1 = ((bf16[8,96,384]{2,1,0:T(8,128)(2,1)}), bf16[8,96,384]{2,1,0:T(8,128)(2,1)S(1)}, u32[]{:S(2)}, u32[]{:S(2)}) async-start(bf16[8,96,384]{2,1,0:T(8,128)(2,1)} %reduce_sum.24), calls=%async_computation.1 | async-start | bytes 1179648 | tf_op jit(solution)/shard_map/all_to_all | solution.py:385
  170.7 32.5 %all-to-all-start.2 = ((bf16[16,96,384]{2,1,0:T(8,128)(2,1)}), bf16[16,96,384]{2,1,0:T(8,128)(2,1)}, u32[]{:S(2)}, u32[]{:S(2)}) async-start(bf16[16,96,384]{2,1,0:T(8,128)(2,1)} %broadcast_in_dim.30), calls=%async_computation.2 | async-start | bytes 2359296 | tf_op jit(solution)/shard_map/all_to_all | solution.py:389
  176.7 19.8 %collective-permute-start.14 = (bf16[2,384,384]{2,1,0:T(8,128)(2,1)}, bf16[2,384,384]{2,1,0:T(8,128)(2,1)S(1)}, u32[]{:S(2)}, u32[]{:S(2)}) collective-permute-start(bf16[2,384,384]{2,1,0:T(8,128)(2,1)} %get-tuple-element.89), channel_id=1, source_target_pairs={{0,1},{1,2},{2,3},{3,4},{4,5},{5,6},{6,7},{7,8},{8,9},{9,10},{10,1... | collective-permute-start | bytes 1769480 | tf_op jit(solution)/shard_map/ppermute | solution.py:305
  181.6 18.4 %collective-permute-start.15 = (bf16[2,384,384]{2,1,0:T(8,128)(2,1)}, bf16[2,384,384]{2,1,0:T(8,128)(2,1)}, u32[]{:S(2)}, u32[]{:S(2)}) collective-permute-start(bf16[2,384,384]{2,1,0:T(8,128)(2,1)} %get-tuple-element.90), channel_id=1, source_target_pairs={{1,0},{2,1},{3,2},{4,3},{5,4},{6,5},{7,6},{8,7},{9,8},{10,9},{11,1... | collective-permute-start | bytes 1769480 | tf_op jit(solution)/shard_map/ppermute | solution.py:305
  196.5 3.5 %copy-start.3 = (bf16[2,384,384]{2,1,0:T(8,128)(2,1)}, bf16[2,384,384]{2,1,0:T(8,128)(2,1)S(1)}, u32[]{:S(2)}) copy-start(bf16[2,384,384]{2,1,0:T(8,128)(2,1)S(1)} %collective-permute-done.14.refs_2_) | copy-start | bytes 1769476
  200.0 5.8 %copy-start.1 = (bf16[192,3072]{1,0:T(8,128)(2,1)S(1)}, bf16[192,3072]{1,0:T(8,128)(2,1)}, u32[]{:S(2)}) copy-start(bf16[192,3072]{1,0:T(8,128)(2,1)} %param.14) | copy-start | bytes 3538948

commit v6 on v4

--- a/solution.py
+++ b/solution.py
@@ -375,15 +375,16 @@
         begun,
     )
     dq, dko, dvo, low, high = most
-    spread, far, dq = lax.optimization_barrier((spread, far, dq))
+    far, dq = lax.optimization_barrier((far, dq))
     rims = rims_of(low, high)
-    clip_sum = spread.astype(F32).sum(0).astype(BF16)
     dq, *rest = attend_group([y + 2], None, [(far, swap(far))], three, 0, [dq])
     pending = [[dko, dvo, *rims], [*rest[:2], *rims_of(*rest[2:])]]
+    spread, dq = lax.optimization_barrier((spread, dq))
+    clip_sum = spread.astype(F32).sum(0).astype(BF16)
 
     met = lax.all_to_all(clip_sum, "dp", 0, 0)
-    met, dq, *rims = lax.optimization_barrier((met, dq, *pending[0][2:]))
-    pending[0][2:] = rims
+    met, *rims = lax.optimization_barrier((met, *pending[0][2:], *pending[1][2:]))
+    pending[0][2:], pending[1][2:] = rims[:2], rims[2:]
     total = met.astype(F32).sum(0).astype(BF16)
     ready = lax.all_to_all(jnp.broadcast_to(total, (n_seq, *piece)), "seq", 0, 0)
     weight_grad = lay_out(ready, n_z)

time: 205 us -> 205 us (level); the launches traced: 204 us -> 201 us
  waiting for transfers between devices: 37.8 us -> 32.7 us
    all_to_all x1, waiting for transfers between devices: 13 us -> 0.01 us  [body(): lax.all_to_all(chip_sum.reshape(n_seq // 2, n_dp, *piece), 'seq', 0, 0, a...]
    all_to_all x1, waiting for transfers between devices: 0.01 us -> 5.87 us  [body(): lax.all_to_all(jnp.broadcast_to(total, (n_seq, *piece)), 'seq', 0, 0)]
  transfers between devices with their start and end apart: 19 -> 19, of which waited for: 8 -> 6; matrix products, arithmetic and copies ran while one was open for 7% -> 8% of each run, Pallas kernels for 43% -> 44%
where the time goes in v6:
time: 205 us; the launch traced here: 201 us
  Pallas kernels  95.8 us (47%)
  starting transfers between devices  51.8 us (25%)
  waiting for transfers between devices  32.7 us (16%)
  other arithmetic  8.62 us (4%)
  matrix products  5.77 us (3%)
  local copies, waits for them, and re-layouts  5.32 us (3%)
    pallas_call x3, Pallas kernels, attend(): pl.pallas_call(functools.partial(attend_kernel, len(slabs)), grid_spec=pl...  57.4 us
    ppermute x12, starting transfers between devices, over_seq(): lax.ppermute(value, 'seq', [(i, j) for i, j in pairs if 0 <= j < n_seq])  27 us
    ppermute x12, waiting for transfers between devices, over_seq(): lax.ppermute(value, 'seq', [(i, j) for i, j in pairs if 0 <= j < n_seq])  26.2 us
    pallas_call x3, Pallas kernels, product(): pl.pallas_call(product_kernel, grid_spec=pltpu.PrefetchScalarGridSpec(num...  20.1 us
    pallas_call x2, Pallas kernels, combine(): pl.pallas_call(functools.partial(combine_kernel, edges), grid_spec=pltpu....  10.4 us
    all_to_all x1, starting transfers between devices, body(): lax.all_to_all(chip_sum.reshape(n_seq // 2, n_dp, *piece), 'seq', 0, 0, a...  7.5 us
    all_to_all x1, starting transfers between devices, body(): lax.all_to_all(jnp.broadcast_to(total, (n_seq, *piece)), 'seq', 0, 0)  7.36 us
    all_to_all x1, waiting for transfers between devices, body(): lax.all_to_all(jnp.broadcast_to(total, (n_seq, *piece)), 'seq', 0, 0)  5.87 us
  transfers between devices with their start and end apart: 19, of which 6 were waited for; matrix products, arithmetic and copies ran while one was open for 8% of the time, Pallas kernels for 44%

profile of v6, /device:TPU:7, one launch (start us, length us, event | category | flops | bytes accessed | tf_op | source)
XLA Modules:
  0.0 200.9 jit_solution(7218651320034746386)
XLA Ops:
  0.7 1.2 copy-done
  2.0 5.3 %shard_map.111 = (bf16[2,384,1536]{2,1,0:T(8,128)(2,1)}, bf16[2,384,1536]{2,1,0:T(8,128)(2,1)}) custom-call(bf16[768,1536]{1,0:T(8,128)(2,1)} %bitcast.36, bf16[768,1536]{1,0:T(8,128)(2,1)} %bitcast.37, bf16[768,1536]{1,0:T(8,128)(2,1)} %bitcast.41, bf16[768,1536]{1,0:T(8,128)(2,1)} %bitcast.42), custom_call_target="tpu_custom_call" | custom-call | tf_op jit(solution)/shard_map/pallas_call | solution.py:273
  7.3 1.6 collective-permute-start.1
  8.9 5.6 %shard_map.112 = bf16[2,2,8,96,384]{4,3,2,1,0:T(8,128)(2,1)} custom-call(s32[1]{0:T(128)} %bitcast.3.which, bf16[768,1536]{1,0:T(8,128)(2,1)} %bitcast.30, bf16[768,3072]{1,0:T(8,128)(2,1)} %bitcast.23), custom_call_target="tpu_custom_call" | custom-call | flops 56623104 | bytes 400000 | tf_op jit(solution)/shard_map/pallas_call | solution.py:216
  14.6 1.0 collective-permute-start
  15.5 5.0 %collective-permute-start.3 = (bf16[2,384,1536]{2,1,0:T(8,128)(2,1)}, bf16[2,384,1536]{2,1,0:T(8,128)(2,1)}, u32[]{:S(2)}, u32[]{:S(2)}) collective-permute-start(bf16[2,384,1536]{2,1,0:T(8,128)(2,1)} %get-tuple-element.54), channel_id=1, source_target_pairs={{0,1},{1,2},{2,3},{3,4},{4,5},{5,6},{6,7},{7,8},{8,9},{9,10},{10,1... | collective-permute-start | bytes 7077896 | tf_op jit(solution)/shard_map/ppermute | solution.py:305
  20.5 1.9 collective-permute-start.4
  22.5 5.9 %shard_map.113 = bf16[2,2,8,96,384]{4,3,2,1,0:T(8,128)(2,1)} custom-call(s32[1]{0:T(128)} %bitcast.6.which, bf16[768,1536]{1,0:T(8,128)(2,1)} %bitcast.31, bf16[768,3072]{1,0:T(8,128)(2,1)} %bitcast.24), custom_call_target="tpu_custom_call" | custom-call | flops 56623104 | bytes 400000 | tf_op jit(solution)/shard_map/pallas_call | solution.py:216
  28.3 0.7 collective-permute-start.2
  29.1 1.1 broadcast_select_fusion.3
  30.2 1.1 pad_maximum_fusion
  31.3 3.8 %collective-permute-done.5 = bf16[384,1536]{1,0:T(8,128)(2,1)S(1)} collective-permute-done((bf16[384,1536]{1,0:T(8,128)(2,1)}, bf16[384,1536]{1,0:T(8,128)(2,1)S(1)}, u32[]{:S(2)}, u32[]{:S(2)}) %collective-permute-start.5) | collective-permute-done | bytes 1179680 | tf_op jit(solution)/shard_map/ppermute | solution.py:305
  35.1 1.3 collective-permute-start.6
  36.4 1.4 collective-permute-start.7
  37.9 0.4 broadcast_select_fusion.1
  38.3 5.8 %fusion.7.refs_10_ = bf16[768,384]{1,0:T(8,128)(2,1)} fusion(bf16[384,1536]{1,0:T(8,128)(2,1)S(1)} %get-tuple-element.95, bf16[384,1536]{1,0:T(8,128)(2,1)S(1)} %get-tuple-element.94, bf16[1,768,3072]{2,1,0:T(8,128)(2,1)} %param.13), kind=kOutput, calls=%fused_computation.5 | convolution fusion | flops 1816952832 | bytes 7667712 | tf_op jit(solution)/shard_map/dot_general | solution.py:23
  44.0 2.6 %collective-permute-done.3.refs_2_.refs_5_ = bf16[2,384,1536]{2,1,0:T(8,128)(2,1)} collective-permute-done((bf16[2,384,1536]{2,1,0:T(8,128)(2,1)}, bf16[2,384,1536]{2,1,0:T(8,128)(2,1)}, u32[]{:S(2)}, u32[]{:S(2)}) %collective-permute-start.3) | collective-permute-done | bytes 2359328 | tf_op jit(solution)/shard_map/ppermute | solution.py:305
  46.6 8.0 %collective-permute-done.4.refs_4_.refs_7_ = bf16[2,384,1536]{2,1,0:T(8,128)(2,1)} collective-permute-done((bf16[2,384,1536]{2,1,0:T(8,128)(2,1)}, bf16[2,384,1536]{2,1,0:T(8,128)(2,1)}, u32[]{:S(2)}, u32[]{:S(2)}) %collective-permute-start.4) | collective-permute-done | bytes 2359328 | tf_op jit(solution)/shard_map/ppermute | solution.py:305
  54.6 8.6 %shard_map.114 = bf16[2,4,8,96,384]{4,3,2,1,0:T(8,128)(2,1)} custom-call(s32[1]{0:T(128)} %bitcast.which, bf16[768,1536]{1,0:T(8,128)(2,1)} %bitcast.32, bf16[768,3072]{1,0:T(8,128)(2,1)} %bitcast.25, bf16[2,2,8,96,384]{4,3,2,1,0:T(8,128)(2,1)} %collective-permute-done.refs_0_, bf16[2,2,8,96,384]{4,3,2,1,0:T(8,128)(2,1)} %collective-permute-done.2.refs_1_), custom_call_target="tpu_custom_call" | custom-call | flops 113246208 | bytes 400000 | tf_op jit(solution)/shard_map/pallas_call | solution.py:216
  63.3 0.7 collective-permute-done.6.refs_12_
  63.9 7.5 %all-to-all-start = ((bf16[8,8,96,384]{3,2,1,0:T(8,128)(2,1)}), bf16[8,8,96,384]{3,2,1,0:T(8,128)(2,1)}, u32[]{:S(2)}, u32[]{:S(2)}) async-start(bf16[8,8,96,384]{3,2,1,0:T(8,128)(2,1)} %bitcast.49), calls=%async_computation | async-start | bytes 9437184 | tf_op jit(solution)/shard_map/all_to_all | solution.py:349
  71.4 1.7 collective-permute-start.10
  73.2 0.1 copy.26
  73.3 0.1 sub.28
  73.4 0.6 copy.28
  74.1 0.6 pad_add_fusion.2.refs_0_
  74.7 0.7 pad_add_fusion.3
  75.3 1.3 collective-permute-start.8
  76.6 11.8 %shard_map.115 = (bf16[768,1536]{1,0:T(8,128)(2,1)}, f32[768,1152]{1,0:T(8,128)}, f32[768,1152]{1,0:T(8,128)}, bf16[2,384,1152]{2,1,0:T(8,128)(2,1)}, bf16[2,384,1152]{2,1,0:T(8,128)(2,1)}) custom-call(s32[10]{0:T(128)} %get-tuple-element.98.refs_0_, bf16[768,1536]{1,0:T(8,128)(2,1)} %bitcast.46, ...), custom_call_target="tpu_custom_call" | custom-call | flops 3397386240 | bytes 6000000 | tf_op jit(solution)/shard_map/pallas_call | solution.py:124
  88.5 1.0 copy-done.2
  89.5 28.9 %shard_map.116 = (bf16[768,1536]{1,0:T(8,128)(2,1)}, f32[768,1152]{1,0:T(8,128)}, f32[768,1152]{1,0:T(8,128)}, bf16[2,384,1152]{2,1,0:T(8,128)(2,1)}, bf16[2,384,1152]{2,1,0:T(8,128)(2,1)}) custom-call(s32[13]{0:T(128)} %pad_add_fusion.2.refs_0_, ...), custom_call_target="tpu_custom_call", output_to_operand_aliasing={{0}: (16, {}), {1}: (17, {}), {2}: (18, {}), {3}: (19, {}),... | custom-call | flops 10418651136 | bytes 12000000 | tf_op jit(solution)/shard_map/pallas_call | solution.py:124
  118.4 0.9 collective-permute-start.11
  119.3 4.5 %collective-permute-start.12 = (bf16[2,384,1152]{2,1,0:T(8,128)(2,1)}, bf16[2,384,1152]{2,1,0:T(8,128)(2,1)}, u32[]{:S(2)}, u32[]{:S(2)}) collective-permute-start(bf16[2,384,1152]{2,1,0:T(8,128)(2,1)} %get-tuple-element.79), channel_id=1, source_target_pairs={{0,1},{1,2},{2,3},{3,4},{4,5},{5,6},{6,7},{7,8},{8,9},{9,10},{10,1... | collective-permute-start | bytes 5308424 | tf_op jit(solution)/shard_map/ppermute | solution.py:305
  123.8 2.1 %collective-permute-start.13 = (bf16[2,384,1152]{2,1,0:T(8,128)(2,1)}, bf16[2,384,1152]{2,1,0:T(8,128)(2,1)}, u32[]{:S(2)}, u32[]{:S(2)}) collective-permute-start(bf16[2,384,1152]{2,1,0:T(8,128)(2,1)} %get-tuple-element.80), channel_id=1, source_target_pairs={{1,0},{2,1},{3,2},{4,3},{5,4},{6,5},{7,6},{8,7},{9,8},{10,9},{11,1... | collective-permute-start | bytes 5308424 | tf_op jit(solution)/shard_map/ppermute | solution.py:305
  125.9 1.0 copy-done.3
  126.9 16.7 %shard_map.117 = (bf16[768,1536]{1,0:T(8,128)(2,1)}, f32[768,384]{1,0:T(8,128)}, f32[768,384]{1,0:T(8,128)}, bf16[2,384,384]{2,1,0:T(8,128)(2,1)}, bf16[2,384,384]{2,1,0:T(8,128)(2,1)}) custom-call(s32[10]{0:T(128)} %get-tuple-element.99.refs_0_, bf16[768,1536]{1,0:T(8,128)(2,1)} %bitcast.48, ...), custom_call_target="tpu_custom_call", output_to_operand_aliasing={{0}: (14, {})} | custom-call | flops 5209325568 | bytes 6000000 | tf_op jit(solution)/shard_map/pallas_call | solution.py:124
  143.7 7.3 %collective-permute-start.14 = (bf16[2,384,384]{2,1,0:T(8,128)(2,1)}, bf16[2,384,384]{2,1,0:T(8,128)(2,1)S(1)}, u32[]{:S(2)}, u32[]{:S(2)}) collective-permute-start(bf16[2,384,384]{2,1,0:T(8,128)(2,1)} %get-tuple-element.81), channel_id=1, source_target_pairs={{0,1},{1,2},{2,3},{3,4},{4,5},{5,6},{6,7},{7,8},{8,9},{9,10},{10,1... | collective-permute-start | bytes 1769480 | tf_op jit(solution)/shard_map/ppermute | solution.py:305
  150.9 1.9 collective-permute-start.15
  152.9 4.0 %reduce_sum.24 = bf16[8,96,384]{2,1,0:T(8,128)(2,1)} reduce(bf16[8,8,96,384]{3,2,1,0:T(8,128)(2,1)} %all-to-all-done, bf16[]{:T(256)} %constant.81.clone.1), dimensions={0}, to_apply=%region_0.1 | reduce | flops 2064384 | bytes 5308418 | tf_op jit(solution)/shard_map/reduce_sum | solution.py:383
  156.8 4.3 %all-to-all-start.1 = ((bf16[8,96,384]{2,1,0:T(8,128)(2,1)}), bf16[8,96,384]{2,1,0:T(8,128)(2,1)S(1)}, u32[]{:S(2)}, u32[]{:S(2)}) async-start(bf16[8,96,384]{2,1,0:T(8,128)(2,1)} %reduce_sum.24), calls=%async_computation.1 | async-start | bytes 1179648 | tf_op jit(solution)/shard_map/all_to_all | solution.py:385
  161.1 11.8 %collective-permute-done.15.refs_3_ = bf16[2,384,384]{2,1,0:T(8,128)(2,1)S(1)} collective-permute-done((bf16[2,384,384]{2,1,0:T(8,128)(2,1)}, bf16[2,384,384]{2,1,0:T(8,128)(2,1)S(1)}, u32[]{:S(2)}, u32[]{:S(2)}) %collective-permute-start.15) | collective-permute-done | bytes 589856 | tf_op jit(solution)/shard_map/ppermute | solution.py:305
  173.0 1.1 broadcast_in_dim.30
  174.1 7.4 %all-to-all-start.2 = ((bf16[16,96,384]{2,1,0:T(8,128)(2,1)}), bf16[16,96,384]{2,1,0:T(8,128)(2,1)}, u32[]{:S(2)}, u32[]{:S(2)}) async-start(bf16[16,96,384]{2,1,0:T(8,128)(2,1)} %broadcast_in_dim.30), calls=%async_computation.2 | async-start | bytes 2359296 | tf_op jit(solution)/shard_map/all_to_all | solution.py:389
  181.5 0.7 pad_add_fusion.4.meta
  182.1 7.2 %shard_map.118 = (bf16[768,1536]{1,0:T(8,128)(2,1)}, bf16[768,1536]{1,0:T(8,128)(2,1)}) custom-call(s32[3]{0:T(128)} %pad_add_fusion.4.meta, f32[768,1152]{1,0:T(8,128)} %get-tuple-element.85.refs_0_, f32[768,1152]{1,0:T(8,128)} %get-tuple-element.86.refs_1_, bf16[2,384,1152]{2,1,0:T(8,128)(2,1)} %collective-permute-done.12.refs_2_, ...), custom_call_target="tpu_custom_call" | custom-call | flops 4000000 | bytes 20000000 | tf_op jit(solution)/shard_map/pallas_call | solution.py:174
  189.3 3.2 %shard_map.119 = (bf16[768,1536]{1,0:T(8,128)(2,1)}, bf16[768,1536]{1,0:T(8,128)(2,1)}) custom-call(s32[1]{0:T(128)} %bitcast.11.meta, f32[768,384]{1,0:T(8,128)} %get-tuple-element.76.refs_0_, f32[768,384]{1,0:T(8,128)} %get-tuple-element.77.refs_1_, bf16[2,384,384]{2,1,0:T(8,128)(2,1)} %copy-done.4, ...), custom_call_target="tpu_custom_call", output_to_operand_aliasing={{0}: (5, {}), {1}: (6, {})} | custom-call | flops 4000000 | bytes 20000000 | tf_op jit(solution)/shard_map/pallas_call | solution.py:174
  192.5 5.9 %all-to-all-done.2.pieces = bf16[16,96,384]{2,1,0:T(8,128)(2,1)} async-done(((bf16[16,96,384]{2,1,0:T(8,128)(2,1)}), bf16[16,96,384]{2,1,0:T(8,128)(2,1)}, u32[]{:S(2)}, u32[]{:S(2)}) %all-to-all-start.2) | async-done | bytes 1179680 | tf_op jit(solution)/shard_map/all_to_all | solution.py:389
  198.4 2.5 %shard_map.120 = f32[192,3072]{1,0:T(8,128)} custom-call(bf16[16,96,384]{2,1,0:T(8,128)(2,1)} %all-to-all-done.2.pieces), custom_call_target="tpu_custom_call" | custom-call | tf_op jit(solution)/shard_map/pallas_call | solution.py:248
  (36 shorter events, 0.3 us)
Async XLA Ops:
  0.6 1.3 copy-start
  7.3 15.2 %collective-permute-start.1 = (bf16[192,1536]{1,0:T(8,128)(2,1)S(1)}, bf16[192,1536]{1,0:T(8,128)(2,1)S(1)}, u32[]{:S(2)}, u32[]{:S(2)}) collective-permute-start(bf16[192,1536]{1,0:T(8,128)(2,1)S(1)} %constant_dynamic-slice_fusion.1), channel_id=1, source_target_pairs={{0,16},{16,0},{32,48},{48,32},{64,80},{80,64},{96,112},{112,96},{1... | collective-permute-start | bytes 1769480 | tf_op jit(solution)/shard_map/ppermute | solution.py:301
  14.6 21.9 %collective-permute-start = (bf16[2,2,8,96,384]{4,3,2,1,0:T(8,128)(2,1)}, bf16[2,2,8,96,384]{4,3,2,1,0:T(8,128)(2,1)}, u32[]{:S(2)}, u32[]{:S(2)}) collective-permute-start(bf16[2,2,8,96,384]{4,3,2,1,0:T(8,128)(2,1)} %shard_map.112), channel_id=1, source_target_pairs={{0,1},{1,0},{2,3},{3,2},{4,5},{5,4},{6,7},{7,6},{8,9},{9,8},{10,11... | collective-permute-start | bytes 7077896 | tf_op jit(solution)/shard_map/ppermute | solution.py:305
  15.5 31.1 %collective-permute-start.3 = (bf16[2,384,1536]{2,1,0:T(8,128)(2,1)}, bf16[2,384,1536]{2,1,0:T(8,128)(2,1)}, u32[]{:S(2)}, u32[]{:S(2)}) collective-permute-start(bf16[2,384,1536]{2,1,0:T(8,128)(2,1)} %get-tuple-element.54), channel_id=1, source_target_pairs={{0,1},{1,2},{2,3},{3,4},{4,5},{5,6},{6,7},{7,8},{8,9},{9,10},{10,1... | collective-permute-start | bytes 7077896 | tf_op jit(solution)/shard_map/ppermute | solution.py:305
  20.5 34.1 %collective-permute-start.4 = (bf16[2,384,1536]{2,1,0:T(8,128)(2,1)}, bf16[2,384,1536]{2,1,0:T(8,128)(2,1)}, u32[]{:S(2)}, u32[]{:S(2)}) collective-permute-start(bf16[2,384,1536]{2,1,0:T(8,128)(2,1)} %get-tuple-element.55), channel_id=1, source_target_pairs={{1,0},{2,1},{3,2},{4,3},{5,4},{6,5},{7,6},{8,7},{9,8},{10,9},{11,1... | collective-permute-start | bytes 7077896 | tf_op jit(solution)/shard_map/ppermute | solution.py:305
  22.5 5.9 %copy-start.6 = (bf16[192,1536]{1,0:T(8,128)(2,1)}, bf16[192,1536]{1,0:T(8,128)(2,1)S(1)}, u32[]{:S(2)}) copy-start(bf16[192,1536]{1,0:T(8,128)(2,1)S(1)} %collective-permute-done.1) | copy-start | bytes 1769476
  28.3 26.3 %collective-permute-start.2 = (bf16[2,2,8,96,384]{4,3,2,1,0:T(8,128)(2,1)}, bf16[2,2,8,96,384]{4,3,2,1,0:T(8,128)(2,1)}, u32[]{:S(2)}, u32[]{:S(2)}) collective-permute-start(bf16[2,2,8,96,384]{4,3,2,1,0:T(8,128)(2,1)} %shard_map.113), channel_id=1, source_target_pairs={{0,1},{1,0},{2,3},{3,2},{4,5},{5,4},{6,7},{7,6},{8,9},{9,8},{10,11... | collective-permute-start | bytes 7077896 | tf_op jit(solution)/shard_map/ppermute | solution.py:305
  31.3 3.8 %collective-permute-start.5 = (bf16[384,1536]{1,0:T(8,128)(2,1)}, bf16[384,1536]{1,0:T(8,128)(2,1)S(1)}, u32[]{:S(2)}, u32[]{:S(2)}) collective-permute-start(bf16[384,1536]{1,0:T(8,128)(2,1)} %pad_maximum_fusion), channel_id=1, source_target_pairs={{0,1},{1,0},{2,3},{3,2},{4,5},{5,4},{6,7},{7,6},{8,9},{9,8},{10,11... | collective-permute-start | bytes 3538952 | tf_op jit(solution)/shard_map/ppermute | solution.py:305
  35.1 28.8 %collective-permute-start.6 = (bf16[384,1536]{1,0:T(8,128)(2,1)}, bf16[384,1536]{1,0:T(8,128)(2,1)}, u32[]{:S(2)}, u32[]{:S(2)}) collective-permute-start(bf16[384,1536]{1,0:T(8,128)(2,1)} %pad_maximum_fusion), channel_id=1, source_target_pairs={{0,32},{16,48},{32,64},{48,80},{64,96},{80,112},{96,0},{112,16},{1... | collective-permute-start | bytes 3538952 | tf_op jit(solution)/shard_map/ppermute | solution.py:301
  36.4 27.5 %collective-permute-start.7 = (bf16[384,1536]{1,0:T(8,128)(2,1)}, bf16[384,1536]{1,0:T(8,128)(2,1)}, u32[]{:S(2)}, u32[]{:S(2)}) collective-permute-start(bf16[384,1536]{1,0:T(8,128)(2,1)} %pad_maximum_fusion), channel_id=1, source_target_pairs={{0,96},{16,112},{32,0},{48,16},{64,32},{80,48},{96,64},{112,80},{1... | collective-permute-start | bytes 3538952 | tf_op jit(solution)/shard_map/ppermute | solution.py:301
  63.9 9.2 %copy-start.8 = (s32[1,32,3]{1,0,2:T(1,128)S(1)}, s32[1,32,3]{1,0,2:T(1,128)}, u32[]{:S(2)}) copy-start(s32[1,32,3]{1,0,2:T(1,128)} %param.15) | copy-start | bytes 1156
  63.9 9.5 %copy-start.7 = (f32[1,12,768]{2,0,1:T(1,128)S(1)}, f32[1,12,768]{2,0,1:T(1,128)}, u32[]{:S(2)}) copy-start(f32[1,12,768]{2,0,1:T(1,128)} %param.12) | copy-start | bytes 110596
  63.9 88.9 %all-to-all-start = ((bf16[8,8,96,384]{3,2,1,0:T(8,128)(2,1)}), bf16[8,8,96,384]{3,2,1,0:T(8,128)(2,1)}, u32[]{:S(2)}, u32[]{:S(2)}) async-start(bf16[8,8,96,384]{3,2,1,0:T(8,128)(2,1)} %bitcast.49), calls=%async_computation | async-start | bytes 9437184 | tf_op jit(solution)/shard_map/all_to_all | solution.py:349
  71.4 17.0 %collective-permute-start.10 = (bf16[384,1536]{1,0:T(8,128)(2,1)}, bf16[384,1536]{1,0:T(8,128)(2,1)S(1)}, u32[]{:S(2)}, u32[]{:S(2)}) collective-permute-start(bf16[384,1536]{1,0:T(8,128)(2,1)} %collective-permute-done.7.refs_14_), channel_id=1, source_target_pairs={{0,1},{1,0},{2,3},{3,2},{4,5},{5,4},{6,7},{7,6},{8,9},{9,8},{10,11... | collective-permute-start | bytes 3538952 | tf_op jit(solution)/shard_map/ppermute | solution.py:305
  73.2 15.3 %collective-permute-start.9 = (bf16[384,1536]{1,0:T(8,128)(2,1)}, bf16[384,1536]{1,0:T(8,128)(2,1)}, u32[]{:S(2)}, u32[]{:S(2)}) collective-permute-start(bf16[384,1536]{1,0:T(8,128)(2,1)} %collective-permute-done.6.refs_12_), channel_id=1, source_target_pairs={{0,1},{1,0},{2,3},{3,2},{4,5},{5,4},{6,7},{7,6},{8,9},{9,8},{10,11... | collective-permute-start | bytes 3538952 | tf_op jit(solution)/shard_map/ppermute | solution.py:305
  75.3 43.1 %collective-permute-start.8 = (bf16[384,1536]{1,0:T(8,128)(2,1)}, bf16[384,1536]{1,0:T(8,128)(2,1)}, u32[]{:S(2)}, u32[]{:S(2)}) collective-permute-start(bf16[384,1536]{1,0:T(8,128)(2,1)} %collective-permute-done.6.refs_12_), channel_id=1, source_target_pairs={{0,32},{16,48},{32,64},{48,80},{64,96},{80,112},{96,0},{112,16},{1... | collective-permute-start | bytes 3538952 | tf_op jit(solution)/shard_map/ppermute | solution.py:301
  88.5 1.0 copy-start.2
  118.4 7.5 %collective-permute-start.11 = (bf16[384,1536]{1,0:T(8,128)(2,1)}, bf16[384,1536]{1,0:T(8,128)(2,1)S(1)}, u32[]{:S(2)}, u32[]{:S(2)}) collective-permute-start(bf16[384,1536]{1,0:T(8,128)(2,1)} %collective-permute-done.8.refs_12_), channel_id=1, source_target_pairs={{0,1},{1,0},{2,3},{3,2},{4,5},{5,4},{6,7},{7,6},{8,9},{9,8},{10,11... | collective-permute-start | bytes 3538952 | tf_op jit(solution)/shard_map/ppermute | solution.py:305
  119.3 53.6 %collective-permute-start.12 = (bf16[2,384,1152]{2,1,0:T(8,128)(2,1)}, bf16[2,384,1152]{2,1,0:T(8,128)(2,1)}, u32[]{:S(2)}, u32[]{:S(2)}) collective-permute-start(bf16[2,384,1152]{2,1,0:T(8,128)(2,1)} %get-tuple-element.79), channel_id=1, source_target_pairs={{0,1},{1,2},{2,3},{3,4},{4,5},{5,6},{6,7},{7,8},{8,9},{9,10},{10,1... | collective-permute-start | bytes 5308424 | tf_op jit(solution)/shard_map/ppermute | solution.py:305
  123.8 49.1 %collective-permute-start.13 = (bf16[2,384,1152]{2,1,0:T(8,128)(2,1)}, bf16[2,384,1152]{2,1,0:T(8,128)(2,1)}, u32[]{:S(2)}, u32[]{:S(2)}) collective-permute-start(bf16[2,384,1152]{2,1,0:T(8,128)(2,1)} %get-tuple-element.80), channel_id=1, source_target_pairs={{1,0},{2,1},{3,2},{4,3},{5,4},{6,5},{7,6},{8,7},{9,8},{10,9},{11,1... | collective-permute-start | bytes 5308424 | tf_op jit(solution)/shard_map/ppermute | solution.py:305
  125.9 1.0 copy-start.3
  143.7 17.4 %collective-permute-start.14 = (bf16[2,384,384]{2,1,0:T(8,128)(2,1)}, bf16[2,384,384]{2,1,0:T(8,128)(2,1)S(1)}, u32[]{:S(2)}, u32[]{:S(2)}) collective-permute-start(bf16[2,384,384]{2,1,0:T(8,128)(2,1)} %get-tuple-element.81), channel_id=1, source_target_pairs={{0,1},{1,2},{2,3},{3,4},{4,5},{5,6},{6,7},{7,8},{8,9},{9,10},{10,1... | collective-permute-start | bytes 1769480 | tf_op jit(solution)/shard_map/ppermute | solution.py:305
  150.9 21.9 %collective-permute-start.15 = (bf16[2,384,384]{2,1,0:T(8,128)(2,1)}, bf16[2,384,384]{2,1,0:T(8,128)(2,1)S(1)}, u32[]{:S(2)}, u32[]{:S(2)}) collective-permute-start(bf16[2,384,384]{2,1,0:T(8,128)(2,1)} %get-tuple-element.82), channel_id=1, source_target_pairs={{1,0},{2,1},{3,2},{4,3},{5,4},{6,5},{7,6},{8,7},{9,8},{10,9},{11,1... | collective-permute-start | bytes 1769480 | tf_op jit(solution)/shard_map/ppermute | solution.py:305
  156.8 16.0 %all-to-all-start.1 = ((bf16[8,96,384]{2,1,0:T(8,128)(2,1)}), bf16[8,96,384]{2,1,0:T(8,128)(2,1)S(1)}, u32[]{:S(2)}, u32[]{:S(2)}) async-start(bf16[8,96,384]{2,1,0:T(8,128)(2,1)} %reduce_sum.24), calls=%async_computation.1 | async-start | bytes 1179648 | tf_op jit(solution)/shard_map/all_to_all | solution.py:385
  161.1 28.2 %copy-start.4 = (bf16[2,384,384]{2,1,0:T(8,128)(2,1)}, bf16[2,384,384]{2,1,0:T(8,128)(2,1)S(1)}, u32[]{:S(2)}) copy-start(bf16[2,384,384]{2,1,0:T(8,128)(2,1)S(1)} %collective-permute-done.14.refs_2_) | copy-start | bytes 1769476
  172.9 16.4 %copy-start.5 = (bf16[2,384,384]{2,1,0:T(8,128)(2,1)}, bf16[2,384,384]{2,1,0:T(8,128)(2,1)S(1)}, u32[]{:S(2)}) copy-start(bf16[2,384,384]{2,1,0:T(8,128)(2,1)S(1)} %collective-permute-done.15.refs_3_) | copy-start | bytes 1769476
  174.1 24.3 %all-to-all-start.2 = ((bf16[16,96,384]{2,1,0:T(8,128)(2,1)}), bf16[16,96,384]{2,1,0:T(8,128)(2,1)}, u32[]{:S(2)}, u32[]{:S(2)}) async-start(bf16[16,96,384]{2,1,0:T(8,128)(2,1)} %broadcast_in_dim.30), calls=%async_computation.2 | async-start | bytes 2359296 | tf_op jit(solution)/shard_map/all_to_all | solution.py:389
  189.3 11.6 %copy-start.1 = (bf16[192,3072]{1,0:T(8,128)(2,1)S(1)}, bf16[192,3072]{1,0:T(8,128)(2,1)}, u32[]{:S(2)}) copy-start(bf16[192,3072]{1,0:T(8,128)(2,1)} %param.14) | copy-start | bytes 3538948

commit v7 on v6

--- a/solution.py
+++ b/solution.py
@@ -378,9 +378,10 @@
     far, dq = lax.optimization_barrier((far, dq))
     rims = rims_of(low, high)
     dq, *rest = attend_group([y + 2], None, [(far, swap(far))], three, 0, [dq])
-    pending = [[dko, dvo, *rims], [*rest[:2], *rims_of(*rest[2:])]]
     spread, dq = lax.optimization_barrier((spread, dq))
     clip_sum = spread.astype(F32).sum(0).astype(BF16)
+    clip_sum, *edges = lax.optimization_barrier((clip_sum, *rest[2:]))
+    pending = [[dko, dvo, *rims], [*rest[:2], *rims_of(*edges)]]
 
     met = lax.all_to_all(clip_sum, "dp", 0, 0)
     met, *rims = lax.optimization_barrier((met, *pending[0][2:], *pending[1][2:]))

time: 205 us -> 205 us (level)
    ppermute x12, waiting for transfers between devices: 26.2 us -> 20.2 us  [over_seq(): lax.ppermute(value, 'seq', [(i, j) for i, j in pairs if 0 <= j < n_seq])]
    all_to_all x1, waiting for transfers between devices: 0.01 us -> 5.92 us  [body(): met = lax.all_to_all(clip_sum, 'dp', 0, 0)]
  transfers between devices with their start and end apart: 19 -> 19, of which waited for: 6 -> 8; matrix products, arithmetic and copies ran while one was open for 8% -> 8% of each run, Pallas kernels for 44% -> 44%
where the time goes in v7:
time: 205 us; the launch traced here: 201 us
  Pallas kernels  95.8 us (47%)
  starting transfers between devices  52 us (25%)
  waiting for transfers between devices  32.7 us (16%)
  other arithmetic  8.63 us (4%)
  matrix products  5.77 us (3%)
  local copies, waits for them, and re-layouts  5.32 us (3%)
    pallas_call x3, Pallas kernels, attend(): pl.pallas_call(functools.partial(attend_kernel, len(slabs)), grid_spec=pl...  57.4 us
    ppermute x12, starting transfers between devices, over_seq(): lax.ppermute(value, 'seq', [(i, j) for i, j in pairs if 0 <= j < n_seq])  27 us
    ppermute x12, waiting for transfers between devices, over_seq(): lax.ppermute(value, 'seq', [(i, j) for i, j in pairs if 0 <= j < n_seq])  20.2 us
    pallas_call x3, Pallas kernels, product(): pl.pallas_call(product_kernel, grid_spec=pltpu.PrefetchScalarGridSpec(num...  20.1 us
    pallas_call x2, Pallas kernels, combine(): pl.pallas_call(functools.partial(combine_kernel, edges), grid_spec=pltpu....  10.4 us
    all_to_all x1, starting transfers between devices, body(): lax.all_to_all(jnp.broadcast_to(total, (n_seq, *piece)), 'seq', 0, 0)  7.6 us
    all_to_all x1, starting transfers between devices, body(): lax.all_to_all(chip_sum.reshape(n_seq // 2, n_dp, *piece), 'seq', 0, 0, a...  7.5 us
    all_to_all x1, waiting for transfers between devices, body(): met = lax.all_to_all(clip_sum, 'dp', 0, 0)  5.92 us
  transfers between devices with their start and end apart: 19, of which 8 were waited for; matrix products, arithmetic and copies ran while one was open for 8% of the time, Pallas kernels for 44%

profile of v7, /device:TPU:7, one launch (start us, length us, event | category | flops | bytes accessed | tf_op | source)
XLA Modules:
  0.0 201.1 jit_solution(7080198844518645140)
XLA Ops:
  0.7 1.2 copy-done
  2.0 5.3 %shard_map.111 = (bf16[2,384,1536]{2,1,0:T(8,128)(2,1)}, bf16[2,384,1536]{2,1,0:T(8,128)(2,1)}) custom-call(bf16[768,1536]{1,0:T(8,128)(2,1)} %bitcast.36, bf16[768,1536]{1,0:T(8,128)(2,1)} %bitcast.37, bf16[768,1536]{1,0:T(8,128)(2,1)} %bitcast.41, bf16[768,1536]{1,0:T(8,128)(2,1)} %bitcast.42), custom_call_target="tpu_custom_call" | custom-call | tf_op jit(solution)/shard_map/pallas_call | solution.py:273
  7.3 1.6 collective-permute-start.1
  8.9 5.6 %shard_map.112 = bf16[2,2,8,96,384]{4,3,2,1,0:T(8,128)(2,1)} custom-call(s32[1]{0:T(128)} %bitcast.3.which, bf16[768,1536]{1,0:T(8,128)(2,1)} %bitcast.30, bf16[768,3072]{1,0:T(8,128)(2,1)} %bitcast.23), custom_call_target="tpu_custom_call" | custom-call | flops 56623104 | bytes 400000 | tf_op jit(solution)/shard_map/pallas_call | solution.py:216
  14.6 1.0 collective-permute-start
  15.5 5.0 %collective-permute-start.3 = (bf16[2,384,1536]{2,1,0:T(8,128)(2,1)}, bf16[2,384,1536]{2,1,0:T(8,128)(2,1)}, u32[]{:S(2)}, u32[]{:S(2)}) collective-permute-start(bf16[2,384,1536]{2,1,0:T(8,128)(2,1)} %get-tuple-element.57), channel_id=1, source_target_pairs={{0,1},{1,2},{2,3},{3,4},{4,5},{5,6},{6,7},{7,8},{8,9},{9,10},{10,1... | collective-permute-start | bytes 7077896 | tf_op jit(solution)/shard_map/ppermute | solution.py:305
  20.5 1.9 collective-permute-start.4
  22.5 5.9 %shard_map.113 = bf16[2,2,8,96,384]{4,3,2,1,0:T(8,128)(2,1)} custom-call(s32[1]{0:T(128)} %bitcast.6.which, bf16[768,1536]{1,0:T(8,128)(2,1)} %bitcast.31, bf16[768,3072]{1,0:T(8,128)(2,1)} %bitcast.24), custom_call_target="tpu_custom_call" | custom-call | flops 56623104 | bytes 400000 | tf_op jit(solution)/shard_map/pallas_call | solution.py:216
  28.3 0.7 collective-permute-start.2
  29.1 1.1 broadcast_select_fusion.3
  30.2 1.1 pad_maximum_fusion
  31.3 3.8 %collective-permute-done.5 = bf16[384,1536]{1,0:T(8,128)(2,1)S(1)} collective-permute-done((bf16[384,1536]{1,0:T(8,128)(2,1)}, bf16[384,1536]{1,0:T(8,128)(2,1)S(1)}, u32[]{:S(2)}, u32[]{:S(2)}) %collective-permute-start.5) | collective-permute-done | bytes 1179680 | tf_op jit(solution)/shard_map/ppermute | solution.py:305
  35.1 1.3 collective-permute-start.6
  36.4 1.4 collective-permute-start.7
  37.9 0.4 broadcast_select_fusion.1
  38.3 5.8 %fusion.7.refs_10_ = bf16[768,384]{1,0:T(8,128)(2,1)} fusion(bf16[384,1536]{1,0:T(8,128)(2,1)S(1)} %get-tuple-element.101, bf16[384,1536]{1,0:T(8,128)(2,1)S(1)} %get-tuple-element.100, bf16[1,768,3072]{2,1,0:T(8,128)(2,1)} %param.13), kind=kOutput, calls=%fused_computation.5 | convolution fusion | flops 1816952832 | bytes 7667712 | tf_op jit(solution)/shard_map/dot_general | solution.py:23
  44.0 2.6 %collective-permute-done.3.refs_2_.refs_5_ = bf16[2,384,1536]{2,1,0:T(8,128)(2,1)} collective-permute-done((bf16[2,384,1536]{2,1,0:T(8,128)(2,1)}, bf16[2,384,1536]{2,1,0:T(8,128)(2,1)}, u32[]{:S(2)}, u32[]{:S(2)}) %collective-permute-start.3) | collective-permute-done | bytes 2359328 | tf_op jit(solution)/shard_map/ppermute | solution.py:305
  46.6 8.0 %collective-permute-done.4.refs_4_.refs_7_ = bf16[2,384,1536]{2,1,0:T(8,128)(2,1)} collective-permute-done((bf16[2,384,1536]{2,1,0:T(8,128)(2,1)}, bf16[2,384,1536]{2,1,0:T(8,128)(2,1)}, u32[]{:S(2)}, u32[]{:S(2)}) %collective-permute-start.4) | collective-permute-done | bytes 2359328 | tf_op jit(solution)/shard_map/ppermute | solution.py:305
  54.6 8.6 %shard_map.114 = bf16[2,4,8,96,384]{4,3,2,1,0:T(8,128)(2,1)} custom-call(s32[1]{0:T(128)} %bitcast.which, bf16[768,1536]{1,0:T(8,128)(2,1)} %bitcast.32, bf16[768,3072]{1,0:T(8,128)(2,1)} %bitcast.25, bf16[2,2,8,96,384]{4,3,2,1,0:T(8,128)(2,1)} %collective-permute-done.refs_0_, bf16[2,2,8,96,384]{4,3,2,1,0:T(8,128)(2,1)} %collective-permute-done.2.refs_1_), custom_call_target="tpu_custom_call" | custom-call | flops 113246208 | bytes 400000 | tf_op jit(solution)/shard_map/pallas_call | solution.py:216
  63.2 0.7 collective-permute-done.6.refs_12_
  63.9 7.5 %all-to-all-start = ((bf16[8,8,96,384]{3,2,1,0:T(8,128)(2,1)}), bf16[8,8,96,384]{3,2,1,0:T(8,128)(2,1)}, u32[]{:S(2)}, u32[]{:S(2)}) async-start(bf16[8,8,96,384]{3,2,1,0:T(8,128)(2,1)} %bitcast.49), calls=%async_computation | async-start | bytes 9437184 | tf_op jit(solution)/shard_map/all_to_all | solution.py:349
  71.4 1.7 collective-permute-start.10
  73.4 0.6 copy.28
  74.1 0.6 pad_add_fusion.2.refs_0_
  74.7 0.6 pad_add_fusion.3
  75.3 1.3 collective-permute-start.8
  76.6 11.8 %shard_map.115 = (bf16[768,1536]{1,0:T(8,128)(2,1)}, f32[768,1152]{1,0:T(8,128)}, f32[768,1152]{1,0:T(8,128)}, bf16[2,384,1152]{2,1,0:T(8,128)(2,1)}, bf16[2,384,1152]{2,1,0:T(8,128)(2,1)}) custom-call(s32[10]{0:T(128)} %get-tuple-element.104.refs_0_, bf16[768,1536]{1,0:T(8,128)(2,1)} %bitcast.46, ...), custom_call_target="tpu_custom_call" | custom-call | flops 3397386240 | bytes 6000000 | tf_op jit(solution)/shard_map/pallas_call | solution.py:124
  88.4 1.0 copy-done.2
  89.4 28.9 %shard_map.116 = (bf16[768,1536]{1,0:T(8,128)(2,1)}, f32[768,1152]{1,0:T(8,128)}, f32[768,1152]{1,0:T(8,128)}, bf16[2,384,1152]{2,1,0:T(8,128)(2,1)}, bf16[2,384,1152]{2,1,0:T(8,128)(2,1)}) custom-call(s32[13]{0:T(128)} %pad_add_fusion.2.refs_0_, ...), custom_call_target="tpu_custom_call", output_to_operand_aliasing={{0}: (16, {}), {1}: (17, {}), {2}: (18, {}), {3}: (19, {}),... | custom-call | flops 10418651136 | bytes 12000000 | tf_op jit(solution)/shard_map/pallas_call | solution.py:124
  118.3 0.9 collective-permute-start.11
  119.2 4.5 %collective-permute-start.12 = (bf16[2,384,1152]{2,1,0:T(8,128)(2,1)}, bf16[2,384,1152]{2,1,0:T(8,128)(2,1)}, u32[]{:S(2)}, u32[]{:S(2)}) collective-permute-start(bf16[2,384,1152]{2,1,0:T(8,128)(2,1)} %get-tuple-element.85), channel_id=1, source_target_pairs={{0,1},{1,2},{2,3},{3,4},{4,5},{5,6},{6,7},{7,8},{8,9},{9,10},{10,1... | collective-permute-start | bytes 5308424 | tf_op jit(solution)/shard_map/ppermute | solution.py:305
  123.7 2.1 %collective-permute-start.13 = (bf16[2,384,1152]{2,1,0:T(8,128)(2,1)}, bf16[2,384,1152]{2,1,0:T(8,128)(2,1)}, u32[]{:S(2)}, u32[]{:S(2)}) collective-permute-start(bf16[2,384,1152]{2,1,0:T(8,128)(2,1)} %get-tuple-element.86), channel_id=1, source_target_pairs={{1,0},{2,1},{3,2},{4,3},{5,4},{6,5},{7,6},{8,7},{9,8},{10,9},{11,1... | collective-permute-start | bytes 5308424 | tf_op jit(solution)/shard_map/ppermute | solution.py:305
  125.9 1.0 copy-done.3
  126.9 16.7 %shard_map.117 = (bf16[768,1536]{1,0:T(8,128)(2,1)}, f32[768,384]{1,0:T(8,128)}, f32[768,384]{1,0:T(8,128)}, bf16[2,384,384]{2,1,0:T(8,128)(2,1)}, bf16[2,384,384]{2,1,0:T(8,128)(2,1)}) custom-call(s32[10]{0:T(128)} %get-tuple-element.105.refs_0_, bf16[768,1536]{1,0:T(8,128)(2,1)} %bitcast.48, ...), custom_call_target="tpu_custom_call", output_to_operand_aliasing={{0}: (14, {})} | custom-call | flops 5209325568 | bytes 6000000 | tf_op jit(solution)/shard_map/pallas_call | solution.py:124
  143.6 4.0 %reduce_sum.24 = bf16[8,96,384]{2,1,0:T(8,128)(2,1)} reduce(bf16[8,8,96,384]{3,2,1,0:T(8,128)(2,1)} %all-to-all-done, bf16[]{:T(256)} %constant.81.clone.1), dimensions={0}, to_apply=%region_0.1 | reduce | flops 2064384 | bytes 5308418 | tf_op jit(solution)/shard_map/reduce_sum | solution.py:382
  147.7 7.2 %collective-permute-start.14 = (bf16[2,384,384]{2,1,0:T(8,128)(2,1)S(1)}, bf16[2,384,384]{2,1,0:T(8,128)(2,1)S(1)}, u32[]{:S(2)}, u32[]{:S(2)}) collective-permute-start(bf16[2,384,384]{2,1,0:T(8,128)(2,1)S(1)} %copy-done.10), channel_id=1, source_target_pairs={{0,1},{1,2},{2,3},{3,4},{4,5},{5,6},{6,7},{7,8},{8,9},{9,10},{10,1... | collective-permute-start | bytes 1769480 | tf_op jit(solution)/shard_map/ppermute | solution.py:305
  154.9 1.9 collective-permute-start.15
  156.9 4.3 %all-to-all-start.1 = ((bf16[8,96,384]{2,1,0:T(8,128)(2,1)}), bf16[8,96,384]{2,1,0:T(8,128)(2,1)S(1)}, u32[]{:S(2)}, u32[]{:S(2)}) async-start(bf16[8,96,384]{2,1,0:T(8,128)(2,1)} %reduce_sum.24), calls=%async_computation.1 | async-start | bytes 1179648 | tf_op jit(solution)/shard_map/all_to_all | solution.py:386
  161.2 1.5 collective-permute-done.13.refs_3_
  162.7 5.9 %all-to-all-done.1 = bf16[8,96,384]{2,1,0:T(8,128)(2,1)S(1)} async-done(((bf16[8,96,384]{2,1,0:T(8,128)(2,1)}), bf16[8,96,384]{2,1,0:T(8,128)(2,1)S(1)}, u32[]{:S(2)}, u32[]{:S(2)}) %all-to-all-start.1) | async-done | bytes 589856 | tf_op jit(solution)/shard_map/all_to_all | solution.py:386
  168.6 4.2 %collective-permute-done.15.refs_3_ = bf16[2,384,384]{2,1,0:T(8,128)(2,1)S(1)} collective-permute-done((bf16[2,384,384]{2,1,0:T(8,128)(2,1)S(1)}, bf16[2,384,384]{2,1,0:T(8,128)(2,1)S(1)}, u32[]{:S(2)}, u32[]{:S(2)}) %collective-permute-start.15) | collective-permute-done | bytes 589856 | tf_op jit(solution)/shard_map/ppermute | solution.py:305
  173.0 1.1 broadcast_in_dim.30
  174.1 7.6 %all-to-all-start.2 = ((bf16[16,96,384]{2,1,0:T(8,128)(2,1)}), bf16[16,96,384]{2,1,0:T(8,128)(2,1)}, u32[]{:S(2)}, u32[]{:S(2)}) async-start(bf16[16,96,384]{2,1,0:T(8,128)(2,1)} %broadcast_in_dim.30), calls=%async_computation.2 | async-start | bytes 2359296 | tf_op jit(solution)/shard_map/all_to_all | solution.py:390
  181.7 0.7 pad_add_fusion.4.meta
  182.3 7.2 %shard_map.118 = (bf16[768,1536]{1,0:T(8,128)(2,1)}, bf16[768,1536]{1,0:T(8,128)(2,1)}) custom-call(s32[3]{0:T(128)} %pad_add_fusion.4.meta, f32[768,1152]{1,0:T(8,128)} %get-tuple-element.91.refs_0_, f32[768,1152]{1,0:T(8,128)} %get-tuple-element.92.refs_1_, bf16[2,384,1152]{2,1,0:T(8,128)(2,1)} %collective-permute-done.12.refs_2_, ...), custom_call_target="tpu_custom_call" | custom-call | flops 4000000 | bytes 20000000 | tf_op jit(solution)/shard_map/pallas_call | solution.py:174
  189.5 3.2 %shard_map.119 = (bf16[768,1536]{1,0:T(8,128)(2,1)}, bf16[768,1536]{1,0:T(8,128)(2,1)}) custom-call(s32[1]{0:T(128)} %bitcast.11.meta, f32[768,384]{1,0:T(8,128)} %get-tuple-element.79.refs_0_, f32[768,384]{1,0:T(8,128)} %get-tuple-element.80.refs_1_, bf16[2,384,384]{2,1,0:T(8,128)(2,1)} %copy-done.4, ...), custom_call_target="tpu_custom_call", output_to_operand_aliasing={{0}: (5, {}), {1}: (6, {})} | custom-call | flops 4000000 | bytes 20000000 | tf_op jit(solution)/shard_map/pallas_call | solution.py:174
  192.7 5.9 %all-to-all-done.2.pieces = bf16[16,96,384]{2,1,0:T(8,128)(2,1)} async-done(((bf16[16,96,384]{2,1,0:T(8,128)(2,1)}), bf16[16,96,384]{2,1,0:T(8,128)(2,1)}, u32[]{:S(2)}, u32[]{:S(2)}) %all-to-all-start.2) | async-done | bytes 1179680 | tf_op jit(solution)/shard_map/all_to_all | solution.py:390
  198.6 2.5 %shard_map.120 = f32[192,3072]{1,0:T(8,128)} custom-call(bf16[16,96,384]{2,1,0:T(8,128)(2,1)} %all-to-all-done.2.pieces), custom_call_target="tpu_custom_call" | custom-call | tf_op jit(solution)/shard_map/pallas_call | solution.py:248
  (40 shorter events, 0.5 us)
Async XLA Ops:
  0.6 1.3 copy-start
  7.3 15.2 %collective-permute-start.1 = (bf16[192,1536]{1,0:T(8,128)(2,1)S(1)}, bf16[192,1536]{1,0:T(8,128)(2,1)S(1)}, u32[]{:S(2)}, u32[]{:S(2)}) collective-permute-start(bf16[192,1536]{1,0:T(8,128)(2,1)S(1)} %constant_dynamic-slice_fusion.1), channel_id=1, source_target_pairs={{0,16},{16,0},{32,48},{48,32},{64,80},{80,64},{96,112},{112,96},{1... | collective-permute-start | bytes 1769480 | tf_op jit(solution)/shard_map/ppermute | solution.py:301
  14.6 21.9 %collective-permute-start = (bf16[2,2,8,96,384]{4,3,2,1,0:T(8,128)(2,1)}, bf16[2,2,8,96,384]{4,3,2,1,0:T(8,128)(2,1)}, u32[]{:S(2)}, u32[]{:S(2)}) collective-permute-start(bf16[2,2,8,96,384]{4,3,2,1,0:T(8,128)(2,1)} %shard_map.112), channel_id=1, source_target_pairs={{0,1},{1,0},{2,3},{3,2},{4,5},{5,4},{6,7},{7,6},{8,9},{9,8},{10,11... | collective-permute-start | bytes 7077896 | tf_op jit(solution)/shard_map/ppermute | solution.py:305
  15.5 31.1 %collective-permute-start.3 = (bf16[2,384,1536]{2,1,0:T(8,128)(2,1)}, bf16[2,384,1536]{2,1,0:T(8,128)(2,1)}, u32[]{:S(2)}, u32[]{:S(2)}) collective-permute-start(bf16[2,384,1536]{2,1,0:T(8,128)(2,1)} %get-tuple-element.57), channel_id=1, source_target_pairs={{0,1},{1,2},{2,3},{3,4},{4,5},{5,6},{6,7},{7,8},{8,9},{9,10},{10,1... | collective-permute-start | bytes 7077896 | tf_op jit(solution)/shard_map/ppermute | solution.py:305
  20.5 34.1 %collective-permute-start.4 = (bf16[2,384,1536]{2,1,0:T(8,128)(2,1)}, bf16[2,384,1536]{2,1,0:T(8,128)(2,1)}, u32[]{:S(2)}, u32[]{:S(2)}) collective-permute-start(bf16[2,384,1536]{2,1,0:T(8,128)(2,1)} %get-tuple-element.58), channel_id=1, source_target_pairs={{1,0},{2,1},{3,2},{4,3},{5,4},{6,5},{7,6},{8,7},{9,8},{10,9},{11,1... | collective-permute-start | bytes 7077896 | tf_op jit(solution)/shard_map/ppermute | solution.py:305
  22.5 5.9 %copy-start.6 = (bf16[192,1536]{1,0:T(8,128)(2,1)}, bf16[192,1536]{1,0:T(8,128)(2,1)S(1)}, u32[]{:S(2)}) copy-start(bf16[192,1536]{1,0:T(8,128)(2,1)S(1)} %collective-permute-done.1) | copy-start | bytes 1769476
  28.3 26.3 %collective-permute-start.2 = (bf16[2,2,8,96,384]{4,3,2,1,0:T(8,128)(2,1)}, bf16[2,2,8,96,384]{4,3,2,1,0:T(8,128)(2,1)}, u32[]{:S(2)}, u32[]{:S(2)}) collective-permute-start(bf16[2,2,8,96,384]{4,3,2,1,0:T(8,128)(2,1)} %shard_map.113), channel_id=1, source_target_pairs={{0,1},{1,0},{2,3},{3,2},{4,5},{5,4},{6,7},{7,6},{8,9},{9,8},{10,11... | collective-permute-start | bytes 7077896 | tf_op jit(solution)/shard_map/ppermute | solution.py:305
  31.3 3.8 %collective-permute-start.5 = (bf16[384,1536]{1,0:T(8,128)(2,1)}, bf16[384,1536]{1,0:T(8,128)(2,1)S(1)}, u32[]{:S(2)}, u32[]{:S(2)}) collective-permute-start(bf16[384,1536]{1,0:T(8,128)(2,1)} %pad_maximum_fusion), channel_id=1, source_target_pairs={{0,1},{1,0},{2,3},{3,2},{4,5},{5,4},{6,7},{7,6},{8,9},{9,8},{10,11... | collective-permute-start | bytes 3538952 | tf_op jit(solution)/shard_map/ppermute | solution.py:305
  35.1 28.8 %collective-permute-start.6 = (bf16[384,1536]{1,0:T(8,128)(2,1)}, bf16[384,1536]{1,0:T(8,128)(2,1)}, u32[]{:S(2)}, u32[]{:S(2)}) collective-permute-start(bf16[384,1536]{1,0:T(8,128)(2,1)} %pad_maximum_fusion), channel_id=1, source_target_pairs={{0,32},{16,48},{32,64},{48,80},{64,96},{80,112},{96,0},{112,16},{1... | collective-permute-start | bytes 3538952 | tf_op jit(solution)/shard_map/ppermute | solution.py:301
  36.4 27.5 %collective-permute-start.7 = (bf16[384,1536]{1,0:T(8,128)(2,1)}, bf16[384,1536]{1,0:T(8,128)(2,1)}, u32[]{:S(2)}, u32[]{:S(2)}) collective-permute-start(bf16[384,1536]{1,0:T(8,128)(2,1)} %pad_maximum_fusion), channel_id=1, source_target_pairs={{0,96},{16,112},{32,0},{48,16},{64,32},{80,48},{96,64},{112,80},{1... | collective-permute-start | bytes 3538952 | tf_op jit(solution)/shard_map/ppermute | solution.py:301
  63.9 9.2 %copy-start.8 = (s32[1,32,3]{1,0,2:T(1,128)S(1)}, s32[1,32,3]{1,0,2:T(1,128)}, u32[]{:S(2)}) copy-start(s32[1,32,3]{1,0,2:T(1,128)} %param.15) | copy-start | bytes 1156
  63.9 9.5 %copy-start.7 = (f32[1,12,768]{2,0,1:T(1,128)S(1)}, f32[1,12,768]{2,0,1:T(1,128)}, u32[]{:S(2)}) copy-start(f32[1,12,768]{2,0,1:T(1,128)} %param.12) | copy-start | bytes 110596
  63.9 79.7 %all-to-all-start = ((bf16[8,8,96,384]{3,2,1,0:T(8,128)(2,1)}), bf16[8,8,96,384]{3,2,1,0:T(8,128)(2,1)}, u32[]{:S(2)}, u32[]{:S(2)}) async-start(bf16[8,8,96,384]{3,2,1,0:T(8,128)(2,1)} %bitcast.49), calls=%async_computation | async-start | bytes 9437184 | tf_op jit(solution)/shard_map/all_to_all | solution.py:349
  71.4 16.9 %collective-permute-start.10 = (bf16[384,1536]{1,0:T(8,128)(2,1)}, bf16[384,1536]{1,0:T(8,128)(2,1)S(1)}, u32[]{:S(2)}, u32[]{:S(2)}) collective-permute-start(bf16[384,1536]{1,0:T(8,128)(2,1)} %collective-permute-done.7.refs_14_), channel_id=1, source_target_pairs={{0,1},{1,0},{2,3},{3,2},{4,5},{5,4},{6,7},{7,6},{8,9},{9,8},{10,11... | collective-permute-start | bytes 3538952 | tf_op jit(solution)/shard_map/ppermute | solution.py:305
  73.2 15.3 %collective-permute-start.9 = (bf16[384,1536]{1,0:T(8,128)(2,1)}, bf16[384,1536]{1,0:T(8,128)(2,1)}, u32[]{:S(2)}, u32[]{:S(2)}) collective-permute-start(bf16[384,1536]{1,0:T(8,128)(2,1)} %collective-permute-done.6.refs_12_), channel_id=1, source_target_pairs={{0,1},{1,0},{2,3},{3,2},{4,5},{5,4},{6,7},{7,6},{8,9},{9,8},{10,11... | collective-permute-start | bytes 3538952 | tf_op jit(solution)/shard_map/ppermute | solution.py:305
  75.3 43.1 %collective-permute-start.8 = (bf16[384,1536]{1,0:T(8,128)(2,1)}, bf16[384,1536]{1,0:T(8,128)(2,1)}, u32[]{:S(2)}, u32[]{:S(2)}) collective-permute-start(bf16[384,1536]{1,0:T(8,128)(2,1)} %collective-permute-done.6.refs_12_), channel_id=1, source_target_pairs={{0,32},{16,48},{32,64},{48,80},{64,96},{80,112},{96,0},{112,16},{1... | collective-permute-start | bytes 3538952 | tf_op jit(solution)/shard_map/ppermute | solution.py:301
  88.4 1.0 copy-start.2
  118.3 7.5 %collective-permute-start.11 = (bf16[384,1536]{1,0:T(8,128)(2,1)}, bf16[384,1536]{1,0:T(8,128)(2,1)S(1)}, u32[]{:S(2)}, u32[]{:S(2)}) collective-permute-start(bf16[384,1536]{1,0:T(8,128)(2,1)} %collective-permute-done.8.refs_12_), channel_id=1, source_target_pairs={{0,1},{1,0},{2,3},{3,2},{4,5},{5,4},{6,7},{7,6},{8,9},{9,8},{10,11... | collective-permute-start | bytes 3538952 | tf_op jit(solution)/shard_map/ppermute | solution.py:305
  119.2 42.0 %collective-permute-start.12 = (bf16[2,384,1152]{2,1,0:T(8,128)(2,1)}, bf16[2,384,1152]{2,1,0:T(8,128)(2,1)}, u32[]{:S(2)}, u32[]{:S(2)}) collective-permute-start(bf16[2,384,1152]{2,1,0:T(8,128)(2,1)} %get-tuple-element.85), channel_id=1, source_target_pairs={{0,1},{1,2},{2,3},{3,4},{4,5},{5,6},{6,7},{7,8},{8,9},{9,10},{10,1... | collective-permute-start | bytes 5308424 | tf_op jit(solution)/shard_map/ppermute | solution.py:305
  123.7 39.0 %collective-permute-start.13 = (bf16[2,384,1152]{2,1,0:T(8,128)(2,1)}, bf16[2,384,1152]{2,1,0:T(8,128)(2,1)}, u32[]{:S(2)}, u32[]{:S(2)}) collective-permute-start(bf16[2,384,1152]{2,1,0:T(8,128)(2,1)} %get-tuple-element.86), channel_id=1, source_target_pairs={{1,0},{2,1},{3,2},{4,3},{5,4},{6,5},{7,6},{8,7},{9,8},{10,9},{11,1... | collective-permute-start | bytes 5308424 | tf_op jit(solution)/shard_map/ppermute | solution.py:305
  125.9 1.0 copy-start.3
  143.6 4.1 %copy-start.10 = (bf16[2,384,384]{2,1,0:T(8,128)(2,1)S(1)}, bf16[2,384,384]{2,1,0:T(8,128)(2,1)}, u32[]{:S(2)}) copy-start(bf16[2,384,384]{2,1,0:T(8,128)(2,1)} %get-tuple-element.87) | copy-start | bytes 1769476
  143.6 11.3 %copy-start.9 = (bf16[2,384,384]{2,1,0:T(8,128)(2,1)S(1)}, bf16[2,384,384]{2,1,0:T(8,128)(2,1)}, u32[]{:S(2)}) copy-start(bf16[2,384,384]{2,1,0:T(8,128)(2,1)} %get-tuple-element.88) | copy-start | bytes 1769476
  147.7 20.9 %collective-permute-start.14 = (bf16[2,384,384]{2,1,0:T(8,128)(2,1)S(1)}, bf16[2,384,384]{2,1,0:T(8,128)(2,1)S(1)}, u32[]{:S(2)}, u32[]{:S(2)}) collective-permute-start(bf16[2,384,384]{2,1,0:T(8,128)(2,1)S(1)} %copy-done.10), channel_id=1, source_target_pairs={{0,1},{1,2},{2,3},{3,4},{4,5},{5,6},{6,7},{7,8},{8,9},{9,10},{10,1... | collective-permute-start | bytes 1769480 | tf_op jit(solution)/shard_map/ppermute | solution.py:305
  154.9 17.9 %collective-permute-start.15 = (bf16[2,384,384]{2,1,0:T(8,128)(2,1)S(1)}, bf16[2,384,384]{2,1,0:T(8,128)(2,1)S(1)}, u32[]{:S(2)}, u32[]{:S(2)}) collective-permute-start(bf16[2,384,384]{2,1,0:T(8,128)(2,1)S(1)} %copy-done.9), channel_id=1, source_target_pairs={{1,0},{2,1},{3,2},{4,3},{5,4},{6,5},{7,6},{8,7},{9,8},{10,9},{11,1... | collective-permute-start | bytes 1769480 | tf_op jit(solution)/shard_map/ppermute | solution.py:305
  156.9 11.7 %all-to-all-start.1 = ((bf16[8,96,384]{2,1,0:T(8,128)(2,1)}), bf16[8,96,384]{2,1,0:T(8,128)(2,1)S(1)}, u32[]{:S(2)}, u32[]{:S(2)}) async-start(bf16[8,96,384]{2,1,0:T(8,128)(2,1)} %reduce_sum.24), calls=%async_computation.1 | async-start | bytes 1179648 | tf_op jit(solution)/shard_map/all_to_all | solution.py:386
  168.6 20.9 %copy-start.4 = (bf16[2,384,384]{2,1,0:T(8,128)(2,1)}, bf16[2,384,384]{2,1,0:T(8,128)(2,1)S(1)}, u32[]{:S(2)}) copy-start(bf16[2,384,384]{2,1,0:T(8,128)(2,1)S(1)} %collective-permute-done.14.refs_2_) | copy-start | bytes 1769476
  172.9 16.6 %copy-start.5 = (bf16[2,384,384]{2,1,0:T(8,128)(2,1)}, bf16[2,384,384]{2,1,0:T(8,128)(2,1)S(1)}, u32[]{:S(2)}) copy-start(bf16[2,384,384]{2,1,0:T(8,128)(2,1)S(1)} %collective-permute-done.15.refs_3_) | copy-start | bytes 1769476
  174.1 24.5 %all-to-all-start.2 = ((bf16[16,96,384]{2,1,0:T(8,128)(2,1)}), bf16[16,96,384]{2,1,0:T(8,128)(2,1)}, u32[]{:S(2)}, u32[]{:S(2)}) async-start(bf16[16,96,384]{2,1,0:T(8,128)(2,1)} %broadcast_in_dim.30), calls=%async_computation.2 | async-start | bytes 2359296 | tf_op jit(solution)/shard_map/all_to_all | solution.py:390
  189.5 11.6 %copy-start.1 = (bf16[192,3072]{1,0:T(8,128)(2,1)S(1)}, bf16[192,3072]{1,0:T(8,128)(2,1)}, u32[]{:S(2)}) copy-start(bf16[192,3072]{1,0:T(8,128)(2,1)} %param.14) | copy-start | bytes 3538948
